TPU v7x, 32 devices: a whole 2x2x4 slice. The times are simulated.
32 devices in a mesh: row: 4 (over y, x), col: 8 (over z, core).
Axes of the slice: x: 2, y: 2, z: 4, core: 2. Of those that a mesh axis runs over, the one named last changes fastest.
Arguments:
- block_input: bfloat16 [4, 10240, 1088], P(None, ('row', 'col')), may hold values from -6 to 6
- paths: int32 [2, 4, 10240], P(None, None, 'row'), may hold values from 0 to 12, as said below
- ln1_gain: float32 [1088], replicated, may hold values from 0.1 to 1.9
- ln1_bias: float32 [1088], replicated, may hold values from -3 to 3
- w_qkv: bfloat16 [1088, 3264], P('row', 'col'), may hold values from -0.1875 to 0.1875
- q_bias: float32 [1088], replicated, may hold values from -3 to 3
- v_bias: float32 [1088], replicated, may hold values from -0.3 to 0.3
- w_out: bfloat16 [1088, 1088], P('row', 'col'), may hold values from -3 to 3
- out_bias: float32 [1088], replicated, may hold values from -3 to 3
- ln2_gain: float32 [1088], replicated, may hold values from 0.1 to 1.9
- ln2_bias: float32 [1088], replicated, may hold values from -3 to 3
- w_up: bfloat16 [1088, 4352], P('row', 'col'), may hold values from -0.1875 to 0.1875
- up_bias: float32 [4352], replicated, may hold values from -3 to 3
- w_down: bfloat16 [4352, 1088], P('col', 'row'), may hold values from -0.09375 to 0.09375
- down_bias: float32 [1088], replicated, may hold values from -3 to 3
- cotangent: bfloat16 [4, 10240, 1088], P(None, ('row', 'col')), may hold values from -6 to 6
Outputs:
- result: bfloat16 [4, 10240, 1088], P(None, ('row', 'col'))
- input_grad: bfloat16 [4, 10240, 1088], P(None, ('row', 'col'))
- ln1_gain_grad: float32 [1088], replicated
- ln1_bias_grad: float32 [1088], replicated
- w_qkv_grad: float32 [1088, 3264], P('row', 'col')
- q_bias_grad: float32 [1088], replicated
- v_bias_grad: float32 [1088], replicated
- w_out_grad: float32 [1088, 1088], P('row', 'col')
- out_bias_grad: float32 [1088], replicated
- ln2_gain_grad: float32 [1088], replicated
- ln2_bias_grad: float32 [1088], replicated
- w_up_grad: float32 [1088, 4352], P('row', 'col')
- up_bias_grad: float32 [4352], replicated
- w_down_grad: float32 [4352, 1088], P('col', 'row')
- down_bias_grad: float32 [1088], replicated
Inputs may be any that keep to these rules, and one draw needn't show every extreme that they name: Within each tree, segment 0 is the trunk and takes the first 1024 rows; the remaining rows form 4 groups of three consecutive segments of 128 rows each: one branch (a segment b from 1 to 4) and its two leaves (segments 2b + 3 and 2b + 4, so 5 to 12), in an order within the group that may differ from group to group; the branch may stand before, between or after its leaves. paths[1] is 0 for the trunk and for branches, and a leaf's branch for a leaf. Every tree holds all 13 segments.
All inputs are finite; a program needn't handle non-finite values.
Results may differ from a plain program's by a relative error of at most 0.013.
Values may be sent and summed in bfloat16 or wider, within the bound.
A program may use at most 704 MiB of HBM per device.

v0:
```python
from functools import partial

import jax
import jax.numpy as jnp
from jax import lax
from jax.sharding import PartitionSpec as P

HEAD_DIM = 64


def layer_norm(value, gain, bias):
    center = value - jnp.mean(value, axis=-1, keepdims=True)
    spread = jnp.mean(center * center, axis=-1, keepdims=True)
    return center * lax.rsqrt(spread + 1e-05) * gain + bias


def against(left, right, right_dim):
    return lax.dot_general(
        left, right, (((1,), (right_dim,)), ((), ())), preferred_element_type=jnp.float32
    )


def outer_rows(left, right):
    return lax.dot_general(
        left, right, (((0,), (0,)), ((), ())), preferred_element_type=jnp.float32
    )


def fetch_weights(w_qkv, w_out, w_up, w_down):
    blocks = (
        lax.all_gather(w_qkv, "row", axis=0, tiled=True),
        lax.all_gather(w_out, "row", axis=0, tiled=True),
        lax.all_gather(w_up, "row", axis=0, tiled=True),
        lax.all_gather(w_down, "row", axis=1, tiled=True),
    )
    return blocks


def tree_rows(value):
    return lax.all_gather(value, "col", axis=0, tiled=True)


def to_tokens(value):
    return lax.all_to_all(value, "col", split_axis=0, concat_axis=1, tiled=True)


def to_columns(value):
    return lax.all_to_all(value, "col", split_axis=1, concat_axis=0, tiled=True)


def column_part(vector, count):
    return lax.dynamic_slice_in_dim(vector, lax.axis_index("col") * count, count)


def place_part(block, total_length):
    empty = jnp.zeros((total_length,), jnp.float32)
    return lax.dynamic_update_slice_in_dim(empty, block, lax.axis_index("col") * block.shape[0], 0)


def sum_back(grad_cols, weight_cols, weight_dim, local_rows):
    piece = lax.slice_in_dim(grad_cols, 0, local_rows * lax.axis_size("col"), axis=0)
    return lax.psum_scatter(
        against(piece, weight_cols, weight_dim), "col", scatter_dimension=0, tiled=True
    )


def local(
    block_input,
    paths,
    ln1_gain,
    ln1_bias,
    w_qkv,
    q_bias,
    v_bias,
    w_out,
    out_bias,
    ln2_gain,
    ln2_bias,
    w_up,
    up_bias,
    w_down,
    down_bias,
    cotangent,
):
    width = block_input.shape[2]
    local_rows = block_input.shape[1]
    tree_length = paths.shape[2]
    heads = width // HEAD_DIM
    scale = HEAD_DIM ** (-0.5)
    column = lax.axis_index("col")
    key_places = jnp.arange(tree_length, dtype=jnp.int32)
    query_places = column * local_rows + jnp.arange(local_rows, dtype=jnp.int32)
    triple_bias_full = jnp.concatenate([q_bias, jnp.zeros_like(q_bias), v_bias])
    gelu_exact = partial(jax.nn.gelu, approximate=False)
    triple_total = 0.0
    out_total = 0.0
    up_total = 0.0
    down_total = 0.0
    gain_one = 0.0
    shift_one = 0.0
    gain_two = 0.0
    shift_two = 0.0
    query_bias_total = 0.0
    value_bias_total = 0.0
    out_bias_total = 0.0
    up_bias_total = 0.0
    down_bias_total = 0.0
    results = []
    input_grads = []
    for micro in range(block_input.shape[0]):
        weights_now = fetch_weights(w_qkv, w_out, w_up, w_down)
        triple_weight, out_weight, up_weight, down_weight = weights_now
        rows_in = block_input[micro].astype(jnp.float32)
        own_all = paths[0, micro]
        parent_all = paths[1, micro]
        own_query = lax.dynamic_slice_in_dim(own_all, column * local_rows, local_rows)
        parent_query = lax.dynamic_slice_in_dim(parent_all, column * local_rows, local_rows)
        first_in = layer_norm(rows_in, ln1_gain, ln1_bias).astype(jnp.bfloat16)
        first_rows = tree_rows(first_in)
        projected = (
            jnp.dot(first_rows, triple_weight, preferred_element_type=jnp.float32)
            + column_part(triple_bias_full, triple_weight.shape[1])
        ).astype(jnp.bfloat16)
        triple = to_tokens(projected)
        query = triple[:, :width]
        keys_local = triple[:, width : 2 * width]
        values_local = triple[:, 2 * width :]
        key_rows, value_rows = (
            lax.all_gather(keys_local, "col", axis=0, tiled=True),
            lax.all_gather(values_local, "col", axis=0, tiled=True),
        )
        query_heads = query.reshape(local_rows, heads, HEAD_DIM)
        key_heads = key_rows.reshape(tree_length, heads, HEAD_DIM)
        value_heads = value_rows.reshape(tree_length, heads, HEAD_DIM)
        scores = (
            jnp.einsum("qhd,khd->hqk", query_heads, key_heads, preferred_element_type=jnp.float32)
            * scale
        )
        visible = (key_places[None, :] <= query_places[:, None]) & (
            (own_all[None, :] == 0)
            | (own_all[None, :] == own_query[:, None])
            | (own_all[None, :] == parent_query[:, None])
        )
        scores = jnp.where(visible[None], scores, -1e30)
        highest = jnp.max(scores, axis=-1, keepdims=True)
        raised = jnp.exp(scores - highest)
        probs = raised / jnp.sum(raised, axis=-1, keepdims=True)
        shares = probs.astype(jnp.bfloat16)
        mixed = jnp.einsum("hqk,khd->qhd", shares, value_heads, preferred_element_type=jnp.float32)
        mixed = mixed.reshape(local_rows, width).astype(jnp.bfloat16)
        mixed_rows = tree_rows(mixed)
        attended_cols = (
            jnp.dot(mixed_rows, out_weight, preferred_element_type=jnp.float32)
            + column_part(out_bias, out_weight.shape[1])
        ).astype(jnp.bfloat16)
        attended = to_tokens(attended_cols).astype(jnp.float32)
        middle = rows_in + attended
        second_in = layer_norm(middle, ln2_gain, ln2_bias).astype(jnp.bfloat16)
        second_rows = tree_rows(second_in)
        widened = jnp.dot(second_rows, up_weight, preferred_element_type=jnp.float32) + column_part(
            up_bias, up_weight.shape[1]
        )
        activated = gelu_exact(widened).astype(jnp.bfloat16)
        lowered = sum_back(activated, down_weight, 0, local_rows)
        results.append((middle + lowered + down_bias).astype(jnp.bfloat16))
        upstream = cotangent[micro]
        seed = upstream.astype(jnp.float32)
        down_bias_total = down_bias_total + jnp.sum(seed, axis=0)
        upstream_rows = tree_rows(upstream)
        down_total = down_total + outer_rows(activated, upstream_rows)
        hidden_grad = against(upstream_rows, down_weight, 1)
        gelu_pull = jax.vjp(gelu_exact, widened)[1]
        widened_grad = gelu_pull(hidden_grad)[0].astype(jnp.bfloat16)
        up_bias_total = up_bias_total + place_part(
            jnp.sum(widened_grad.astype(jnp.float32), axis=0), up_bias.shape[0]
        )
        up_total = up_total + outer_rows(second_rows, widened_grad)
        second_grad = sum_back(widened_grad, up_weight, 1, local_rows)
        second_pull = jax.vjp(layer_norm, middle, ln2_gain, ln2_bias)[1]
        middle_norm_grad, gain_two_grad, shift_two_grad = second_pull(second_grad)
        gain_two = gain_two + gain_two_grad
        shift_two = shift_two + shift_two_grad
        middle_grad = seed + middle_norm_grad
        attended_grad = middle_grad.astype(jnp.bfloat16)
        out_bias_total = out_bias_total + jnp.sum(attended_grad.astype(jnp.float32), axis=0)
        attended_grad_cols = to_columns(attended_grad)
        out_total = out_total + outer_rows(mixed_rows, attended_grad_cols)
        mixed_grad = sum_back(attended_grad_cols, out_weight, 1, local_rows).astype(jnp.bfloat16)
        mixed_grad_heads = mixed_grad.reshape(local_rows, heads, HEAD_DIM)
        value_grad = jnp.einsum(
            "hqk,qhd->khd", shares, mixed_grad_heads, preferred_element_type=jnp.float32
        )
        share_grad = jnp.einsum(
            "qhd,khd->hqk", mixed_grad_heads, value_heads, preferred_element_type=jnp.float32
        )
        inner = jnp.sum(probs * share_grad, axis=-1, keepdims=True)
        score_grad = (probs * (share_grad - inner)).astype(jnp.bfloat16)
        query_grad = (
            jnp.einsum("hqk,khd->qhd", score_grad, key_heads, preferred_element_type=jnp.float32)
            * scale
        )
        key_grad = (
            jnp.einsum("hqk,qhd->khd", score_grad, query_heads, preferred_element_type=jnp.float32)
            * scale
        )
        key_part, value_part = (
            lax.psum_scatter(
                key_grad.reshape(tree_length, width), "col", scatter_dimension=0, tiled=True
            ),
            lax.psum_scatter(
                value_grad.reshape(tree_length, width), "col", scatter_dimension=0, tiled=True
            ),
        )
        triple_grad = jnp.concatenate(
            [query_grad.reshape(local_rows, width), key_part, value_part], axis=1
        ).astype(jnp.bfloat16)
        query_bias_total = query_bias_total + jnp.sum(
            triple_grad[:, :width].astype(jnp.float32), axis=0
        )
        value_bias_total = value_bias_total + jnp.sum(
            triple_grad[:, 2 * width :].astype(jnp.float32), axis=0
        )
        triple_grad_cols = to_columns(triple_grad)
        triple_total = triple_total + outer_rows(first_rows, triple_grad_cols)
        first_grad = sum_back(triple_grad_cols, triple_weight, 1, local_rows)
        first_pull = jax.vjp(layer_norm, rows_in, ln1_gain, ln1_bias)[1]
        input_norm_grad, gain_one_grad, shift_one_grad = first_pull(first_grad)
        gain_one = gain_one + gain_one_grad
        shift_one = shift_one + shift_one_grad
        input_grads.append((middle_grad + input_norm_grad).astype(jnp.bfloat16))
    triple_total, out_total, up_total, down_total = (
        lax.psum_scatter(
            triple_total.astype(jnp.bfloat16), "row", scatter_dimension=0, tiled=True
        ).astype(jnp.float32),
        lax.psum_scatter(
            out_total.astype(jnp.bfloat16), "row", scatter_dimension=0, tiled=True
        ).astype(jnp.float32),
        lax.psum_scatter(
            up_total.astype(jnp.bfloat16), "row", scatter_dimension=0, tiled=True
        ).astype(jnp.float32),
        lax.psum_scatter(
            down_total.astype(jnp.bfloat16), "row", scatter_dimension=1, tiled=True
        ).astype(jnp.float32),
    )
    summed = lax.psum(
        (
            gain_one,
            shift_one,
            query_bias_total,
            value_bias_total,
            out_bias_total,
            gain_two,
            shift_two,
            up_bias_total,
            down_bias_total,
        ),
        ("row", "col"),
    )
    return (
        jnp.stack(results),
        jnp.stack(input_grads),
        summed[0],
        summed[1],
        triple_total,
        summed[2],
        summed[3],
        out_total,
        summed[4],
        summed[5],
        summed[6],
        up_total,
        summed[7],
        down_total,
        summed[8],
    )


def solution(mesh):
    placed = (
        P(None, ("row", "col"), None),
        P(None, None, "row"),
        P(),
        P(),
        P("row", "col"),
        P(),
        P(),
        P("row", "col"),
        P(),
        P(),
        P(),
        P("row", "col"),
        P(),
        P("col", "row"),
        P(),
        P(None, ("row", "col"), None),
    )
    return jax.shard_map(
        local,
        mesh=mesh,
        in_specs=placed,
        out_specs=(
            P(None, ("row", "col"), None),
            P(None, ("row", "col"), None),
            P(),
            P(),
            P("row", "col"),
            P(),
            P(),
            P("row", "col"),
            P(),
            P(),
            P(),
            P("row", "col"),
            P(),
            P("col", "row"),
            P(),
        ),
        check_vma=False,
    )
```

profile of v0, /device:TPU:8, one launch (start us, length us, event | category | flops | bytes accessed | tf_op | source)
XLA Modules:
  0.0 5349.8 jit_solution(1490101711338773957)
XLA Ops:
  32.8 45.0 all-gather.66.cloned.1.call-done
  89.2 102.9 %all_to_all.268 = bf16[8,320,408]{1,2,0:T(8,128)(2,1)S(1)} all-to-all(bf16[8,320,408]{1,2,0:T(8,128)(2,1)S(1)} %copy.158), channel_id=1, replica_groups=mesh['row'=4,'col'=8] {'col'}, dimensions={0} | all-to-all | bytes 4177920 | tf_op jit(solution)/shard_map/all_to_all | solution.py:44
  206.7 107.8 %all_to_all.269 = bf16[8,320,408]{1,2,0:T(8,128)(2,1)S(1)} all-to-all(bf16[8,320,408]{1,2,0:T(8,128)(2,1)S(1)} %copy.150), channel_id=1, replica_groups=mesh['row'=4,'col'=8] {'col'}, dimensions={0} | all-to-all | bytes 4177920 | tf_op jit(solution)/shard_map/all_to_all | solution.py:44
  329.8 98.3 %all_to_all.270 = bf16[8,320,408]{1,2,0:T(8,128)(2,1)S(1)} all-to-all(bf16[8,320,408]{1,2,0:T(8,128)(2,1)S(1)} %copy.142), channel_id=1, replica_groups=mesh['row'=4,'col'=8] {'col'}, dimensions={0} | all-to-all | bytes 4177920 | tf_op jit(solution)/shard_map/all_to_all | solution.py:44
  522.5 53.1 all-gather.58.cloned.1.call-done
  646.3 53.6 %all-gather.48.cloned.1.call-done = bf16[2560,1088]{1,0:T(8,128)(2,1)} async-done(((bf16[320,1088]{1,0:T(8,128)(2,1)}), bf16[2560,1088]{1,0:T(8,128)(2,1)}) %all-gather.48.cloned.1.call-update) | async-done | bytes 5570576 | tf_op jit(solution)/shard_map/all_gather | solution.py:130
  784.8 53.3 all-gather.62.cloned.1.call-done
  853.8 63.5 %all-gather.52.cloned.1.call-done = bf16[2560,1088]{1,0:T(8,128)(2,1)} async-done(((bf16[320,1088]{1,0:T(8,128)(2,1)}), bf16[2560,1088]{1,0:T(8,128)(2,1)}) %all-gather.52.cloned.1.call-update) | async-done | bytes 5570576 | tf_op jit(solution)/shard_map/all_gather | solution.py:40
  972.6 56.3 %all-gather.74.cloned.1.call-done = bf16[2560,1088]{1,0:T(8,128)(2,1)} async-done(((bf16[320,1088]{1,0:T(8,128)(2,1)}), bf16[2560,1088]{1,0:T(8,128)(2,1)}) %all-gather.74.cloned.1.call-update) | async-done | bytes 5570576 | tf_op jit(solution)/shard_map/all_gather | solution.py:40
  1038.2 52.8 all-gather.64.cloned.1.call-done
  1100.0 53.3 all-gather.54.cloned.1.call-done
  1153.3 44.0 multiply_convert_fusion.6
  1197.4 48.9 all-gather.82.cloned.1.call-done
  1410.9 80.1 %reduce-scatter.73.cloned.1.call-done = f32[320,1088]{1,0:T(8,128)} async-done(((f32[2560,1088]{1,0:T(8,128)}), f32[320,1088]{1,0:T(8,128)}) %reduce-scatter.73.cloned.1.call-update) | async-done | bytes 1392656 | tf_op jit(solution)/shard_map/reduce_scatter | solution.py:62
  1494.1 119.4 %reduce-scatter.41.cloned.1.call-done = f32[320,1088]{1,0:T(8,128)} async-done(((f32[2560,1088]{1,0:T(8,128)}), f32[320,1088]{1,0:T(8,128)}) %reduce-scatter.41.cloned.1.call-update) | async-done | bytes 1392656 | tf_op jit(solution)/shard_map/reduce_scatter | solution.py:62
  1613.5 122.3 %reduce-scatter.53.cloned.1.call-done = f32[320,1088]{1,0:T(8,128)} async-done(((f32[2560,1088]{1,0:T(8,128)}), f32[320,1088]{1,0:T(8,128)}) %reduce-scatter.53.cloned.1.call-update) | async-done | bytes 1392656 | tf_op jit(solution)/shard_map/reduce_scatter | solution.py:62
  1735.8 122.4 %reduce-scatter.63.cloned.1.call-done = f32[320,1088]{1,0:T(8,128)} async-done(((f32[2560,1088]{1,0:T(8,128)}), f32[320,1088]{1,0:T(8,128)}) %reduce-scatter.63.cloned.1.call-update) | async-done | bytes 1392656 | tf_op jit(solution)/shard_map/reduce_scatter | solution.py:62
  1864.9 115.6 %reduce-scatter.37.cloned.1.call-done = f32[320,1088]{1,0:T(8,128)} async-done(((f32[2560,1088]{1,0:T(8,128)}), f32[320,1088]{1,0:T(8,128)}) %reduce-scatter.37.cloned.1.call-update) | async-done | bytes 1392656 | tf_op jit(solution)/shard_map/reduce_scatter | solution.py:62
  1980.5 122.4 %reduce-scatter.39.cloned.1.call-done = f32[320,1088]{1,0:T(8,128)} async-done(((f32[2560,1088]{1,0:T(8,128)}), f32[320,1088]{1,0:T(8,128)}) %reduce-scatter.39.cloned.1.call-update) | async-done | bytes 1392656 | tf_op jit(solution)/shard_map/reduce_scatter | solution.py:62
  2239.1 56.9 %reduce-scatter.65.cloned.1.call-done = f32[320,1088]{1,0:T(8,128)} async-done(((f32[2560,1088]{1,0:T(8,128)}), f32[320,1088]{1,0:T(8,128)}) %reduce-scatter.65.cloned.1.call-update) | async-done | bytes 1392656 | tf_op jit(solution)/shard_map/reduce_scatter | solution.py:62
  2335.9 41.5 multiply_reduce_fusion.1
  2377.5 45.3 multiply_convert_fusion.1
  2489.3 41.5 multiply_reduce_fusion.2
  2530.8 45.8 multiply_convert_fusion.2
  2644.4 41.7 multiply_reduce_fusion
  2686.1 45.3 multiply_convert_fusion
  2796.2 102.6 %all_to_all.274 = bf16[320,8,408]{0,2,1:T(8,128)(2,1)S(1)} all-to-all(bf16[320,8,408]{0,2,1:T(8,128)(2,1)} %bitcast.547), channel_id=1, replica_groups=mesh['row'=4,'col'=8] {'col'}, dimensions={1} | all-to-all | bytes 4177920 | tf_op jit(solution)/shard_map/all_to_all | solution.py:48
  2960.5 126.7 %reduce-scatter.57.cloned.1.call-done = f32[320,1088]{1,0:T(8,128)} async-done(((f32[2560,1088]{1,0:T(8,128)}), f32[320,1088]{1,0:T(8,128)}) %reduce-scatter.57.cloned.1.call-update) | async-done | bytes 1392656 | tf_op jit(solution)/shard_map/reduce_scatter | solution.py:207
  3093.9 102.3 %all_to_all.275 = bf16[320,8,408]{0,2,1:T(8,128)(2,1)S(1)} all-to-all(bf16[320,8,408]{0,2,1:T(8,128)(2,1)} %bitcast.548), channel_id=1, replica_groups=mesh['row'=4,'col'=8] {'col'}, dimensions={1} | all-to-all | bytes 4177920 | tf_op jit(solution)/shard_map/all_to_all | solution.py:48
  3258.1 126.7 %reduce-scatter.77.cloned.1.call-done = f32[320,1088]{1,0:T(8,128)} async-done(((f32[2560,1088]{1,0:T(8,128)}), f32[320,1088]{1,0:T(8,128)}) %reduce-scatter.77.cloned.1.call-update) | async-done | bytes 1392656 | tf_op jit(solution)/shard_map/reduce_scatter | solution.py:207
  3391.5 102.3 %all_to_all.276 = bf16[320,8,408]{0,2,1:T(8,128)(2,1)S(1)} all-to-all(bf16[320,8,408]{0,2,1:T(8,128)(2,1)} %bitcast.549), channel_id=1, replica_groups=mesh['row'=4,'col'=8] {'col'}, dimensions={1} | all-to-all | bytes 4177920 | tf_op jit(solution)/shard_map/all_to_all | solution.py:48
  3510.9 45.0 reduce-scatter.71.cloned.1.call-done
  3555.9 126.7 %reduce-scatter.61.cloned.1.call-done = f32[320,1088]{1,0:T(8,128)} async-done(((f32[2560,1088]{1,0:T(8,128)}), f32[320,1088]{1,0:T(8,128)}) %reduce-scatter.61.cloned.1.call-update) | async-done | bytes 1392656 | tf_op jit(solution)/shard_map/reduce_scatter | solution.py:62
  3682.6 122.4 %reduce-scatter.81.cloned.1.call-done = f32[320,1088]{1,0:T(8,128)} async-done(((f32[2560,1088]{1,0:T(8,128)}), f32[320,1088]{1,0:T(8,128)}) %reduce-scatter.81.cloned.1.call-update) | async-done | bytes 1392656 | tf_op jit(solution)/shard_map/reduce_scatter | solution.py:62
  3811.0 60.6 %all-gather.32.cloned.1.call-done = bf16[2560,1088]{1,0:T(8,128)(2,1)} async-done(((bf16[320,1088]{1,0:T(8,128)(2,1)}), bf16[2560,1088]{1,0:T(8,128)(2,1)}) %all-gather.32.cloned.1.call-update) | async-done | bytes 5570576 | tf_op jit(solution)/shard_map/all_gather | solution.py:40
  3886.0 60.9 %all_to_all.277 = bf16[8,320,408]{1,2,0:T(8,128)(2,1)S(1)} all-to-all(bf16[8,320,408]{1,2,0:T(8,128)(2,1)S(1)} %copy.133), channel_id=1, replica_groups=mesh['row'=4,'col'=8] {'col'}, dimensions={0} | all-to-all | bytes 4177920 | tf_op jit(solution)/shard_map/all_to_all | solution.py:44
  3953.7 56.8 %all-gather.36.cloned.1.call-done = bf16[2560,1088]{1,0:T(8,128)(2,1)} async-done(((bf16[320,1088]{1,0:T(8,128)(2,1)}), bf16[2560,1088]{1,0:T(8,128)(2,1)}) %all-gather.36.cloned.1.call-update) | async-done | bytes 5570576 | tf_op jit(solution)/shard_map/all_gather | solution.py:129
  4105.5 60.1 %all-gather.38.cloned.1.call-done = bf16[2560,1088]{1,0:T(8,128)(2,1)} async-done(((bf16[320,1088]{1,0:T(8,128)(2,1)}), bf16[2560,1088]{1,0:T(8,128)(2,1)}) %all-gather.38.cloned.1.call-update) | async-done | bytes 5570576 | tf_op jit(solution)/shard_map/all_gather | solution.py:40
  4209.7 58.6 %all-gather.40.cloned.1.call-done = bf16[2560,1088]{1,0:T(8,128)(2,1)} async-done(((bf16[320,1088]{1,0:T(8,128)(2,1)}), bf16[2560,1088]{1,0:T(8,128)(2,1)}) %all-gather.40.cloned.1.call-update) | async-done | bytes 5570576 | tf_op jit(solution)/shard_map/all_gather | solution.py:40
  4288.4 41.6 all-gather.76.cloned.1.call-done
  4361.9 110.2 %reduce-scatter.43.cloned.1.call-done = f32[320,1088]{1,0:T(8,128)} async-done(((f32[2560,1088]{1,0:T(8,128)}), f32[320,1088]{1,0:T(8,128)}) %reduce-scatter.43.cloned.1.call-update) | async-done | bytes 1392656 | tf_op jit(solution)/shard_map/reduce_scatter | solution.py:62
  4474.6 119.7 %reduce-scatter.35.cloned.1.call-done = f32[320,1088]{1,0:T(8,128)} async-done(((f32[2560,1088]{1,0:T(8,128)}), f32[320,1088]{1,0:T(8,128)}) %reduce-scatter.35.cloned.1.call-update) | async-done | bytes 1392656 | tf_op jit(solution)/shard_map/reduce_scatter | solution.py:62
  4634.3 118.7 %reduce-scatter.45.cloned.1.call-done = f32[320,1088]{1,0:T(8,128)} async-done(((f32[2560,1088]{1,0:T(8,128)}), f32[320,1088]{1,0:T(8,128)}) %reduce-scatter.45.cloned.1.call-update) | async-done | bytes 1392656 | tf_op jit(solution)/shard_map/reduce_scatter | solution.py:62
  4792.0 41.5 multiply_reduce_fusion.3
  4833.6 45.5 multiply_convert_fusion.3
  4971.7 62.7 %reduce-scatter.47.cloned.1.call-done = f32[320,1088]{1,0:T(8,128)} async-done(((f32[2560,1088]{1,0:T(8,128)}), f32[320,1088]{1,0:T(8,128)}) %reduce-scatter.47.cloned.1.call-update) | async-done | bytes 1392656 | tf_op jit(solution)/shard_map/reduce_scatter | solution.py:207
  5164.8 119.4 %reduce-scatter.51.cloned.1.call-done = f32[320,1088]{1,0:T(8,128)} async-done(((f32[2560,1088]{1,0:T(8,128)}), f32[320,1088]{1,0:T(8,128)}) %reduce-scatter.51.cloned.1.call-update) | async-done | bytes 1392656 | tf_op jit(solution)/shard_map/reduce_scatter | solution.py:62
  5297.6 44.6 all-reduce.2
  (788 shorter events, 1642.0 us)
Async XLA Ops:
  17.0 177.8 %all-gather.56.cloned.1.call-start = ((), (), s32[]{:S(2)}) async-start(), calls=%async_computation.58 | async-start | bytes 6635520 | tf_op jit(solution)/shard_map/all_gather | solution.py:40
  17.8 300.4 %all-gather.46.cloned.1.call-start = ((), (), s32[]{:S(2)}) async-start(), calls=%async_computation.52 | async-start | bytes 6635520 | tf_op jit(solution)/shard_map/all_gather | solution.py:40
  18.5 421.1 %all-gather.70.cloned.1.call-start = ((), (), s32[]{:S(2)}) async-start(), calls=%async_computation.66 | async-start | bytes 6635520 | tf_op jit(solution)/shard_map/all_gather | solution.py:129
  193.5 256.8 %all-gather.68.cloned.1.call-start = ((), (), s32[]{:S(2)}) async-start(), calls=%async_computation.65 | async-start | bytes 6635520 | tf_op jit(solution)/shard_map/all_gather | solution.py:130
  194.8 319.0 %all-gather.60.cloned.1.call-start = ((), (), s32[]{:S(2)}) async-start(), calls=%async_computation.60 | async-start | bytes 6635520 | tf_op jit(solution)/shard_map/all_gather | solution.py:129
  316.8 258.9 %all-gather.58.cloned.1.call-start = ((), (), s32[]{:S(2)}) async-start(), calls=%async_computation.59 | async-start | bytes 6635520 | tf_op jit(solution)/shard_map/all_gather | solution.py:130
  318.1 319.5 %all-gather.50.cloned.1.call-start = ((), (), s32[]{:S(2)}) async-start(), calls=%async_computation.54 | async-start | bytes 6635520 | tf_op jit(solution)/shard_map/all_gather | solution.py:129
  430.5 269.5 %all-gather.48.cloned.1.call-start = ((), (), s32[]{:S(2)}) async-start(), calls=%async_computation.53 | async-start | bytes 6635520 | tf_op jit(solution)/shard_map/all_gather | solution.py:130
  432.4 339.4 %all-gather.72.cloned.1.call-start = ((), (), s32[]{:S(2)}) async-start(), calls=%async_computation.67 | async-start | bytes 6635520 | tf_op jit(solution)/shard_map/all_gather | solution.py:40
  511.0 327.2 %all-gather.62.cloned.1.call-start = ((), (), s32[]{:S(2)}) async-start(), calls=%async_computation.61 | async-start | bytes 6635520 | tf_op jit(solution)/shard_map/all_gather | solution.py:40
  636.4 280.9 %all-gather.52.cloned.1.call-start = ((), (), s32[]{:S(2)}) async-start(), calls=%async_computation.55 | async-start | bytes 6635520 | tf_op jit(solution)/shard_map/all_gather | solution.py:40
  966.3 124.7 %all-gather.64.cloned.1.call-start = ((), (), s32[]{:S(2)}) async-start(), calls=%async_computation.62 | async-start | bytes 6635520 | tf_op jit(solution)/shard_map/all_gather | solution.py:40
  966.9 186.4 %all-gather.54.cloned.1.call-start = ((), (), s32[]{:S(2)}) async-start(), calls=%async_computation.56 | async-start | bytes 6635520 | tf_op jit(solution)/shard_map/all_gather | solution.py:40
  967.6 229.7 %all-gather.44.cloned.1.call-start = ((), (), s32[]{:S(2)}) async-start(), calls=%async_computation.50 | async-start | bytes 1740800 | tf_op jit(solution)/shard_map/all_gather | solution.py:34
  968.4 277.9 %all-gather.82.cloned.1.call-start = ((), (), s32[]{:S(2)}) async-start(), calls=%async_computation.94 | async-start | bytes 6635520 | tf_op jit(solution)/shard_map/all_gather | solution.py:40
  970.2 337.6 %all-gather.78.cloned.1.call-start = ((), (), s32[]{:S(2)}) async-start(), calls=%async_computation.92 | async-start | bytes 6635520 | tf_op jit(solution)/shard_map/all_gather | solution.py:40
  970.8 398.6 %all-gather.80.cloned.1.call-start = ((), (), s32[]{:S(2)}) async-start(), calls=%async_computation.93 | async-start | bytes 6635520 | tf_op jit(solution)/shard_map/all_gather | solution.py:40
  971.4 519.7 %reduce-scatter.73.cloned.1.call-start = ((), (), s32[]{:S(2)}) async-start(), calls=%async_computation.85 | async-start | bytes 13271040 | tf_op jit(solution)/shard_map/reduce_scatter | solution.py:62
  1268.9 344.6 %reduce-scatter.41.cloned.1.call-start = ((), (), s32[]{:S(2)}) async-start(), calls=%async_computation.69 | async-start | bytes 13271040 | tf_op jit(solution)/shard_map/reduce_scatter | solution.py:62
  1279.4 456.3 %reduce-scatter.53.cloned.1.call-start = ((), (), s32[]{:S(2)}) async-start(), calls=%async_computation.75 | async-start | bytes 13271040 | tf_op jit(solution)/shard_map/reduce_scatter | solution.py:62
  1330.1 528.1 %reduce-scatter.63.cloned.1.call-start = ((), (), s32[]{:S(2)}) async-start(), calls=%async_computation.80 | async-start | bytes 13271040 | tf_op jit(solution)/shard_map/reduce_scatter | solution.py:62
  1391.6 588.8 %reduce-scatter.37.cloned.1.call-start = ((), (), s32[]{:S(2)}) async-start(), calls=%async_computation.57 | async-start | bytes 13271040 | tf_op jit(solution)/shard_map/reduce_scatter | solution.py:62
  1401.2 701.7 %reduce-scatter.39.cloned.1.call-start = ((), (), s32[]{:S(2)}) async-start(), calls=%async_computation.63 | async-start | bytes 13271040 | tf_op jit(solution)/shard_map/reduce_scatter | solution.py:62
  1410.9 885.1 %reduce-scatter.65.cloned.1.call-start = ((), (), s32[]{:S(2)}) async-start(), calls=%async_computation.81 | async-start | bytes 13271040 | tf_op jit(solution)/shard_map/reduce_scatter | solution.py:62
  2146.3 303.6 %reduce-scatter.55.cloned.1.call-start = ((), (), s32[]{:S(2)}) async-start(), calls=%async_computation.76 | async-start | bytes 13271040 | tf_op jit(solution)/shard_map/reduce_scatter | solution.py:62
  2192.4 412.3 %reduce-scatter.75.cloned.1.call-start = ((), (), s32[]{:S(2)}) async-start(), calls=%async_computation.86 | async-start | bytes 13271040 | tf_op jit(solution)/shard_map/reduce_scatter | solution.py:62
  2239.0 535.4 %reduce-scatter.69.cloned.1.call-start = ((), (), s32[]{:S(2)}) async-start(), calls=%async_computation.83 | async-start | bytes 13271040 | tf_op jit(solution)/shard_map/reduce_scatter | solution.py:210
  2335.7 453.8 %reduce-scatter.67.cloned.1.call-start = ((), (), s32[]{:S(2)}) async-start(), calls=%async_computation.82 | async-start | bytes 13271040 | tf_op jit(solution)/shard_map/reduce_scatter | solution.py:207
  2449.8 510.6 %reduce-scatter.59.cloned.1.call-start = ((), (), s32[]{:S(2)}) async-start(), calls=%async_computation.78 | async-start | bytes 13271040 | tf_op jit(solution)/shard_map/reduce_scatter | solution.py:210
  2489.0 598.1 %reduce-scatter.57.cloned.1.call-start = ((), (), s32[]{:S(2)}) async-start(), calls=%async_computation.77 | async-start | bytes 13271040 | tf_op jit(solution)/shard_map/reduce_scatter | solution.py:207
  2604.7 653.4 %reduce-scatter.79.cloned.1.call-start = ((), (), s32[]{:S(2)}) async-start(), calls=%async_computation.88 | async-start | bytes 13271040 | tf_op jit(solution)/shard_map/reduce_scatter | solution.py:210
  2644.1 740.7 %reduce-scatter.77.cloned.1.call-start = ((), (), s32[]{:S(2)}) async-start(), calls=%async_computation.87 | async-start | bytes 13271040 | tf_op jit(solution)/shard_map/reduce_scatter | solution.py:207
  2759.5 796.4 %reduce-scatter.71.cloned.1.call-start = ((), (), s32[]{:S(2)}) async-start(), calls=%async_computation.84 | async-start | bytes 13271040 | tf_op jit(solution)/shard_map/reduce_scatter | solution.py:62
  2915.2 767.4 %reduce-scatter.61.cloned.1.call-start = ((), (), s32[]{:S(2)}) async-start(), calls=%async_computation.79 | async-start | bytes 13271040 | tf_op jit(solution)/shard_map/reduce_scatter | solution.py:62
  3212.6 592.4 %reduce-scatter.81.cloned.1.call-start = ((), (), s32[]{:S(2)}) async-start(), calls=%async_computation.89 | async-start | bytes 13271040 | tf_op jit(solution)/shard_map/reduce_scatter | solution.py:62
  3510.3 361.4 %all-gather.32.cloned.1.call-start = ((), (), s32[]{:S(2)}) async-start(), calls=%async_computation.44 | async-start | bytes 6635520 | tf_op jit(solution)/shard_map/all_gather | solution.py:40
  3810.9 199.5 %all-gather.36.cloned.1.call-start = ((), (), s32[]{:S(2)}) async-start(), calls=%async_computation.46 | async-start | bytes 6635520 | tf_op jit(solution)/shard_map/all_gather | solution.py:129
  3950.8 121.4 %all-gather.34.cloned.1.call-start = ((), (), s32[]{:S(2)}) async-start(), calls=%async_computation.45 | async-start | bytes 6635520 | tf_op jit(solution)/shard_map/all_gather | solution.py:130
  3953.2 212.3 %all-gather.38.cloned.1.call-start = ((), (), s32[]{:S(2)}) async-start(), calls=%async_computation.47 | async-start | bytes 6635520 | tf_op jit(solution)/shard_map/all_gather | solution.py:40
  4105.4 162.9 %all-gather.40.cloned.1.call-start = ((), (), s32[]{:S(2)}) async-start(), calls=%async_computation.48 | async-start | bytes 6635520 | tf_op jit(solution)/shard_map/all_gather | solution.py:40
  4208.9 121.1 %all-gather.76.cloned.1.call-start = ((), (), s32[]{:S(2)}) async-start(), calls=%async_computation.91 | async-start | bytes 6635520 | tf_op jit(solution)/shard_map/all_gather | solution.py:40
  4209.7 262.4 %reduce-scatter.43.cloned.1.call-start = ((), (), s32[]{:S(2)}) async-start(), calls=%async_computation.70 | async-start | bytes 13271040 | tf_op jit(solution)/shard_map/reduce_scatter | solution.py:62
  4352.5 241.8 %reduce-scatter.35.cloned.1.call-start = ((), (), s32[]{:S(2)}) async-start(), calls=%async_computation.51 | async-start | bytes 13271040 | tf_op jit(solution)/shard_map/reduce_scatter | solution.py:62
  4361.8 391.2 %reduce-scatter.45.cloned.1.call-start = ((), (), s32[]{:S(2)}) async-start(), calls=%async_computation.71 | async-start | bytes 13271040 | tf_op jit(solution)/shard_map/reduce_scatter | solution.py:62
  4634.2 337.5 %reduce-scatter.49.cloned.1.call-start = ((), (), s32[]{:S(2)}) async-start(), calls=%async_computation.73 | async-start | bytes 13271040 | tf_op jit(solution)/shard_map/reduce_scatter | solution.py:210
  4792.0 242.5 %reduce-scatter.47.cloned.1.call-start = ((), (), s32[]{:S(2)}) async-start(), calls=%async_computation.72 | async-start | bytes 13271040 | tf_op jit(solution)/shard_map/reduce_scatter | solution.py:207
  4907.2 239.4 %reduce-scatter.89.cloned.1.call-start = ((), (), s32[]{:S(2)}) async-start(), calls=%async_computation.97 | async-start | bytes 1740800
  5132.8 151.4 %reduce-scatter.51.cloned.1.call-start = ((), (), s32[]{:S(2)}) async-start(), calls=%async_computation.74 | async-start | bytes 13271040 | tf_op jit(solution)/shard_map/reduce_scatter | solution.py:62
  (198 other events, 13557.3 us)
Sparse Core Ops, SparseCore 0:
  17.2 60.5 all-gather.65
  79.4 104.9 all-gather.55
  186.7 95.5 all-gather.45
  283.8 92.9 all-gather.69
  378.3 71.9 all-gather.67
  451.8 61.9 all-gather.59
  515.5 60.1 all-gather.57
  577.3 60.1 all-gather.49
  639.8 60.1 all-gather.47
  701.5 60.1 all-gather.71
  763.3 74.7 all-gather.61
  839.6 77.6 all-gather.51
  2146.4 149.5 reduce-scatter.64
  2298.1 124.2 reduce-scatter.54
  2424.6 120.1 reduce-scatter.74
  2547.0 120.1 reduce-scatter.68
  2669.3 120.1 reduce-scatter.66
  2791.7 168.7 reduce-scatter.58
  2962.8 124.2 reduce-scatter.56
  3089.3 168.7 reduce-scatter.78
  3260.4 124.2 reduce-scatter.76
  3387.1 168.7 reduce-scatter.70
  3558.2 124.2 reduce-scatter.60
  3684.8 120.1 reduce-scatter.80
Sparse Core Ops, SparseCore 1:
  937.8 30.2 all-gather.41
  969.5 59.3 all-gather.73
  1031.0 60.0 all-gather.63
  1093.3 60.0 all-gather.53
  1155.2 29.9 all-gather.43
  1186.9 59.3 all-gather.81
  1247.8 60.0 all-gather.77
  1309.4 60.0 all-gather.79
  1371.6 119.4 reduce-scatter.72
  1493.4 120.0 reduce-scatter.40
  1615.7 120.0 reduce-scatter.52
  1738.1 120.0 reduce-scatter.62
  1860.4 120.0 reduce-scatter.36
  1982.8 120.0 reduce-scatter.38
  3811.0 60.6 all-gather.31
  3950.9 59.5 all-gather.35
  4012.1 60.0 all-gather.33
  4105.5 60.0 all-gather.37
  4209.0 59.2 all-gather.39
  4269.9 60.0 all-gather.75
  4352.6 119.4 reduce-scatter.42
  4474.2 120.0 reduce-scatter.34
  4634.3 118.6 reduce-scatter.44
  4792.0 120.1 reduce-scatter.48
  4914.3 120.0 reduce-scatter.46
  5037.5 32.0 reduce-scatter.88
  5072.6 30.7 reduce-scatter.86
  5106.6 25.0 reduce-scatter.84
  5134.7 28.1 reduce-scatter.82
  5165.4 118.7 reduce-scatter.50
where the time goes:
time: 5370 us; the launch traced here: 5350 us
  waiting for transfers between devices  2790 us (52%)
  matrix products  1000 us (19%)
  blocking collectives  899 us (17%)
  local copies, waits for them, and re-layouts  321 us (6%)
  other arithmetic  278 us (5%)
    reduce_scatter x16, waiting for transfers between devices, sum_back(): lax.psum_scatter(against(piece, weight_cols, weight_dim), 'col', scatter_...  1500 us
    all_gather x16, waiting for transfers between devices, tree_rows(): return lax.all_gather(value, 'col', axis=0, tiled=True)  661 us
    all_to_all x7, blocking collectives, to_columns(): return lax.all_to_all(value, 'col', split_axis=1, concat_axis=0, tiled=True)  435 us
    all_to_all x5, blocking collectives, to_tokens(): return lax.all_to_all(value, 'col', split_axis=0, concat_axis=1, tiled=True)  395 us
    reduce_scatter x4, waiting for transfers between devices, local(): lax.psum_scatter(key_grad.reshape(tree_length, width), 'col', scatter_dim...  331 us
    convert_element_type x4, other arithmetic, local(): score_grad = (probs * (share_grad - inner)).astype(jnp.bfloat16)  182 us
    dot_general x20, matrix products, against(): lax.dot_general(left, right, (((1,), (right_dim,)), ((), ())), preferred_...  181 us
    dot_general x4, matrix products, local(): jnp.einsum('qhd,khd->hqk', mixed_grad_heads, value_heads, preferred_eleme...  166 us
  transfers between devices with their start and end apart: 58, of which 43 were waited for; matrix products, arithmetic and copies ran while one was open for 26% of the time, Pallas kernels for 0%

commit v1 on v0

v1 whole, which is shorter than its diff:
```python
import math
from functools import partial

import jax
import jax.numpy as jnp
import numpy as np
from jax import lax
from jax.experimental import pallas as pl
from jax.experimental.pallas import tpu as pltpu
from jax.sharding import PartitionSpec as P

HEAD_DIM = 64
TRUNK = 1024
GROUP = 384
QT = 256
LOG2E = 1.4426950408889634
LN2 = 0.6931471805599453


def dot_nn(a, b):
    return jnp.dot(a, b, preferred_element_type=jnp.float32)


def dot_nt(a, b):
    return lax.dot_general(a, b, (((1,), (1,)), ((), ())), preferred_element_type=jnp.float32)


def dot_tn(a, b):
    return lax.dot_general(a, b, (((0,), (0,)), ((), ())), preferred_element_type=jnp.float32)


def lane_masks(head):
    lane = lax.broadcasted_iota(jnp.int32, (1, 128), 1)
    inside = (lane // HEAD_DIM) == head
    return inside, inside.astype(jnp.float32).astype(jnp.bfloat16), lane % HEAD_DIM


def fill_trunk(parts, own_ref, other_ref, out_ref):
    own = TRUNK // parts
    for tile in range(own // QT):
        for part in range(parts):
            rows = (
                own_ref[tile * QT : (tile + 1) * QT, :]
                if part == 0
                else other_ref[(part - 1) * own + tile * QT : (part - 1) * own + (tile + 1) * QT, :]
            )
            start = (tile * parts + part) * QT
            out_ref[start : start + QT, :] = rows


def fwd_kernel(parts, heads, start, extra, q_ref, k_ref, v_ref, ko_ref, vo_ref, mt_ref, mg_ref, *refs):
    o_ref, lse_ref, kt, vt, va = refs[extra:]
    pair = start + pl.program_id(0)
    own = TRUNK // parts
    tiles = own // QT
    groups = (TRUNK // 256) // parts
    fill_trunk(parts, k_ref, ko_ref, kt)
    fill_trunk(parts, v_ref, vo_ref, vt)
    o_ref[...] = jnp.zeros_like(o_ref)
    lse_ref[...] = jnp.zeros_like(lse_ref)

    def finish(rows, top, total, inside):
        turned = pltpu.roll(total, HEAD_DIM, 1)
        o_ref[rows, :] += jnp.where(inside, total / turned, 0.0).astype(jnp.bfloat16)
        lse_ref[rows, :] += jnp.where(inside, 0.0, top + jnp.log2(total))

    def head_body(head, carry):
        inside, hm, _ = lane_masks(head)
        rest = 1 - hm
        va[...] = vt[...] * hm + rest
        for tile in range(tiles):
            rows = pl.ds(tile * QT, QT)
            q = q_ref[rows, :] * hm
            near = tile * parts * QT
            s_near = dot_nt(q, kt[near : near + parts * QT, :]) + mt_ref[tile]
            top = jnp.max(s_near, axis=1, keepdims=True)
            if tile > 0:
                s_far = dot_nt(q, kt[:near, :])
                top = jnp.maximum(top, jnp.max(s_far, axis=1, keepdims=True))
            p_near = jnp.exp2(s_near - top).astype(jnp.bfloat16)
            total = dot_nn(p_near, va[near : near + parts * QT, :])
            if tile > 0:
                total += dot_nn(jnp.exp2(s_far - top).astype(jnp.bfloat16), va[:near, :])
            finish(rows, top, total, inside)

        def group_body(group, carry):
            rows = pl.ds(pl.multiple_of(own + group * GROUP, 128), GROUP)
            q = q_ref[rows, :] * hm
            s_near = dot_nt(q, k_ref[rows, :]) + mg_ref[group]
            s_far = dot_nt(q, kt[...])
            top = jnp.maximum(
                jnp.max(s_near, axis=1, keepdims=True), jnp.max(s_far, axis=1, keepdims=True)
            )
            near = v_ref[rows, :] * hm + rest
            total = dot_nn(jnp.exp2(s_near - top).astype(jnp.bfloat16), near)
            total += dot_nn(jnp.exp2(s_far - top).astype(jnp.bfloat16), va[...])
            finish(rows, top, total, inside)
            return carry

        return lax.fori_loop(0, groups, group_body, carry)

    lax.fori_loop(0, jnp.minimum(2, heads - 2 * pair), head_body, 0)


def attention_forward(parts, heads, triple, others, mask_trunk, mask_group, start, stop, deps=()):
    rows = triple.shape[0]
    pairs = triple.shape[1] // (3 * 128)
    extra = others.shape[0]
    block = lambda count, shift: pl.BlockSpec((count, 128), lambda i: (0, i + shift))
    whole = lambda shape: pl.BlockSpec(shape, lambda i: (0,) * len(shape))
    return pl.pallas_call(
        partial(fwd_kernel, parts, heads, start, len(deps)),
        grid=(stop - start,),
        in_specs=[
            block(rows, start),
            block(rows, start + pairs),
            block(rows, start + 2 * pairs),
            block(extra, start),
            block(extra, start + pairs),
            whole(mask_trunk.shape),
            whole(mask_group.shape),
        ]
        + [pl.BlockSpec(memory_space=pl.ANY)] * len(deps),
        out_specs=[block(rows, 0), block(rows, 0)],
        out_shape=[
            jax.ShapeDtypeStruct((rows, (stop - start) * 128), jnp.bfloat16),
            jax.ShapeDtypeStruct((rows, (stop - start) * 128), jnp.float32),
        ],
        scratch_shapes=[
            pltpu.VMEM((TRUNK, 128), jnp.bfloat16),
            pltpu.VMEM((TRUNK, 128), jnp.bfloat16),
            pltpu.VMEM((TRUNK, 128), jnp.bfloat16),
        ],
        compiler_params=pltpu.CompilerParams(vmem_limit_bytes=48 * 1024 * 1024),
        cost_estimate=pl.CostEstimate(
            flops=(stop - start) * rows * 6_800_000, bytes_accessed=rows * pairs * 2000, transcendentals=0
        ),
        name="attention_forward",
    )(triple, triple, triple, others, others, mask_trunk, mask_group, *deps)


def split_three(value, place, outside):
    high = value.astype(jnp.bfloat16)
    left = value - high.astype(jnp.float32)
    middle = left.astype(jnp.bfloat16)
    low = (left - middle.astype(jnp.float32)).astype(jnp.bfloat16)
    high, middle, low = (v.astype(jnp.float32) for v in (high, middle, low))
    picked = jnp.where(place == 0, high, jnp.where(place == 1, middle, jnp.where(place == 2, low, 0.0)))
    return jnp.where(outside, picked, 0.0).astype(jnp.bfloat16)


def bwd_kernel(
    parts, heads, start, extra, q_ref, k_ref, v_ref, ko_ref, vo_ref, o_ref, do_ref, lse_ref, mt_ref, mg_ref,
    *refs,
):
    dq_ref, dk_ref, dv_ref, dko_ref, dvo_ref = refs[extra : extra + 5]
    kt, vt, ka, va, qa, da, qm, dm, dkt, dvt, dkg, dvg, dqs = refs[extra + 5 :]
    pair = start + pl.program_id(0)
    own = TRUNK // parts
    tiles = own // QT
    groups = (TRUNK // 256) // parts
    rows_all = own + groups * GROUP
    fill_trunk(parts, k_ref, ko_ref, kt)
    fill_trunk(parts, v_ref, vo_ref, vt)
    dkt[...] = jnp.zeros_like(dkt)
    dvt[...] = jnp.zeros_like(dvt)
    dkg[...] = jnp.zeros_like(dkg)
    dvg[...] = jnp.zeros_like(dvg)
    dqs[...] = jnp.zeros_like(dqs)

    def head_body(head, carry):
        inside, hm, place = lane_masks(head)
        rest = 1 - hm
        outside = jnp.logical_not(inside)
        ka[:TRUNK, :] = kt[...] * hm + rest
        va[:TRUNK, :] = vt[...] * hm + rest
        ka[TRUNK:, :] = k_ref[own:, :] * hm + rest
        va[TRUNK:, :] = v_ref[own:, :] * hm + rest

        def prepare(step, carry):
            rows = pl.ds(pl.multiple_of(step * 128, 128), 128)
            q = q_ref[rows, :] * hm
            d = do_ref[rows, :] * hm
            qm[rows, :] = q
            dm[rows, :] = d
            qa[rows, :] = q - split_three(lse_ref[rows, :], place, outside)
            delta = jnp.sum(
                d.astype(jnp.float32) * o_ref[rows, :].astype(jnp.float32), axis=1, keepdims=True
            )
            da[rows, :] = d - split_three(jnp.broadcast_to(delta, (128, 128)), place, outside)
            return carry

        lax.fori_loop(0, rows_all // 128, prepare, 0)

        def step(rows, keys, mask, keep, dk, dv):
            st = dot_nt(ka[keys, :], qa[rows, :])
            if mask is not None:
                st = st + mask
            p = jnp.exp2(st)
            dp = dot_nt(va[keys, :], da[rows, :])
            ds = (p * dp).astype(jnp.bfloat16)
            dv[keep, :] += dot_nn(p.astype(jnp.bfloat16), dm[rows, :])
            dk[keep, :] += dot_nn(ds, qm[rows, :])
            dqs[rows, :] += jnp.where(inside, dot_tn(ds, ka[keys, :]), 0.0)

        span = parts * QT
        for tile in range(tiles):
            rows = pl.ds(tile * QT, QT)
            for near in range(tile + 1):
                keys = pl.ds(near * span, span)
                step(rows, keys, mt_ref[tile] if near == tile else None, keys, dkt, dvt)
        count = QT if (groups * GROUP) % QT == 0 else 128

        def far_body(index, carry):
            rows = pl.ds(pl.multiple_of(own + index * count, 128), count)
            keys = pl.ds(0, TRUNK)
            step(rows, keys, None, keys, dkt, dvt)
            return carry

        lax.fori_loop(0, groups * GROUP // count, far_body, 0)

        def near_body(group, carry):
            rows = pl.ds(pl.multiple_of(own + group * GROUP, 128), GROUP)
            keys = pl.ds(pl.multiple_of(TRUNK + group * GROUP, 128), GROUP)
            keep = pl.ds(pl.multiple_of(group * GROUP, 128), GROUP)
            step(rows, keys, mg_ref[group], keep, dkg, dvg)
            return carry

        return lax.fori_loop(0, groups, near_body, carry)

    lax.fori_loop(0, jnp.minimum(2, heads - 2 * pair), head_body, 0)
    dq_ref[...] = (dqs[...] * HEAD_DIM**-0.5).astype(jnp.bfloat16)
    dk_ref[own:, :] = dkg[...] * LN2
    dv_ref[own:, :] = dvg[...]
    for tile in range(tiles):
        for part in range(parts):
            source = pl.ds((tile * parts + part) * QT, QT)
            if part == 0:
                dk_ref[tile * QT : (tile + 1) * QT, :] = dkt[source, :] * LN2
                dv_ref[tile * QT : (tile + 1) * QT, :] = dvt[source, :]
            else:
                start = (part - 1) * own + tile * QT
                dko_ref[start : start + QT, :] = (dkt[source, :] * LN2).astype(jnp.bfloat16)
                dvo_ref[start : start + QT, :] = dvt[source, :].astype(jnp.bfloat16)


def attention_backward(
    parts, heads, triple, others, mixed, mixed_grad, lse, mask_trunk, mask_group, start, stop, deps=()
):
    rows = triple.shape[0]
    pairs = triple.shape[1] // (3 * 128)
    extra = others.shape[0]
    block = lambda count, shift: pl.BlockSpec((count, 128), lambda i: (0, i + shift))
    whole = lambda shape: pl.BlockSpec(shape, lambda i: (0,) * len(shape))
    near = rows - TRUNK // parts
    return pl.pallas_call(
        partial(bwd_kernel, parts, heads, start, len(deps)),
        grid=(stop - start,),
        in_specs=[
            block(rows, start),
            block(rows, start + pairs),
            block(rows, start + 2 * pairs),
            block(extra, start),
            block(extra, start + pairs),
            block(rows, start),
            block(rows, start),
            block(rows, start),
            whole(mask_trunk.shape),
            whole(mask_group.shape),
        ]
        + [pl.BlockSpec(memory_space=pl.ANY)] * len(deps),
        out_specs=[block(rows, 0), block(rows, 0), block(rows, 0), block(extra, 0), block(extra, 0)],
        out_shape=[
            jax.ShapeDtypeStruct((rows, (stop - start) * 128), jnp.bfloat16),
            jax.ShapeDtypeStruct((rows, (stop - start) * 128), jnp.float32),
            jax.ShapeDtypeStruct((rows, (stop - start) * 128), jnp.float32),
            jax.ShapeDtypeStruct((extra, (stop - start) * 128), jnp.bfloat16),
            jax.ShapeDtypeStruct((extra, (stop - start) * 128), jnp.bfloat16),
        ],
        scratch_shapes=[
            pltpu.VMEM((TRUNK, 128), jnp.bfloat16),
            pltpu.VMEM((TRUNK, 128), jnp.bfloat16),
            pltpu.VMEM((TRUNK + near, 128), jnp.bfloat16),
            pltpu.VMEM((TRUNK + near, 128), jnp.bfloat16),
            pltpu.VMEM((rows, 128), jnp.bfloat16),
            pltpu.VMEM((rows, 128), jnp.bfloat16),
            pltpu.VMEM((rows, 128), jnp.bfloat16),
            pltpu.VMEM((rows, 128), jnp.bfloat16),
            pltpu.VMEM((TRUNK, 128), jnp.float32),
            pltpu.VMEM((TRUNK, 128), jnp.float32),
            pltpu.VMEM((near, 128), jnp.float32),
            pltpu.VMEM((near, 128), jnp.float32),
            pltpu.VMEM((rows, 128), jnp.float32),
        ],
        compiler_params=pltpu.CompilerParams(vmem_limit_bytes=56 * 1024 * 1024),
        cost_estimate=pl.CostEstimate(
            flops=(stop - start) * rows * 12_200_000, bytes_accessed=rows * pairs * 4000, transcendentals=0
        ),
        name="attention_backward",
    )(triple, triple, triple, others, others, mixed, mixed_grad, lse, mask_trunk, mask_group, *deps)


ERF_TOP = (
    -2.72614225801306e-10, 2.77068142495902e-08, -2.10102402082508e-06, -5.69250639462346e-05,
    -7.34990630326855e-04, -2.95459980854025e-03, -1.60960333262415e-02,
)
ERF_LOW = (
    -1.45660718464996e-05, -2.13374055278905e-04, -1.68282697438203e-03, -7.37332916720468e-03,
    -1.42647390514189e-02,
)


def erf_float(value):
    value = jnp.clip(value, -3.832506856900711, 3.832506856900711)
    square = value * value
    top = jnp.full_like(value, ERF_TOP[0])
    for c in ERF_TOP[1:]:
        top = top * square + c
    low = jnp.full_like(value, ERF_LOW[0])
    for c in ERF_LOW[1:]:
        low = low * square + c
    return value * top / low


FF_BLOCK = 256
ROW_CHUNK = 640


def ffn_kernel(
    sizes, outs, chunk, scalars, *refs,
):
    count = len(sizes)
    mine, theirs = refs[:count], refs[count : 2 * count]
    second, second_t, seed, seed_t, bias = refs[2 * count : 2 * count + 5]
    edge = 2 * count + 8
    lowered, second_grad, bias_grad = refs[2 * count + 5 : edge]
    mine_grads, theirs_grads = refs[edge : edge + outs], refs[edge + outs : edge + 2 * outs]
    up, down, act, wide, up_grad, down_grad = refs[edge + 2 * outs :]
    step = pl.program_id(0)
    role = scalars[0]

    def place(first_part, second_part):
        for index, size in enumerate(sizes):
            rows = pl.ds(pl.multiple_of(scalars[1 + index], 16), size)
            up[rows, :] = first_part[index][...]
            down[rows, :] = second_part[index][...]

    @pl.when(role == 0)
    def _():
        place(mine, theirs)

    @pl.when(role != 0)
    def _():
        place(theirs, mine)

    @pl.when(step == 0)
    def _():
        lowered[...] = jnp.zeros_like(lowered)
        second_grad[...] = jnp.zeros_like(second_grad)

    total = jnp.zeros((1, FF_BLOCK), jnp.float32)
    for start in range(0, second.shape[0], chunk):
        rows = pl.ds(start, chunk)
        wide_in = dot_nn(second[rows, :], up[...]) + bias[...]
        hidden = dot_nn(seed[rows, :], down[...])
        share = 0.5 + 0.5 * erf_float(wide_in * 0.7071067811865476)
        act_now = (wide_in * share).astype(jnp.bfloat16)
        slope = share + wide_in * (jnp.exp(-0.5 * wide_in * wide_in) * 0.3989422804014327)
        wide_now = (hidden * slope).astype(jnp.bfloat16)
        total += jnp.sum(wide_now.astype(jnp.float32), axis=0, keepdims=True)
        act[rows, :] = act_now
        wide[rows, :] = wide_now
        lowered[rows, :] += dot_nt(act_now, down[...])
        second_grad[rows, :] += dot_nt(wide_now, up[...])
    bias_grad[...] = total
    up_grad[...] = dot_nn(second_t[...], wide[...]).astype(jnp.bfloat16)
    down_grad[...] = dot_nn(seed_t[...], act[...]).astype(jnp.bfloat16)

    def deliver(first_grad, second_grad):
        for index in range(outs):
            size = mine_grads[index].shape[0]
            rows = pl.ds(pl.multiple_of(scalars[1 + index], 16), size)
            mine_grads[index][...] = first_grad[rows, :]
            theirs_grads[index][...] = second_grad[rows, :]

    @pl.when(role == 0)
    def _():
        deliver(up_grad, down_grad)

    @pl.when(role != 0)
    def _():
        deliver(down_grad, up_grad)


def feed_forward(scalars, mine, theirs, second, seed, bias, outs):
    rows, width = second.shape
    hidden = mine[0].shape[1]
    sizes = tuple(piece.shape[0] for piece in mine)
    piece_specs = [pl.BlockSpec((size, FF_BLOCK), lambda j, s: (0, j)) for size in sizes]
    whole = lambda shape: pl.BlockSpec(shape, lambda j, s: (0, 0))
    grad_spec = pl.BlockSpec((width // outs, FF_BLOCK), lambda j, s: (0, j))
    grad_shape = jax.ShapeDtypeStruct((width // outs, hidden), jnp.bfloat16)
    line = pl.BlockSpec((1, FF_BLOCK), lambda j, s: (0, j))
    chunk = ROW_CHUNK if rows % ROW_CHUNK == 0 else rows // 2
    return pl.pallas_call(
        partial(ffn_kernel, sizes, outs, chunk),
        grid_spec=pltpu.PrefetchScalarGridSpec(
            num_scalar_prefetch=1,
            grid=(hidden // FF_BLOCK,),
            in_specs=piece_specs * 2 + [
                whole((rows, width)), whole((width, rows)), whole((rows, width)), whole((width, rows)), line,
            ],
            out_specs=[whole((rows, width)), whole((rows, width)), line] + [grad_spec] * (2 * outs),
            scratch_shapes=[
                pltpu.VMEM((width, FF_BLOCK), jnp.bfloat16),
                pltpu.VMEM((width, FF_BLOCK), jnp.bfloat16),
                pltpu.VMEM((rows, FF_BLOCK), jnp.bfloat16),
                pltpu.VMEM((rows, FF_BLOCK), jnp.bfloat16),
                pltpu.VMEM((width, FF_BLOCK), jnp.bfloat16),
                pltpu.VMEM((width, FF_BLOCK), jnp.bfloat16),
            ],
        ),
        out_shape=[
            jax.ShapeDtypeStruct((rows, width), jnp.float32),
            jax.ShapeDtypeStruct((rows, width), jnp.float32),
            jax.ShapeDtypeStruct((1, hidden), jnp.float32),
        ]
        + [grad_shape] * (2 * outs),
        compiler_params=pltpu.CompilerParams(vmem_limit_bytes=60 * 1024 * 1024),
        cost_estimate=pl.CostEstimate(
            flops=24 * rows * width * hidden, bytes_accessed=8 * width * hidden + 20 * rows * width,
            transcendentals=rows * hidden,
        ),
        name="feed_forward",
    )(scalars, *mine, *theirs, second, second.T, seed, seed.T, bias.reshape(1, hidden))


def layer_norm(value, gain, bias):
    center = value - jnp.mean(value, axis=-1, keepdims=True)
    spread = jnp.mean(center * center, axis=-1, keepdims=True)
    return center * lax.rsqrt(spread + 1e-05) * gain + bias


def own_rows(parts, part):
    blocks = TRUNK // (128 * parts)
    starts = []
    for k in range(blocks):
        base = (k // 2) * 2 * parts
        starts.append(128 * (base + (part if k % 2 == 0 else 2 * parts - 1 - part)))
    rows = [np.arange(128) + s for s in starts]
    groups = (TRUNK // 256) // parts
    rows.append(TRUNK + part * groups * GROUP + np.arange(groups * GROUP))
    return np.concatenate(rows)


def spread_kernel(grain, table, *refs):
    pieces, out = refs[:-1], refs[-1]
    each = pieces[0].shape[0] // grain
    for index, piece in enumerate(pieces):
        for i in range(each):
            target = table[index * each + i]

            @pl.when(target >= 0)
            def _():
                rows = pl.ds(pl.multiple_of(target * grain, grain), grain)
                out[rows, :] = piece[i * grain : (i + 1) * grain, :]


def spread(table, pieces, grain, count):
    width = pieces[0].shape[1]
    whole = lambda rows: pl.BlockSpec((rows, width), lambda i, s: (0, 0))
    return pl.pallas_call(
        partial(spread_kernel, grain),
        grid_spec=pltpu.PrefetchScalarGridSpec(
            num_scalar_prefetch=1,
            grid=(1,),
            in_specs=[whole(p.shape[0]) for p in pieces],
            out_specs=whole(count),
        ),
        out_shape=jax.ShapeDtypeStruct((count, width), pieces[0].dtype),
        compiler_params=pltpu.CompilerParams(vmem_limit_bytes=48 * 1024 * 1024),
        cost_estimate=pl.CostEstimate(flops=0, bytes_accessed=6 * count * width, transcendentals=0),
        name="spread_rows",
    )(table, *pieces)


def collect_kernel(grain, count, table, *refs):
    sources, outs = refs[:-count], refs[-count:]
    each = outs[0].shape[0] // grain
    for index, out in enumerate(outs):
        for i in range(each):
            owner = table[2 * (index * each + i)]
            start = table[2 * (index * each + i) + 1]
            for which, source in enumerate(sources):

                @pl.when(owner == which)
                def _():
                    rows = pl.ds(pl.multiple_of(start * grain, grain), grain)
                    out[i * grain : (i + 1) * grain, :] = source[rows, :]


def collect(table, sources, grain, count, length):
    width = sources[0].shape[1]
    whole = lambda rows: pl.BlockSpec((rows, width), lambda i, s: (0, 0))
    return pl.pallas_call(
        partial(collect_kernel, grain, count),
        grid_spec=pltpu.PrefetchScalarGridSpec(
            num_scalar_prefetch=1,
            grid=(1,),
            in_specs=[whole(s.shape[0]) for s in sources],
            out_specs=[whole(length)] * count,
        ),
        out_shape=[jax.ShapeDtypeStruct((length, width), sources[0].dtype)] * count,
        compiler_params=pltpu.CompilerParams(vmem_limit_bytes=48 * 1024 * 1024),
        cost_estimate=pl.CostEstimate(flops=0, bytes_accessed=6 * count * length * width, transcendentals=0),
        name="collect_rows",
    )(table, *sources)


class Place:
    def __init__(self, micro, tree):
        self.columns = lax.axis_size("col")
        self.micro = micro
        self.parts = self.columns // micro
        self.tree = tree
        self.length = tree // self.columns
        self.grain = math.gcd(self.length, 128)
        me = lax.axis_index("col")
        self.quarter, self.part = me // self.parts, me % self.parts
        self.own = np.stack([own_rows(self.parts, part) for part in range(self.parts)])
        self.count = self.own.shape[1]

    def quarter_perm(self, shift):
        p = self.parts
        return [(c, ((c // p) ^ shift) * p + c % p) for c in range(self.columns)]

    def part_perm(self, shift):
        return [(c, c ^ shift) for c in range(self.columns)]

    def swap_quarters(self, value):
        groups = [
            [q * self.parts + part for q in range(self.micro)] for part in range(self.parts)
        ]
        return lax.all_to_all(value, "col", 0, 0, axis_index_groups=groups, tiled=True)

    def to_tree_sources(self, value):
        mine = self.swap_quarters(value).reshape(self.micro * self.length, value.shape[2])
        return [mine] + [lax.ppermute(mine, "col", self.part_perm(e)) for e in range(1, self.parts)]

    def to_tree(self, sources):
        grain, each = self.grain, self.length // self.grain
        table = np.full((self.parts, self.tree // grain), -1, np.int32)
        for part in range(self.parts):
            table[part, self.own[part, ::grain] // grain] = np.arange(self.count // grain)
        mine = lax.dynamic_index_in_dim(jnp.asarray(table), self.part, 0, keepdims=False)
        e, rest = np.divmod(np.arange(self.tree // grain, dtype=np.int32), self.micro * each)
        quarter, inside = np.divmod(rest, each)
        chunk = (quarter * self.parts + (self.part ^ e)) * each + inside
        return spread(mine[chunk], sources, grain, self.count)

    def from_tree_sources(self, value):
        return [value] + [lax.ppermute(value, "col", self.part_perm(e)) for e in range(1, self.parts)]

    def from_tree_parts(self, sources):
        grain, each, parts = self.grain, self.length // self.grain, self.parts
        owner = np.zeros(self.tree // grain, np.int32)
        local = np.zeros(self.tree // grain, np.int32)
        for part in range(parts):
            owner[self.own[part, ::grain] // grain] = part
            local[self.own[part, ::grain] // grain] = np.arange(self.count // grain)
        quarter, inside = np.divmod(np.arange(self.micro * each, dtype=np.int32), each)
        chunk = (quarter * parts + self.part) * each + inside
        table = jnp.stack([jnp.asarray(owner)[chunk] ^ self.part, jnp.asarray(local)[chunk]], axis=1)
        (out,) = collect(table.reshape(-1), sources, grain, 1, self.micro * self.length)
        return out.reshape(self.micro, self.length, sources[0].shape[1])

    def masks(self, own_ids, parent_ids):
        parts = self.parts
        own = jnp.asarray(self.own, jnp.int32)
        mine = lax.dynamic_index_in_dim(own, self.part, 0, keepdims=False)
        trunk_rows = TRUNK // parts
        tiles = trunk_rows // QT
        trunk = []
        for tile in range(tiles):
            span = slice(tile * QT, (tile + 1) * QT)
            keys = jnp.concatenate(
                [
                    lax.dynamic_index_in_dim(own, self.part ^ e, 0, keepdims=False)[span]
                    for e in range(parts)
                ]
            )
            trunk.append(jnp.where(keys[None, :] <= mine[span][:, None], 0.0, -1e30))
        group = []
        groups = (TRUNK // 256) // parts
        places = jnp.arange(GROUP)
        for g in range(groups):
            start = TRUNK + (self.part * groups + g) * GROUP
            ids = lax.dynamic_slice_in_dim(own_ids, start, GROUP)
            parent = lax.dynamic_slice_in_dim(parent_ids, start, GROUP)
            seen = (places[None, :] <= places[:, None]) & (
                (ids[None, :] == 0) | (ids[None, :] == ids[:, None]) | (ids[None, :] == parent[:, None])
            )
            group.append(jnp.where(seen, 0.0, -1e30))
        return jnp.stack(trunk).astype(jnp.float32), jnp.stack(group).astype(jnp.float32)


BOTH = ("row", "col")
ROW_CUT = 144


def plain_gather(block):
    full = lax.all_gather(block, BOTH, axis=0, tiled=False)
    full = full.reshape(lax.axis_size("row"), lax.axis_size("col"), *block.shape)
    return full.transpose(0, 2, 1, 3).reshape(full.shape[0] * full.shape[2], full.shape[1] * full.shape[3])


def plain_scatter(grad):
    rows, cols = lax.axis_size("row"), lax.axis_size("col")
    blocks = grad.astype(jnp.bfloat16).reshape(rows, grad.shape[0] // rows, cols, grad.shape[1] // cols)
    blocks = blocks.transpose(0, 2, 1, 3).reshape(rows * cols, grad.shape[0] // rows, grad.shape[1] // cols)
    return lax.psum_scatter(blocks, BOTH, scatter_dimension=0, tiled=False).astype(jnp.float32)


def across(value, shift):
    return lax.ppermute(value, "row", [(r, r ^ shift) for r in range(lax.axis_size("row"))])


def row_gather(block):
    beside = across(block, 1)
    below = across(block, 2)
    return [block, beside, below, across(beside[:ROW_CUT], 2), across(below[ROW_CUT:], 1)]


def row_starts(rows):
    me = lax.axis_index("row")
    far = (me ^ 3) * rows
    return [me * rows, (me ^ 1) * rows, (me ^ 2) * rows, far, far + ROW_CUT]


def core_swap(place, value):
    return lax.ppermute(value, "col", place.part_perm(1))


def far_sums(own, swapped):
    f32, bf16 = jnp.float32, jnp.bfloat16
    add = lambda d, part: (own[d][part].astype(f32) + swapped[d][part].astype(f32)).astype(bf16)
    top, bottom = slice(0, ROW_CUT), slice(ROW_CUT, None)
    return add(3, top), add(3, bottom), add(1, bottom), add(2, top)


def far_sends(sums):
    return across(sums[0], 2), across(sums[1], 1), across(sums[2], 1), across(sums[3], 2)


def near_sums(own, swapped, received):
    f32 = jnp.float32
    beside = own[1][:ROW_CUT].astype(f32) + swapped[1][:ROW_CUT].astype(f32) + received[0].astype(f32)
    below = own[2][ROW_CUT:].astype(f32) + swapped[2][ROW_CUT:].astype(f32) + received[1].astype(f32)
    return beside.astype(jnp.bfloat16), below.astype(jnp.bfloat16)


def near_sends(sums):
    return across(sums[0], 1), across(sums[1], 2)


def row_total(own, swapped, received, last):
    f32 = jnp.float32
    base = own[0].astype(f32) + swapped[0].astype(f32)
    beside = jnp.concatenate([last[0], received[2]], axis=0).astype(f32)
    below = jnp.concatenate([received[3], last[1]], axis=0).astype(f32)
    return (base + beside + below).astype(jnp.bfloat16)


def column_scatter(place, pick):
    total = pick(0)
    for d in range(1, place.micro):
        total = total + lax.ppermute(
            pick(d).astype(jnp.bfloat16), "col", place.quarter_perm(d)
        ).astype(jnp.float32)
    return total


def sum_all(values):
    sizes = [v.shape[0] for v in values]
    flat = jnp.concatenate(values)
    flat = jnp.pad(flat, (0, -flat.shape[0] % 1024)).reshape(-1, 128)
    for axis in ("col", "row"):
        size = lax.axis_size(axis)
        shift = 1
        while shift < size:
            flat = flat + lax.ppermute(flat, axis, [(i, i ^ shift) for i in range(size)])
            shift *= 2
    flat = flat.reshape(-1)
    out, start = [], 0
    for size in sizes:
        out.append(flat[start : start + size])
        start += size
    return out


def assemble_kernel(sizes, edge, scalars, *refs):
    count = len(sizes)
    mine, theirs = refs[:count], refs[count : 2 * count]
    triple, out = refs[2 * count :]
    step = pl.program_id(0)
    use_mine = (step < edge) == (scalars[0] == 0)
    total = sum(sizes)

    def fill(target, pieces):
        for index, size in enumerate(sizes):
            rows = pl.ds(pl.multiple_of(scalars[1 + index], 16), size)
            target[rows, :] = pieces[index][...]

    for own in (True, False):
        for low in (True, False):

            @pl.when(jnp.logical_and(use_mine == own, (step < edge + edge // 2) == low))
            def _():
                fill(triple if low else out, mine if own else theirs)

    @pl.when(step >= edge + edge // 2)
    def _():
        out[total:, :] = jnp.zeros((out.shape[0] - total, out.shape[1]), out.dtype)


def assemble(scalars, mine, theirs, padded):
    block = 384
    edge = 2 * padded // block
    sizes = tuple(piece.shape[0] for piece in mine)
    width = sum(sizes)

    def source(own):
        def index(j, s):
            first = (s[0] == 0) if own else (s[0] != 0)
            return (0, jnp.where(first, jnp.minimum(j, edge - 1), jnp.maximum(j - edge, 0)))

        return [pl.BlockSpec((size, block), index) for size in sizes]

    return pl.pallas_call(
        partial(assemble_kernel, sizes, edge),
        grid_spec=pltpu.PrefetchScalarGridSpec(
            num_scalar_prefetch=1,
            grid=(2 * edge,),
            in_specs=source(True) + source(False),
            out_specs=[
                pl.BlockSpec((width, block), lambda j, s: (0, jnp.minimum(j, 3 * edge // 2 - 1))),
                pl.BlockSpec((padded, block), lambda j, s: (0, jnp.maximum(j - 3 * edge // 2, 0))),
            ],
        ),
        out_shape=[
            jax.ShapeDtypeStruct((width, 3 * padded), jnp.bfloat16),
            jax.ShapeDtypeStruct((padded, padded), jnp.bfloat16),
        ],
        compiler_params=pltpu.CompilerParams(vmem_limit_bytes=48 * 1024 * 1024),
        cost_estimate=pl.CostEstimate(flops=0, bytes_accessed=16 * width * padded, transcendentals=0),
        name="assemble_weights",
    )(scalars, *mine, *theirs)


class QuickWeights:
    def __init__(self, place, w_qkv, w_out, w_up, w_down, padded):
        self.place, self.padded = place, padded
        self.rows = w_qkv.shape[0]
        self.cols = place.columns
        self.width = w_out.shape[1] * self.cols
        self.qkv_cols, self.out_cols, self.up_cols = w_qkv.shape[1], w_out.shape[1], w_up.shape[1]
        self.main = self.up_cols // 256 * 256
        self.rest = self.up_cols - self.main
        starts = row_starts(self.rows)
        self.role = place.part
        self.scalars = jnp.stack([self.role] + starts).astype(jnp.int32)
        pad = padded - self.width

        pack = jnp.concatenate([w_qkv, w_out], axis=1)
        full = lax.all_gather(pack, "col", axis=0, tiled=False).transpose(1, 0, 2)
        qkv = full[:, :, : self.qkv_cols].reshape(self.rows, 3, self.width)
        out = full[:, :, self.qkv_cols :].reshape(self.rows, 1, self.width)
        four = jnp.pad(jnp.concatenate([qkv, out], axis=1), ((0, 0), (0, 0), (0, pad)))
        mine = jnp.where(self.role == 0, four[:, :2], four[:, 2:]).reshape(self.rows, 2 * padded)
        mine = row_gather(mine)
        theirs = [core_swap(place, piece) for piece in mine]
        self.triple, self.out = assemble(self.scalars, mine, theirs, padded)

        main = self.main
        down = w_down.T
        pack = jnp.concatenate([w_up[:, :main], down[:, :main], w_up[:, main:], down[:, main:]], axis=1)
        full = lax.all_gather(pack, "col", axis=0, tiled=False)
        rest = self.rest

        def role_part(role):
            body = full[:, :, role * main : (role + 1) * main].transpose(1, 0, 2)
            tail = full[:, :, 2 * main + role * rest : 2 * main + (role + 1) * rest].transpose(1, 0, 2)
            return jnp.concatenate(
                [body.reshape(self.rows, self.cols * main), tail.reshape(self.rows, self.cols * rest)], axis=1
            )

        self.mine = row_gather(jnp.where(self.role == 0, role_part(0), role_part(1)))
        self.theirs = [core_swap(place, piece) for piece in self.mine]

    def bias_order(self, bias):
        blocks = bias.reshape(self.cols, self.up_cols)
        return jnp.concatenate([blocks[:, : self.main].reshape(-1), blocks[:, self.main :].reshape(-1)])

    def bias_back(self, grad):
        edge = self.cols * self.main
        return jnp.concatenate(
            [grad[:edge].reshape(self.cols, self.main), grad[edge:].reshape(self.cols, self.rest)], axis=1
        ).reshape(-1)

    def pair_total(self, total):
        place = self.place
        other = core_swap(place, total)
        edge = self.cols * self.main

        def pick(d):
            shard = (place.quarter ^ d) * place.parts + place.part
            out = []
            for start, size in ((0, self.main), (edge, self.rest)):
                for value in (total, other):
                    out.append(lax.dynamic_slice_in_dim(value, start + shard * size, size, 1))
            return jnp.concatenate(out, axis=1).astype(jnp.float32)

        final = column_scatter(place, pick)
        main, rest = self.main, self.rest
        own = jnp.concatenate([final[:, :main], final[:, 2 * main : 2 * main + rest]], axis=1)
        far = jnp.concatenate([final[:, main : 2 * main], final[:, 2 * main + rest :]], axis=1)
        up = jnp.where(self.role == 0, own, far)
        down = jnp.where(self.role == 0, far, own)
        return up, down.T

    def first_pieces(self, triple_grad, out_grad):
        padded, rows = self.padded, self.rows
        low = triple_grad[:, : 2 * padded]
        high = jnp.concatenate([triple_grad[:, 2 * padded :], out_grad], axis=1)
        mine = jnp.where(self.role == 0, low, high)
        theirs = jnp.where(self.role == 0, high, low)
        me = lax.axis_index("row")
        cut = lambda value: [
            lax.dynamic_slice_in_dim(value, (me ^ d) * rows, rows, 0) for d in range(4)
        ]
        return cut(mine), cut(theirs)

    def first_total(self, total):
        place, padded, width = self.place, self.padded, self.width
        other = core_swap(place, total)
        low = jnp.where(self.role == 0, total, other).reshape(self.rows, 2, padded)
        high = jnp.where(self.role == 0, other, total).reshape(self.rows, 2, padded)
        four = jnp.concatenate([low, high], axis=1)[:, :, :width]
        qkv = four[:, :3].reshape(self.rows, self.cols, self.qkv_cols)
        out = four[:, 3].reshape(self.rows, self.cols, self.out_cols)
        blocks = jnp.concatenate([qkv, out], axis=2).transpose(1, 0, 2)

        def pick(d):
            shard = (place.quarter ^ d) * place.parts + place.part
            return lax.dynamic_index_in_dim(blocks, shard, 0, keepdims=False).astype(jnp.float32)

        final = column_scatter(place, pick)
        return final[:, : self.qkv_cols], final[:, self.qkv_cols :]


class PlainWeights:
    def __init__(self, place, w_qkv, w_out, w_up, w_down, padded):
        self.place, self.padded = place, padded
        qkv, out = plain_gather(w_qkv), plain_gather(w_out)
        self.width = width = out.shape[1]
        pad = padded - width
        self.triple = jnp.pad(qkv.reshape(width, 3, width), ((0, 0), (0, 0), (0, pad))).reshape(
            width, 3 * padded
        )
        self.out = jnp.pad(out, ((0, pad), (0, pad)))
        self.mine = [plain_gather(w_up)]
        self.theirs = [plain_gather(w_down.T)]
        self.scalars = jnp.zeros((2,), jnp.int32)

    def bias_order(self, bias):
        return bias

    def bias_back(self, grad):
        return grad

    def scatter_pair(self, mine, theirs):
        return plain_scatter(mine), plain_scatter(theirs).T

    def scatter_first(self, triple_grad, out_grad):
        width, padded = self.width, self.padded
        qkv = triple_grad.reshape(width, 3, padded)[:, :, :width].reshape(width, 3 * width)
        return plain_scatter(qkv), plain_scatter(out_grad[:, :width])


def cuts_of(pairs, count):
    edges = [round(i * pairs / count) for i in range(count + 1)]
    return list(zip(edges[:-1], edges[1:]))


def local(
    block_input, paths, ln1_gain, ln1_bias, w_qkv, q_bias, v_bias, w_out, out_bias,
    ln2_gain, ln2_bias, w_up, up_bias, w_down, down_bias, cotangent,
):
    micro, _, width = block_input.shape
    place = Place(micro, paths.shape[2])
    parts = place.parts
    heads = width // HEAD_DIM
    padded = (heads + 1) // 2 * 128
    pairs = padded // 128
    pad = padded - width
    own_trunk = TRUNK // parts
    f32, bf16 = jnp.float32, jnp.bfloat16

    quick = lax.axis_size("row") == 4 and parts == 2 and w_qkv.shape[0] == 272
    weights = (QuickWeights if quick else PlainWeights)(place, w_qkv, w_out, w_up, w_down, padded)

    own_ids = lax.dynamic_index_in_dim(paths[0], place.quarter, 0, keepdims=False)
    parent_ids = lax.dynamic_index_in_dim(paths[1], place.quarter, 0, keepdims=False)
    mask_trunk, mask_group = place.masks(own_ids, parent_ids)

    rows_in = place.to_tree(place.to_tree_sources(block_input)).astype(f32)
    seed_rows = place.to_tree(place.to_tree_sources(cotangent))

    q_scale = HEAD_DIM**-0.5 * LOG2E
    triple_bias = jnp.concatenate(
        [jnp.pad(q_bias * q_scale, (0, pad)), jnp.zeros((padded,), f32), jnp.pad(v_bias, (0, pad))]
    )
    triple_scale = jnp.concatenate([jnp.full((padded,), q_scale, f32), jnp.ones((2 * padded,), f32)])
    first = layer_norm(rows_in, ln1_gain, ln1_bias).astype(bf16)
    triple = (dot_nn(first, weights.triple) * triple_scale + triple_bias).astype(bf16)
    shared = triple[:own_trunk, padded:]
    others = jnp.concatenate(
        [lax.ppermute(shared, "col", place.part_perm(e)) for e in range(1, parts)], axis=0
    )
    forward_cuts, backward_cuts = cuts_of(pairs, 3), cuts_of(pairs, 4)
    mixed, lse = [], []
    for start, stop in forward_cuts:
        one, two = attention_forward(
            parts, heads, triple, others, mask_trunk, mask_group, start, stop
        )
        mixed.append(one)
        lse.append(two)
    mixed, lse = jnp.concatenate(mixed, axis=1), jnp.concatenate(lse, axis=1)
    out_weight = weights.out[:, :width]
    attended = (dot_nn(mixed, out_weight) + out_bias).astype(bf16)
    middle = rows_in + attended.astype(f32)
    second = layer_norm(middle, ln2_gain, ln2_bias).astype(bf16)
    seed = seed_rows.astype(f32)
    outs = 4 if quick else 1
    lowered, second_grad, up_bias_grad, *pair_grads = feed_forward(
        weights.scalars, weights.mine, weights.theirs, second, seed_rows, weights.bias_order(up_bias), outs
    )
    pair_mine, pair_theirs = pair_grads[:outs], pair_grads[outs:]
    up_bias_grad = weights.bias_back(up_bias_grad.reshape(-1))
    result = (middle + lowered + down_bias).astype(bf16)

    down_bias_grad = jnp.sum(seed, axis=0)
    norm_grad, gain_two, shift_two = jax.vjp(layer_norm, middle, ln2_gain, ln2_bias)[1](second_grad)
    middle_grad = seed + norm_grad
    attended_grad = middle_grad.astype(bf16)
    out_bias_grad = jnp.sum(attended_grad.astype(f32), axis=0)
    out_weight_grad = dot_tn(mixed, attended_grad)[:width].astype(bf16)
    mixed_grad = dot_nt(attended_grad, out_weight).astype(bf16)
    early = sum_all([out_bias_grad, gain_two, shift_two, up_bias_grad, down_bias_grad])

    turned = jnp.swapaxes(mask_trunk, 1, 2), jnp.swapaxes(mask_group, 1, 2)
    result_sources = place.from_tree_sources(result)
    if quick:
        pair_swapped = {d: core_swap(place, pair_theirs[d]) for d in (3, 1, 2, 0)}
        sums = far_sums(pair_mine, pair_swapped)
    grads = []
    for index, (start, stop) in enumerate(backward_cuts):
        deps = ()
        if quick and index == 0:
            deps = sums
            received = far_sends(sums)
        if index == 1:
            result_parts = place.from_tree_parts(result_sources)
            deps = (result_parts,)
            result_out = place.swap_quarters(result_parts)
            if quick:
                sums = near_sums(pair_mine, pair_swapped, received)
                deps = deps + sums
                last = near_sends(sums)
        if quick and index == 3:
            total = row_total(pair_mine, pair_swapped, received, last)
            deps = (total,)
        grads.append(
            attention_backward(
                parts, heads, triple, others, mixed, mixed_grad, lse, *turned, start, stop, deps
            )
        )
    if quick:
        up_grad, down_grad = weights.pair_total(total)
    else:
        up_grad, down_grad = weights.scatter_pair(pair_mine[0], pair_theirs[0])
    dq, dk, dv, dko, dvo = (jnp.concatenate(part, axis=1) for part in zip(*grads))
    both = jnp.concatenate([dko, dvo], axis=1)
    key_value = jnp.concatenate([dk, dv], axis=1)
    for e in range(1, parts):
        block = both[(e - 1) * own_trunk : e * own_trunk]
        key_value = key_value.at[:own_trunk].add(
            lax.ppermute(block, "col", place.part_perm(e)).astype(f32)
        )
    triple_grad = jnp.concatenate([dq, key_value.astype(bf16)], axis=1)
    first_grad = dot_nt(triple_grad, weights.triple)
    q_bias_grad = jnp.sum(triple_grad[:, :width].astype(f32), axis=0)
    v_bias_grad = jnp.sum(triple_grad[:, 2 * padded : 2 * padded + width].astype(f32), axis=0)
    norm_grad, gain_one, shift_one = jax.vjp(layer_norm, rows_in, ln1_gain, ln1_bias)[1](first_grad)
    input_grad = (middle_grad + norm_grad).astype(bf16)
    input_grad_out = place.swap_quarters(place.from_tree_parts(place.from_tree_sources(input_grad)))
    triple_weight_grad = dot_tn(first, triple_grad).astype(bf16)
    out_padded = jnp.pad(out_weight_grad, ((0, 0), (0, pad)))
    if quick:
        mine, theirs = weights.first_pieces(triple_weight_grad, out_padded)
        swapped = {d: core_swap(place, theirs[d]) for d in (3, 1, 2, 0)}
        received = far_sends(far_sums(mine, swapped))
        last = near_sends(near_sums(mine, swapped, received))
        qkv_grad, out_grad = weights.first_total(row_total(mine, swapped, received, last))
    else:
        qkv_grad, out_grad = weights.scatter_first(triple_weight_grad, out_padded)
    late = sum_all([gain_one, shift_one, q_bias_grad, v_bias_grad])
    return (
        result_out, input_grad_out, late[0], late[1], qkv_grad, late[2], late[3],
        out_grad, early[0], early[1], early[2], up_grad, early[3], down_grad, early[4],
    )


def solution(mesh):
    rows = P(None, BOTH, None)
    placed = (
        rows, P(None, None, "row"), P(), P(), P("row", "col"), P(), P(), P("row", "col"), P(),
        P(), P(), P("row", "col"), P(), P("col", "row"), P(), rows,
    )
    out = (
        rows, rows, P(), P(), P("row", "col"), P(), P(), P("row", "col"), P(),
        P(), P(), P("row", "col"), P(), P("col", "row"), P(),
    )
    return jax.shard_map(local, mesh=mesh, in_specs=placed, out_specs=out, check_vma=False)
```

time: 5370 us -> 1160 us (0.22)
  waiting for transfers between devices: 2790 us -> 319 us
  matrix products: 1000 us -> 60.7 us
  blocking collectives: 899 us -> 0 us
  Pallas kernels: 0 us -> 356 us
  other arithmetic: 278 us -> 123 us
  local copies, waits for them, and re-layouts: 321 us -> 212 us
    reduce_scatter x25 -> x0, waiting for transfers between devices: 1900 us -> none  [the longest x16 1500 us: sum_back(): lax.psum_scatter(against(piece, weight_cols, weight_dim), 'col', scatter_...]
    all_to_all x12 -> x0, blocking collectives: 831 us -> none  [the longest x7 435 us: to_columns(): return lax.all_to_all(value, 'col', split_axis=1, concat_axis=0, tiled=True)]
    dot_general x68 -> x6, matrix products: 887 us -> 60.7 us  [the longest x2 24.1 us: dot_nt(): lax.dot_general(a, b, (((1,), (1,)), ((), ())), preferred_element_type=jn...]
    all_gather x26 -> x2, waiting for transfers between devices: 853 us -> 70 us  [the longest x1 70 us: __init__(): full = lax.all_gather(pack, 'col', axis=0, tiled=False).transpose(1, 0, 2)]
    pallas_call x0 -> x13, Pallas kernels: none -> 356 us  [the longest x4 134 us: attention_backward(): pl.pallas_call(partial(bwd_kernel, parts, heads, start, len(deps)), grid=...]
    ppermute x0 -> x62, waiting for transfers between devices: none -> 218 us  [the longest x6 140 us: column_scatter(): lax.ppermute(pick(d).astype(jnp.bfloat16), 'col', place.quarter_perm(d))]
    convert_element_type x20 -> x13, other arithmetic: 208 us -> 34.2 us  [the longest x6 15.1 us: far_sums(): (own[d][part].astype(f32) + swapped[d][part].astype(f32)).astype(bf16)]
    sub x4 -> x0, matrix products: 117 us -> none  [local(): raised = jnp.exp(scores - highest)]
  transfers between devices with their start and end apart: 58 -> 68, of which waited for: 43 -> 19; matrix products, arithmetic and copies ran while one was open for 26% -> 29% of each run, Pallas kernels for 0% -> 20%
where the time goes in v1:
time: 1160 us
  Pallas kernels  356 us (31%)
  waiting for transfers between devices  319 us (28%)
  local copies, waits for them, and re-layouts  212 us (18%)
  other arithmetic  123 us (11%)
  starting transfers between devices  69 us (6%)
  matrix products  60.7 us (5%)
  between operations  16 us (1%)
    ppermute x6, waiting for transfers between devices, column_scatter(): lax.ppermute(pick(d).astype(jnp.bfloat16), 'col', place.quarter_perm(d))  140 us
    pallas_call x4, Pallas kernels, attention_backward(): pl.pallas_call(partial(bwd_kernel, parts, heads, start, len(deps)), grid=...  134 us
    pallas_call x1, Pallas kernels, feed_forward(): pl.pallas_call(partial(ffn_kernel, sizes, outs, chunk), grid_spec=pltpu.P...  127 us
    ppermute x20, waiting for transfers between devices, across(): lax.ppermute(value, 'row', [(r, r ^ shift) for r in range(lax.axis_size('...  73.1 us
    pallas_call x3, Pallas kernels, attention_forward(): pl.pallas_call(partial(fwd_kernel, parts, heads, start, len(deps)), grid=...  70.5 us
    all_gather x1, waiting for transfers between devices, __init__(): full = lax.all_gather(pack, 'col', axis=0, tiled=False).transpose(1, 0, 2)  70 us
    unnamed x258, local copies, waits for them, and re-layouts  68 us
    all_to_all x4, waiting for transfers between devices, swap_quarters(): lax.all_to_all(value, 'col', 0, 0, axis_index_groups=groups, tiled=True)  31.5 us
  transfers between devices with their start and end apart: 68, of which 19 were waited for; matrix products, arithmetic and copies ran while one was open for 29% of the time, Pallas kernels for 20%

profile of v1, /device:TPU:8, one launch (start us, length us, event | category | flops | bytes accessed | tf_op | source)
XLA Modules:
  0.0 1155.5 jit_solution(17582212962918032338)
XLA Ops:
  7.2 5.5 all-to-all-start
  20.4 70.0 %all-gather.5.cloned.1.call-done = bf16[2176,544]{1,0:T(8,128)(2,1)} async-done(((bf16[272,544]{1,0:T(8,128)(2,1)}), bf16[2176,544]{1,0:T(8,128)(2,1)}) %all-gather.5.cloned.1.call-update) | async-done | bytes 2367504 | tf_op jit(solution)/shard_map/all_gather | solution.py:775
  90.5 4.7 copy.98
  102.4 7.5 all-to-all-start.1
  117.9 5.4 copy.95
  127.3 18.5 %collective-permute-done.1.refs_1_ = bf16[272,2304]{1,0:T(8,128)(2,1)} collective-permute-done((bf16[272,2304]{1,0:T(8,128)(2,1)}, bf16[272,2304]{1,0:T(8,128)(2,1)}, u32[]{:S(2)}, u32[]{:S(2)}) %collective-permute-start.1) | collective-permute-done | bytes 1253408 | tf_op jit(solution)/shard_map/ppermute | solution.py:625
  149.9 4.2 collective-permute-done.2.refs_2_
  161.2 8.7 collective-permute-done.4.refs_4_
  176.6 31.5 %all-to-all-done.1 = bf16[4,320,1088]{2,1,0:T(8,128)(2,1)S(1)} async-done(((bf16[4,320,1088]{2,1,0:T(8,128)(2,1)}), bf16[4,320,1088]{2,1,0:T(8,128)(2,1)S(1)}, u32[]{:S(2)}, u32[]{:S(2)}) %all-to-all-start.1) | async-done | bytes 2785312 | tf_op jit(solution)/shard_map/all_to_all | solution.py:544
  213.2 12.7 %assemble_weights.1 = (bf16[1088,3456]{1,0:T(8,128)(2,1)}, bf16[1152,1152]{1,0:T(8,128)(2,1)}) custom-call(s32[6]{0:T(128)S(1)} %stack.53.scalars, bf16[272,2304]{1,0:T(8,128)(2,1)S(1)} %copy-done.11, bf16[272,2304]{1,0:T(8,128)(2,1)} %collective-permute-done.1.refs_1_, bf16[272,2304]{1,0:T(8,128)(2,1)} %collective-permute-done.2.refs_2_, ...), custom_call_target="tpu_custom_call" | custom-call | bytes 20054016 | tf_op jit(solution)/shard_map/assemble_weights/pallas_call | solution.py:739
  225.9 5.4 copy.96.refs_1_
  238.8 13.4 %fusion.1.q_ref.k_ref.v_ref = bf16[1280,3456]{1,0:T(8,128)(2,1)S(1)} fusion(bf16[1088,3456]{1,0:T(8,128)(2,1)S(1)} %copy-done.98, f32[3456]{0:T(1024)S(1)} %copy-done.88, f32[3456]{0:T(1024)S(1)} %copy-done.108, bf16[1280,1088]{1,0:T(8,128)(2,1)S(1)} %spread_rows.2, f32[1088]{0:T(1024)S(1)} %copy-done.106, f32[1088]{0:T(1024)S(1)} %copy-done.78, ...), kind=kOutput, calls=%fused_computation.5 | convolution fusion | flops 9647554560 | bytes 19199488 | tf_op jit(solution)/shard_map/dot_general | solution.py:21
  265.7 5.4 copy.114.refs_1_
  277.7 5.4 copy.115
  304.0 24.7 %attention_forward.3 = (bf16[1280,384]{1,0:T(8,128)(2,1)S(1)}, f32[1280,384]{1,0:T(8,128)S(1)}) custom-call(bf16[1280,3456]{1,0:T(8,128)(2,1)} %copy-done.53, bf16[1280,3456]{1,0:T(8,128)(2,1)} %copy-done.53, bf16[1280,3456]{1,0:T(8,128)(2,1)} %copy-done.53, bf16[512,2304]{1,0:T(8,128)(2,1)} %collective-permute-done.10.ko_ref.vo_ref, ...), custom_call_target="tpu_custom_call" | custom-call | flops 26112000000 | bytes 23040000 | tf_op jit(solution)/shard_map/attention_forward/pallas_call | solution.py:111
  331.0 20.9 %attention_forward.5 = (bf16[1280,384]{1,0:T(8,128)(2,1)S(1)}, f32[1280,384]{1,0:T(8,128)S(1)}) custom-call(bf16[1280,3456]{1,0:T(8,128)(2,1)} %copy-done.53, bf16[1280,3456]{1,0:T(8,128)(2,1)} %copy-done.53, bf16[1280,3456]{1,0:T(8,128)(2,1)} %copy-done.53, bf16[512,2304]{1,0:T(8,128)(2,1)} %collective-permute-done.10.ko_ref.vo_ref, ...), custom_call_target="tpu_custom_call" | custom-call | flops 26112000000 | bytes 23040000 | tf_op jit(solution)/shard_map/attention_forward/pallas_call | solution.py:111
  353.3 24.9 %attention_forward.4 = (bf16[1280,384]{1,0:T(8,128)(2,1)S(1)}, f32[1280,384]{1,0:T(8,128)S(1)}) custom-call(bf16[1280,3456]{1,0:T(8,128)(2,1)} %copy-done.53, bf16[1280,3456]{1,0:T(8,128)(2,1)} %copy-done.53, bf16[1280,3456]{1,0:T(8,128)(2,1)} %copy-done.53, bf16[512,2304]{1,0:T(8,128)(2,1)} %collective-permute-done.10.ko_ref.vo_ref, ...), custom_call_target="tpu_custom_call" | custom-call | flops 26112000000 | bytes 23040000 | tf_op jit(solution)/shard_map/attention_forward/pallas_call | solution.py:111
  381.4 6.3 fusion.63
  394.8 5.6 copy.116.refs_11_
  403.0 15.3 %collective-permute-done.14.refs_4_ = bf16[128,4352]{1,0:T(8,128)(2,1)} collective-permute-done((bf16[128,4352]{1,0:T(8,128)(2,1)}, bf16[128,4352]{1,0:T(8,128)(2,1)}, u32[]{:S(2)}, u32[]{:S(2)}) %collective-permute-start.14) | collective-permute-done | bytes 1114144 | tf_op jit(solution)/shard_map/ppermute | solution.py:625
  425.5 126.7 %feed_forward.1 = (f32[1280,1088]{1,0:T(8,128)}, f32[1280,1088]{1,0:T(8,128)}, f32[1,4352]{1,0:T(1,128)}, bf16[272,4352]{1,0:T(8,128)(2,1)}, bf16[272,4352]{1,0:...) custom-call(s32[6]{0:T(128)} %copy-done.20, ...), custom_call_target="tpu_custom_call" | custom-call | flops 145458462720 | bytes 65732608 | tf_op jit(solution)/shard_map/feed_forward/pallas_call | solution.py:405
  553.8 6.7 multiply_reduce_fusion
  561.6 4.8 fusion.55
  570.2 5.8 convolution_convert_fusion.1.do_ref
  576.0 5.6 fusion.65
  587.1 45.5 %attention_backward.6 = (bf16[1280,384]{1,0:T(8,128)(2,1)}, f32[1280,384]{1,0:T(8,128)}, f32[1280,384]{1,0:T(8,128)}, bf16[512,384]{1,0:T(8,128)(2,1)}, bf16[512,384]{1,0:T(8,128)(2,1)}) custom-call(bf16[1280,3456]{1,0:T(8,128)(2,1)} %copy-done.53, bf16[1280,3456]{1,0:T(8,128)(2,1)} %copy-done.53, bf16[1280,3456]{1,0:T(8,128)(2,1)} %copy-done.53, ...), custom_call_target="tpu_custom_call" | custom-call | flops 46848000000 | bytes 46080000 | tf_op jit(solution)/shard_map/attention_backward/pallas_call | solution.py:256
  646.0 31.5 %attention_backward.4 = (bf16[1280,256]{1,0:T(8,128)(2,1)}, f32[1280,256]{1,0:T(8,128)}, f32[1280,256]{1,0:T(8,128)}, bf16[512,256]{1,0:T(8,128)(2,1)}, bf16[512,256]{1,0:T(8,128)(2,1)}) custom-call(bf16[1280,3456]{1,0:T(8,128)(2,1)} %copy-done.53, bf16[1280,3456]{1,0:T(8,128)(2,1)} %copy-done.53, bf16[1280,3456]{1,0:T(8,128)(2,1)} %copy-done.53, ...), custom_call_target="tpu_custom_call" | custom-call | flops 31232000000 | bytes 46080000 | tf_op jit(solution)/shard_map/attention_backward/pallas_call | solution.py:256
  685.3 5.4 copy.118.refs_1_
  695.1 8.5 all-to-all-start.2
  709.9 31.7 %attention_backward.5 = (bf16[1280,256]{1,0:T(8,128)(2,1)}, f32[1280,256]{1,0:T(8,128)}, f32[1280,256]{1,0:T(8,128)}, bf16[512,256]{1,0:T(8,128)(2,1)}, bf16[512,256]{1,0:T(8,128)(2,1)}) custom-call(bf16[1280,3456]{1,0:T(8,128)(2,1)} %copy-done.53, bf16[1280,3456]{1,0:T(8,128)(2,1)} %copy-done.53, bf16[1280,3456]{1,0:T(8,128)(2,1)} %copy-done.53, ...), custom_call_target="tpu_custom_call" | custom-call | flops 31232000000 | bytes 46080000 | tf_op jit(solution)/shard_map/attention_backward/pallas_call | solution.py:256
  751.1 24.9 %attention_backward.7 = (bf16[1280,256]{1,0:T(8,128)(2,1)}, f32[1280,256]{1,0:T(8,128)}, f32[1280,256]{1,0:T(8,128)}, bf16[512,256]{1,0:T(8,128)(2,1)}, bf16[512,256]{1,0:T(8,128)(2,1)}) custom-call(bf16[1280,3456]{1,0:T(8,128)(2,1)} %copy-done.53, bf16[1280,3456]{1,0:T(8,128)(2,1)} %copy-done.53, bf16[1280,3456]{1,0:T(8,128)(2,1)} %copy-done.53, ...), custom_call_target="tpu_custom_call" | custom-call | flops 31232000000 | bytes 46080000 | tf_op jit(solution)/shard_map/attention_backward/pallas_call | solution.py:256
  791.6 5.1 fusion.19
  796.6 9.4 constant_dynamic-update-slice_fusion.22
  806.1 18.3 %fusion.64 = (f32[1088]{0:T(1024)}, f32[1280,1088]{0,1:T(8,128)}) fusion(bf16[1280,3456]{1,0:T(8,128)(2,1)} %get-tuple-element.161, bf16[1088,3456]{1,0:T(8,128)(2,1)} %get-tuple-element.66), kind=kOutput, calls=%fused_computation.219 | convolution fusion | flops 9627319296 | bytes 21942528 | tf_op jit(solution)/shard_map/dot_general | solution.py:25
  824.5 11.3 convolution_convert_fusion
  843.5 7.6 copy.119
  864.7 8.5 convert_reduce_fusion.1
  902.2 13.9 %collective-permute-done.42 = bf16[144,2304]{1,0:T(8,128)(2,1)S(1)} collective-permute-done((bf16[144,2304]{1,0:T(8,128)(2,1)S(1)}, bf16[144,2304]{1,0:T(8,128)(2,1)S(1)}, u32[]{:S(2)}, u32[]{:S(2)}) %collective-permute-start.42) | collective-permute-done | bytes 663584 | tf_op jit(solution)/shard_map/ppermute | solution.py:625
  920.0 10.8 collective-permute-done.47
  947.3 5.4 copy.121.refs_1_
  957.1 5.9 all-to-all-start.3
  972.7 53.1 %collective-permute-done.59 = bf16[272,1088]{1,0:T(8,128)(2,1)S(1)} collective-permute-done((bf16[272,1088]{1,0:T(8,128)(2,1)S(1)}, bf16[272,1088]{1,0:T(8,128)(2,1)S(1)}, u32[]{:S(2)}, u32[]{:S(2)}) %collective-permute-start.59) | collective-permute-done | bytes 591904 | tf_op jit(solution)/shard_map/ppermute | solution.py:677
  1025.7 42.1 %collective-permute-done.60 = bf16[272,1088]{1,0:T(8,128)(2,1)S(1)} collective-permute-done((bf16[272,1088]{1,0:T(8,128)(2,1)S(1)}, bf16[272,1088]{1,0:T(8,128)(2,1)S(1)}, u32[]{:S(2)}, u32[]{:S(2)}) %collective-permute-start.60) | collective-permute-done | bytes 591904 | tf_op jit(solution)/shard_map/ppermute | solution.py:677
  1067.8 12.1 %collective-permute-done.61 = bf16[272,1088]{1,0:T(8,128)(2,1)S(1)} collective-permute-done((bf16[272,1088]{1,0:T(8,128)(2,1)S(1)}, bf16[272,1088]{1,0:T(8,128)(2,1)S(1)}, u32[]{:S(2)}, u32[]{:S(2)}) %collective-permute-start.61) | collective-permute-done | bytes 591904 | tf_op jit(solution)/shard_map/ppermute | solution.py:677
  1090.5 6.1 copy.123
  1106.2 9.7 collective-permute-done.50
  1116.0 14.5 %collective-permute-done.51 = bf16[272,544]{0,1:T(8,128)(2,1)S(1)} collective-permute-done((bf16[272,544]{0,1:T(8,128)(2,1)S(1)}, bf16[272,544]{0,1:T(8,128)(2,1)S(1)}, u32[]{:S(2)}, u32[]{:S(2)}) %collective-permute-start.51) | collective-permute-done | bytes 295968 | tf_op jit(solution)/shard_map/ppermute | solution.py:677
  1130.4 8.7 collective-permute-done.52
  (528 shorter events, 304.0 us)
Async XLA Ops:
  7.2 93.5 %all-to-all-start = ((bf16[4,320,1088]{2,1,0:T(8,128)(2,1)}), bf16[4,320,1088]{2,1,0:T(8,128)(2,1)S(1)}, u32[]{:S(2)}, u32[]{:S(2)}) async-start(bf16[4,320,1088]{2,1,0:T(8,128)(2,1)} %param.35), calls=%async_computation | async-start | bytes 5898240 | tf_op jit(solution)/shard_map/all_to_all | solution.py:544
  12.7 77.8 %all-gather.5.cloned.1.call-start = ((), (), s32[]{:S(2)}) async-start(), calls=%async_computation.4 | async-start | bytes 3133440 | tf_op jit(solution)/shard_map/all_gather | solution.py:775
  14.6 268.4 %all-gather.7.cloned.1.call-start = ((), (), s32[]{:S(2)}) async-start(), calls=%async_computation.5 | async-start | bytes 5640192 | tf_op jit(solution)/shard_map/all_gather | solution.py:787
  102.4 105.8 %all-to-all-start.1 = ((bf16[4,320,1088]{2,1,0:T(8,128)(2,1)}), bf16[4,320,1088]{2,1,0:T(8,128)(2,1)S(1)}, u32[]{:S(2)}, u32[]{:S(2)}) async-start(bf16[4,320,1088]{2,1,0:T(8,128)(2,1)} %param.50), calls=%async_computation.1 | async-start | bytes 5898240 | tf_op jit(solution)/shard_map/all_to_all | solution.py:544
  116.4 29.4 %collective-permute-start.1 = (bf16[272,2304]{1,0:T(8,128)(2,1)}, bf16[272,2304]{1,0:T(8,128)(2,1)}, u32[]{:S(2)}, u32[]{:S(2)}) collective-permute-start(bf16[272,2304]{1,0:T(8,128)(2,1)} %copy.127.refs_0_), channel_id=1, source_target_pairs={{0,8},{8,0},{16,24},{24,16},{1,9},{9,1},{17,25},{25,17},{2,10},{10... | collective-permute-start | bytes 3760136 | tf_op jit(solution)/shard_map/ppermute | solution.py:625
  123.3 102.6 %collective-permute-start = (bf16[1280,1088]{0,1:T(8,128)(2,1)}, bf16[1280,1088]{0,1:T(8,128)(2,1)}, u32[]{:S(2)}, u32[]{:S(2)}) collective-permute-start(bf16[1280,1088]{0,1:T(8,128)(2,1)} %copy.95), channel_id=1, source_target_pairs={{0,1},{1,0},{2,3},{3,2},{4,5},{5,4},{6,7},{7,6},{8,9},{9,8},{10,11... | collective-permute-start | bytes 8355848 | tf_op jit(solution)/shard_map/ppermute | solution.py:548
  123.4 30.7 %collective-permute-start.2 = (bf16[272,2304]{1,0:T(8,128)(2,1)}, bf16[272,2304]{1,0:T(8,128)(2,1)}, u32[]{:S(2)}, u32[]{:S(2)}) collective-permute-start(bf16[272,2304]{1,0:T(8,128)(2,1)} %copy.127.refs_0_), channel_id=1, source_target_pairs={{0,16},{8,24},{16,0},{24,8},{1,17},{9,25},{17,1},{25,9},{2,18},{10... | collective-permute-start | bytes 3760136 | tf_op jit(solution)/shard_map/ppermute | solution.py:625
  124.9 30.9 %collective-permute-start.5 = (bf16[272,2304]{1,0:T(8,128)(2,1)}, bf16[272,2304]{1,0:T(8,128)(2,1)}, u32[]{:S(2)}, u32[]{:S(2)}) collective-permute-start(bf16[272,2304]{1,0:T(8,128)(2,1)} %copy.127.refs_0_), channel_id=1, source_target_pairs={{0,1},{1,0},{2,3},{3,2},{4,5},{5,4},{6,7},{7,6},{8,9},{9,8},{10,11... | collective-permute-start | bytes 3760136 | tf_op jit(solution)/shard_map/ppermute | solution.py:641
  155.9 56.0 %collective-permute-start.6 = (bf16[272,2304]{1,0:T(8,128)(2,1)}, bf16[272,2304]{1,0:T(8,128)(2,1)}, u32[]{:S(2)}, u32[]{:S(2)}) collective-permute-start(bf16[272,2304]{1,0:T(8,128)(2,1)} %collective-permute-done.1.refs_1_), channel_id=1, source_target_pairs={{0,1},{1,0},{2,3},{3,2},{4,5},{5,4},{6,7},{7,6},{8,9},{9,8},{10,11... | collective-permute-start | bytes 3760136 | tf_op jit(solution)/shard_map/ppermute | solution.py:641
  155.9 56.0 %collective-permute-start.7 = (bf16[272,2304]{1,0:T(8,128)(2,1)}, bf16[272,2304]{1,0:T(8,128)(2,1)}, u32[]{:S(2)}, u32[]{:S(2)}) collective-permute-start(bf16[272,2304]{1,0:T(8,128)(2,1)} %collective-permute-done.2.refs_2_), channel_id=1, source_target_pairs={{0,1},{1,0},{2,3},{3,2},{4,5},{5,4},{6,7},{7,6},{8,9},{9,8},{10,11... | collective-permute-start | bytes 3760136 | tf_op jit(solution)/shard_map/ppermute | solution.py:641
  169.9 41.9 %collective-permute-start.9 = (bf16[128,2304]{1,0:T(8,128)(2,1)S(1)}, bf16[128,2304]{1,0:T(8,128)(2,1)}, u32[]{:S(2)}, u32[]{:S(2)}) collective-permute-start(bf16[128,2304]{1,0:T(8,128)(2,1)S(1)} %collective-permute-done.4.refs_4_), channel_id=1, source_target_pairs={{0,1},{1,0},{2,3},{3,2},{4,5},{5,4},{6,7},{7,6},{8,9},{9,8},{10,11... | collective-permute-start | bytes 1769480 | tf_op jit(solution)/shard_map/ppermute | solution.py:641
  169.9 42.0 %collective-permute-start.8 = (bf16[144,2304]{1,0:T(8,128)(2,1)}, bf16[144,2304]{1,0:T(8,128)(2,1)}, u32[]{:S(2)}, u32[]{:S(2)}) collective-permute-start(bf16[144,2304]{1,0:T(8,128)(2,1)} %collective-permute-done.3.refs_3_), channel_id=1, source_target_pairs={{0,1},{1,0},{2,3},{3,2},{4,5},{5,4},{6,7},{7,6},{8,9},{9,8},{10,11... | collective-permute-start | bytes 1990664 | tf_op jit(solution)/shard_map/ppermute | solution.py:641
  211.8 53.9 %collective-permute-start.20 = (bf16[1280,1088]{0,1:T(8,128)(2,1)}, bf16[1280,1088]{0,1:T(8,128)(2,1)}, u32[]{:S(2)}, u32[]{:S(2)}) collective-permute-start(bf16[1280,1088]{0,1:T(8,128)(2,1)} %copy.113), channel_id=1, source_target_pairs={{0,1},{1,0},{2,3},{3,2},{4,5},{5,4},{6,7},{7,6},{8,9},{9,8},{10,11... | collective-permute-start | bytes 8355848 | tf_op jit(solution)/shard_map/ppermute | solution.py:548
  253.8 50.1 %collective-permute-start.10 = (bf16[512,2304]{1,0:T(8,128)(2,1)}, bf16[512,2304]{1,0:T(8,128)(2,1)}, u32[]{:S(2)}, u32[]{:S(2)}) collective-permute-start(bf16[512,2304]{1,0:T(8,128)(2,1)} %slice.353), channel_id=1, source_target_pairs={{0,1},{1,0},{2,3},{3,2},{4,5},{5,4},{6,7},{7,6},{8,9},{9,8},{10,11... | collective-permute-start | bytes 7077896 | tf_op jit(solution)/shard_map/ppermute | solution.py:928
  300.8 87.8 %collective-permute-start.11 = (bf16[272,4352]{1,0:T(8,128)(2,1)}, bf16[272,4352]{1,0:T(8,128)(2,1)S(1)}, u32[]{:S(2)}, u32[]{:S(2)}) collective-permute-start(bf16[272,4352]{1,0:T(8,128)(2,1)} %maximum_select_fusion.refs_0_), channel_id=1, source_target_pairs={{0,8},{8,0},{16,24},{24,16},{1,9},{9,1},{17,25},{25,17},{2,10},{10... | collective-permute-start | bytes 7102472 | tf_op jit(solution)/shard_map/ppermute | solution.py:625
  302.5 87.7 %collective-permute-start.12 = (bf16[272,4352]{1,0:T(8,128)(2,1)}, bf16[272,4352]{1,0:T(8,128)(2,1)S(1)}, u32[]{:S(2)}, u32[]{:S(2)}) collective-permute-start(bf16[272,4352]{1,0:T(8,128)(2,1)} %maximum_select_fusion.refs_0_), channel_id=1, source_target_pairs={{0,16},{8,24},{16,0},{24,8},{1,17},{9,25},{17,1},{25,9},{2,18},{10... | collective-permute-start | bytes 7102472 | tf_op jit(solution)/shard_map/ppermute | solution.py:625
  303.9 118.4 %collective-permute-start.15 = (bf16[272,4352]{1,0:T(8,128)(2,1)}, bf16[272,4352]{1,0:T(8,128)(2,1)}, u32[]{:S(2)}, u32[]{:S(2)}) collective-permute-start(bf16[272,4352]{1,0:T(8,128)(2,1)} %maximum_select_fusion.refs_0_), channel_id=1, source_target_pairs={{0,1},{1,0},{2,3},{3,2},{4,5},{5,4},{6,7},{7,6},{8,9},{9,8},{10,11... | collective-permute-start | bytes 7102472 | tf_op jit(solution)/shard_map/ppermute | solution.py:641
  389.6 30.3 %collective-permute-start.13 = (bf16[144,4352]{1,0:T(8,128)(2,1)}, bf16[144,4352]{1,0:T(8,128)(2,1)}, u32[]{:S(2)}, u32[]{:S(2)}) collective-permute-start(bf16[144,4352]{1,0:T(8,128)(2,1)} %slice.360), channel_id=1, source_target_pairs={{0,16},{8,24},{16,0},{24,8},{1,17},{9,25},{17,1},{25,9},{2,18},{10... | collective-permute-start | bytes 3760136 | tf_op jit(solution)/shard_map/ppermute | solution.py:625
  391.8 26.5 %collective-permute-start.14 = (bf16[128,4352]{1,0:T(8,128)(2,1)}, bf16[128,4352]{1,0:T(8,128)(2,1)}, u32[]{:S(2)}, u32[]{:S(2)}) collective-permute-start(bf16[128,4352]{1,0:T(8,128)(2,1)} %slice.361), channel_id=1, source_target_pairs={{0,8},{8,0},{16,24},{24,16},{1,9},{9,1},{17,25},{25,17},{2,10},{10... | collective-permute-start | bytes 3342344 | tf_op jit(solution)/shard_map/ppermute | solution.py:625
  581.6 51.0 %collective-permute-start.22 = (bf16[272,4352]{1,0:T(8,128)(2,1)}, bf16[272,4352]{1,0:T(8,128)(2,1)}, u32[]{:S(2)}, u32[]{:S(2)}) collective-permute-start(bf16[272,4352]{1,0:T(8,128)(2,1)} %get-tuple-element.77), channel_id=1, source_target_pairs={{0,1},{1,0},{2,3},{3,2},{4,5},{5,4},{6,7},{7,6},{8,9},{9,8},{10,11... | collective-permute-start | bytes 7102472 | tf_op jit(solution)/shard_map/ppermute | solution.py:641
  582.1 56.4 %collective-permute-start.24 = (bf16[272,4352]{1,0:T(8,128)(2,1)}, bf16[272,4352]{1,0:T(8,128)(2,1)}, u32[]{:S(2)}, u32[]{:S(2)}) collective-permute-start(bf16[272,4352]{1,0:T(8,128)(2,1)} %get-tuple-element.81), channel_id=1, source_target_pairs={{0,1},{1,0},{2,3},{3,2},{4,5},{5,4},{6,7},{7,6},{8,9},{9,8},{10,11... | collective-permute-start | bytes 7102472 | tf_op jit(solution)/shard_map/ppermute | solution.py:641
  582.1 59.4 %collective-permute-start.23 = (bf16[272,4352]{1,0:T(8,128)(2,1)}, bf16[272,4352]{1,0:T(8,128)(2,1)}, u32[]{:S(2)}, u32[]{:S(2)}) collective-permute-start(bf16[272,4352]{1,0:T(8,128)(2,1)} %get-tuple-element.79), channel_id=1, source_target_pairs={{0,1},{1,0},{2,3},{3,2},{4,5},{5,4},{6,7},{7,6},{8,9},{9,8},{10,11... | collective-permute-start | bytes 7102472 | tf_op jit(solution)/shard_map/ppermute | solution.py:641
  582.6 164.5 %collective-permute-start.27 = (bf16[272,4352]{1,0:T(8,128)(2,1)}, bf16[272,4352]{1,0:T(8,128)(2,1)}, u32[]{:S(2)}, u32[]{:S(2)}) collective-permute-start(bf16[272,4352]{1,0:T(8,128)(2,1)} %get-tuple-element.86), channel_id=1, source_target_pairs={{0,1},{1,0},{2,3},{3,2},{4,5},{5,4},{6,7},{7,6},{8,9},{9,8},{10,11... | collective-permute-start | bytes 7102472 | tf_op jit(solution)/shard_map/ppermute | solution.py:641
  585.9 98.0 %collective-permute-start.21 = (bf16[1280,1088]{0,1:T(8,128)(2,1)}, bf16[1280,1088]{0,1:T(8,128)(2,1)}, u32[]{:S(2)}, u32[]{:S(2)}) collective-permute-start(bf16[1280,1088]{0,1:T(8,128)(2,1)} %copy.117), channel_id=1, source_target_pairs={{0,1},{1,0},{2,3},{3,2},{4,5},{5,4},{6,7},{7,6},{8,9},{9,8},{10,11... | collective-permute-start | bytes 8355848 | tf_op jit(solution)/shard_map/ppermute | solution.py:562
  635.3 68.3 %collective-permute-start.26 = (bf16[128,4352]{1,0:T(8,128)(2,1)}, bf16[128,4352]{1,0:T(8,128)(2,1)}, u32[]{:S(2)}, u32[]{:S(2)}) collective-permute-start(bf16[128,4352]{1,0:T(8,128)(2,1)} %add_convert_fusion.10.refs_1_), channel_id=1, source_target_pairs={{0,8},{8,0},{16,24},{24,16},{1,9},{9,1},{17,25},{25,17},{2,10},{10... | collective-permute-start | bytes 3342344 | tf_op jit(solution)/shard_map/ppermute | solution.py:625
  638.5 68.2 %collective-permute-start.25 = (bf16[144,4352]{1,0:T(8,128)(2,1)}, bf16[144,4352]{1,0:T(8,128)(2,1)}, u32[]{:S(2)}, u32[]{:S(2)}) collective-permute-start(bf16[144,4352]{1,0:T(8,128)(2,1)} %add_convert_fusion.7.refs_0_), channel_id=1, source_target_pairs={{0,16},{8,24},{16,0},{24,8},{1,17},{9,25},{17,1},{25,9},{2,18},{10... | collective-permute-start | bytes 3760136 | tf_op jit(solution)/shard_map/ppermute | solution.py:625
  641.5 105.5 %collective-permute-start.30 = (bf16[144,4352]{1,0:T(8,128)(2,1)}, bf16[144,4352]{1,0:T(8,128)(2,1)}, u32[]{:S(2)}, u32[]{:S(2)}) collective-permute-start(bf16[144,4352]{1,0:T(8,128)(2,1)} %add_convert_fusion.6.refs_3_), channel_id=1, source_target_pairs={{0,16},{8,24},{16,0},{24,8},{1,17},{9,25},{17,1},{25,9},{2,18},{10... | collective-permute-start | bytes 3760136 | tf_op jit(solution)/shard_map/ppermute | solution.py:625
  683.9 63.2 %collective-permute-start.29 = (bf16[128,4352]{1,0:T(8,128)(2,1)}, bf16[128,4352]{1,0:T(8,128)(2,1)}, u32[]{:S(2)}, u32[]{:S(2)}) collective-permute-start(bf16[128,4352]{1,0:T(8,128)(2,1)} %add_convert_fusion.9.refs_2_), channel_id=1, source_target_pairs={{0,8},{8,0},{16,24},{24,16},{1,9},{9,1},{17,25},{25,17},{2,10},{10... | collective-permute-start | bytes 3342344 | tf_op jit(solution)/shard_map/ppermute | solution.py:625
  695.1 188.9 %all-to-all-start.2 = ((bf16[4,320,1088]{2,1,0:T(8,128)(2,1)}), bf16[4,320,1088]{2,1,0:T(8,128)(2,1)}, u32[]{:S(2)}, u32[]{:S(2)}) async-start(bf16[4,320,1088]{2,1,0:T(8,128)(2,1)} %bitcast.91), calls=%async_computation.2 | async-start | bytes 5898240 | tf_op jit(solution)/shard_map/all_to_all | solution.py:544
  706.1 41.0 %collective-permute-start.31 = (bf16[128,4352]{1,0:T(8,128)(2,1)S(1)}, bf16[128,4352]{1,0:T(8,128)(2,1)S(1)}, u32[]{:S(2)}, u32[]{:S(2)}) collective-permute-start(bf16[128,4352]{1,0:T(8,128)(2,1)S(1)} %add_convert_fusion.8.refs_2_), channel_id=1, source_target_pairs={{0,16},{8,24},{16,0},{24,8},{1,17},{9,25},{17,1},{25,9},{2,18},{10... | collective-permute-start | bytes 3342344 | tf_op jit(solution)/shard_map/ppermute | solution.py:625
  708.9 38.2 %collective-permute-start.28 = (bf16[144,4352]{1,0:T(8,128)(2,1)S(1)}, bf16[144,4352]{1,0:T(8,128)(2,1)S(1)}, u32[]{:S(2)}, u32[]{:S(2)}) collective-permute-start(bf16[144,4352]{1,0:T(8,128)(2,1)S(1)} %add_convert_fusion.5.refs_1_), channel_id=1, source_target_pairs={{0,8},{8,0},{16,24},{24,16},{1,9},{9,1},{17,25},{25,17},{2,10},{10... | collective-permute-start | bytes 3760136 | tf_op jit(solution)/shard_map/ppermute | solution.py:625
  780.5 109.2 %collective-permute-start.58 = (bf16[272,4352]{1,0:T(8,128)(2,1)}, bf16[272,4352]{1,0:T(8,128)(2,1)}, u32[]{:S(2)}, u32[]{:S(2)}) collective-permute-start(bf16[272,4352]{1,0:T(8,128)(2,1)} %add_convert_fusion.3.refs_0_), channel_id=1, source_target_pairs={{0,1},{1,0},{2,3},{3,2},{4,5},{5,4},{6,7},{7,6},{8,9},{9,8},{10,11... | collective-permute-start | bytes 7102472 | tf_op jit(solution)/shard_map/ppermute | solution.py:641
  851.1 43.5 %collective-permute-start.41 = (bf16[272,2304]{1,0:T(8,128)(2,1)}, bf16[272,2304]{1,0:T(8,128)(2,1)}, u32[]{:S(2)}, u32[]{:S(2)}) collective-permute-start(bf16[272,2304]{1,0:T(8,128)(2,1)} %get-tuple-element.173), channel_id=1, source_target_pairs={{0,1},{1,0},{2,3},{3,2},{4,5},{5,4},{6,7},{7,6},{8,9},{9,8},{10,11... | collective-permute-start | bytes 3760136 | tf_op jit(solution)/shard_map/ppermute | solution.py:641
  851.3 45.0 %collective-permute-start.45 = (bf16[272,2304]{1,0:T(8,128)(2,1)}, bf16[272,2304]{1,0:T(8,128)(2,1)}, u32[]{:S(2)}, u32[]{:S(2)}) collective-permute-start(bf16[272,2304]{1,0:T(8,128)(2,1)} %get-tuple-element.172), channel_id=1, source_target_pairs={{0,1},{1,0},{2,3},{3,2},{4,5},{5,4},{6,7},{7,6},{8,9},{9,8},{10,11... | collective-permute-start | bytes 3760136 | tf_op jit(solution)/shard_map/ppermute | solution.py:641
  892.2 70.9 %collective-permute-start.39 = (bf16[272,2304]{1,0:T(8,128)(2,1)}, bf16[272,2304]{1,0:T(8,128)(2,1)}, u32[]{:S(2)}, u32[]{:S(2)}) collective-permute-start(bf16[272,2304]{1,0:T(8,128)(2,1)} %get-tuple-element.175), channel_id=1, source_target_pairs={{0,1},{1,0},{2,3},{3,2},{4,5},{5,4},{6,7},{7,6},{8,9},{9,8},{10,11... | collective-permute-start | bytes 3760136 | tf_op jit(solution)/shard_map/ppermute | solution.py:641
  894.6 41.1 %collective-permute-start.33 = (bf16[1280,1088]{0,1:T(8,128)(2,1)S(1)}, bf16[1280,1088]{0,1:T(8,128)(2,1)S(1)}, u32[]{:S(2)}, u32[]{:S(2)}) collective-permute-start(bf16[1280,1088]{0,1:T(8,128)(2,1)S(1)} %copy.120), channel_id=1, source_target_pairs={{0,1},{1,0},{2,3},{3,2},{4,5},{5,4},{6,7},{7,6},{8,9},{9,8},{10,11... | collective-permute-start | bytes 8355848 | tf_op jit(solution)/shard_map/ppermute | solution.py:562
  901.0 33.9 %collective-permute-start.56 = (f32[72,128]{1,0:T(8,128)S(1)}, f32[72,128]{1,0:T(8,128)S(1)}, u32[]{:S(2)}, u32[]{:S(2)}) collective-permute-start(f32[72,128]{1,0:T(8,128)S(1)} %add.493), channel_id=1, source_target_pairs={{0,8},{8,0},{16,24},{24,16},{1,9},{9,1},{17,25},{25,17},{2,10},{10... | collective-permute-start | bytes 110600 | tf_op jit(solution)/shard_map/ppermute | solution.py:691
  919.5 43.7 %collective-permute-start.46 = (bf16[144,2304]{1,0:T(8,128)(2,1)}, bf16[144,2304]{1,0:T(8,128)(2,1)}, u32[]{:S(2)}, u32[]{:S(2)}) collective-permute-start(bf16[144,2304]{1,0:T(8,128)(2,1)} %get-tuple-element.168), channel_id=1, source_target_pairs={{0,16},{8,24},{16,0},{24,8},{1,17},{9,25},{17,1},{25,9},{2,18},{10... | collective-permute-start | bytes 1990664 | tf_op jit(solution)/shard_map/ppermute | solution.py:625
  930.8 37.4 %collective-permute-start.43 = (bf16[144,2304]{1,0:T(8,128)(2,1)}, bf16[144,2304]{1,0:T(8,128)(2,1)}, u32[]{:S(2)}, u32[]{:S(2)}) collective-permute-start(bf16[144,2304]{1,0:T(8,128)(2,1)} %add_convert_fusion.12), channel_id=1, source_target_pairs={{0,8},{8,0},{16,24},{24,16},{1,9},{9,1},{17,25},{25,17},{2,10},{10... | collective-permute-start | bytes 1990664 | tf_op jit(solution)/shard_map/ppermute | solution.py:625
  934.8 31.2 %collective-permute-start.44 = (bf16[128,2304]{1,0:T(8,128)(2,1)}, bf16[128,2304]{1,0:T(8,128)(2,1)}, u32[]{:S(2)}, u32[]{:S(2)}) collective-permute-start(bf16[128,2304]{1,0:T(8,128)(2,1)} %get-tuple-element.171), channel_id=1, source_target_pairs={{0,8},{8,0},{16,24},{24,16},{1,9},{9,1},{17,25},{25,17},{2,10},{10... | collective-permute-start | bytes 1769480 | tf_op jit(solution)/shard_map/ppermute | solution.py:625
  937.3 29.3 %collective-permute-start.48 = (bf16[128,2304]{1,0:T(8,128)(2,1)}, bf16[128,2304]{1,0:T(8,128)(2,1)}, u32[]{:S(2)}, u32[]{:S(2)}) collective-permute-start(bf16[128,2304]{1,0:T(8,128)(2,1)} %get-tuple-element.170), channel_id=1, source_target_pairs={{0,16},{8,24},{16,0},{24,8},{1,17},{9,25},{17,1},{25,9},{2,18},{10... | collective-permute-start | bytes 1769480 | tf_op jit(solution)/shard_map/ppermute | solution.py:625
  957.1 184.0 %all-to-all-start.3 = ((bf16[4,320,1088]{2,1,0:T(8,128)(2,1)}), bf16[4,320,1088]{2,1,0:T(8,128)(2,1)}, u32[]{:S(2)}, u32[]{:S(2)}) async-start(bf16[4,320,1088]{2,1,0:T(8,128)(2,1)} %bitcast.93), calls=%async_computation.3 | async-start | bytes 5898240 | tf_op jit(solution)/shard_map/all_to_all | solution.py:544
  963.1 62.7 %collective-permute-start.59 = (bf16[272,1088]{1,0:T(8,128)(2,1)S(1)}, bf16[272,1088]{1,0:T(8,128)(2,1)S(1)}, u32[]{:S(2)}, u32[]{:S(2)}) collective-permute-start(bf16[272,1088]{1,0:T(8,128)(2,1)S(1)} %copy-done.54), channel_id=1, source_target_pairs={{0,2},{1,3},{2,0},{3,1},{4,6},{5,7},{6,4},{7,5},{8,10},{9,11},{10,... | collective-permute-start | bytes 1775624 | tf_op jit(solution)/shard_map/ppermute | solution.py:677
  963.2 104.7 %collective-permute-start.60 = (bf16[272,1088]{1,0:T(8,128)(2,1)S(1)}, bf16[272,1088]{1,0:T(8,128)(2,1)S(1)}, u32[]{:S(2)}, u32[]{:S(2)}) collective-permute-start(bf16[272,1088]{1,0:T(8,128)(2,1)S(1)} %copy-done.55), channel_id=1, source_target_pairs={{0,4},{1,5},{2,6},{3,7},{4,0},{5,1},{6,2},{7,3},{8,12},{9,13},{10,... | collective-permute-start | bytes 1775624 | tf_op jit(solution)/shard_map/ppermute | solution.py:677
  966.1 113.9 %collective-permute-start.61 = (bf16[272,1088]{1,0:T(8,128)(2,1)S(1)}, bf16[272,1088]{1,0:T(8,128)(2,1)S(1)}, u32[]{:S(2)}, u32[]{:S(2)}) collective-permute-start(bf16[272,1088]{1,0:T(8,128)(2,1)S(1)} %copy-done.56), channel_id=1, source_target_pairs={{0,6},{1,7},{2,4},{3,5},{4,2},{5,3},{6,0},{7,1},{8,14},{9,15},{10,... | collective-permute-start | bytes 1775624 | tf_op jit(solution)/shard_map/ppermute | solution.py:677
  971.2 111.2 %collective-permute-start.49 = (bf16[272,2304]{1,0:T(8,128)(2,1)S(1)}, bf16[272,2304]{1,0:T(8,128)(2,1)S(1)}, u32[]{:S(2)}, u32[]{:S(2)}) collective-permute-start(bf16[272,2304]{1,0:T(8,128)(2,1)S(1)} %add_convert_fusion.4), channel_id=1, source_target_pairs={{0,1},{1,0},{2,3},{3,2},{4,5},{5,4},{6,7},{7,6},{8,9},{9,8},{10,11... | collective-permute-start | bytes 3760136 | tf_op jit(solution)/shard_map/ppermute | solution.py:641
  1100.4 30.0 %collective-permute-start.51 = (bf16[272,544]{0,1:T(8,128)(2,1)S(1)}, bf16[272,544]{0,1:T(8,128)(2,1)S(1)}, u32[]{:S(2)}, u32[]{:S(2)}) collective-permute-start(bf16[272,544]{0,1:T(8,128)(2,1)S(1)} %get-tuple-element.181), channel_id=1, source_target_pairs={{0,4},{1,5},{2,6},{3,7},{4,0},{5,1},{6,2},{7,3},{8,12},{9,13},{10,... | collective-permute-start | bytes 887816 | tf_op jit(solution)/shard_map/ppermute | solution.py:677
  1102.4 36.7 %collective-permute-start.52 = (bf16[272,544]{0,1:T(8,128)(2,1)S(1)}, bf16[272,544]{0,1:T(8,128)(2,1)S(1)}, u32[]{:S(2)}, u32[]{:S(2)}) collective-permute-start(bf16[272,544]{0,1:T(8,128)(2,1)S(1)} %get-tuple-element.182), channel_id=1, source_target_pairs={{0,6},{1,7},{2,4},{3,5},{4,2},{5,3},{6,0},{7,1},{8,14},{9,15},{10,... | collective-permute-start | bytes 887816 | tf_op jit(solution)/shard_map/ppermute | solution.py:677
  (135 other events, 1755.4 us)
Sparse Core Ops, SparseCore 0:
  15.7 74.7 all-gather.4
  92.7 101.3 all-gather.6

commit v2 on v1

--- a/solution.py
+++ b/solution.py
@@ -230,14 +230,14 @@
 
     lax.fori_loop(0, jnp.minimum(2, heads - 2 * pair), head_body, 0)
     dq_ref[...] = (dqs[...] * HEAD_DIM**-0.5).astype(jnp.bfloat16)
-    dk_ref[own:, :] = dkg[...] * LN2
-    dv_ref[own:, :] = dvg[...]
+    dk_ref[own:, :] = (dkg[...] * LN2).astype(jnp.bfloat16)
+    dv_ref[own:, :] = dvg[...].astype(jnp.bfloat16)
     for tile in range(tiles):
         for part in range(parts):
             source = pl.ds((tile * parts + part) * QT, QT)
             if part == 0:
-                dk_ref[tile * QT : (tile + 1) * QT, :] = dkt[source, :] * LN2
-                dv_ref[tile * QT : (tile + 1) * QT, :] = dvt[source, :]
+                dk_ref[tile * QT : (tile + 1) * QT, :] = (dkt[source, :] * LN2).astype(jnp.bfloat16)
+                dv_ref[tile * QT : (tile + 1) * QT, :] = dvt[source, :].astype(jnp.bfloat16)
             else:
                 start = (part - 1) * own + tile * QT
                 dko_ref[start : start + QT, :] = (dkt[source, :] * LN2).astype(jnp.bfloat16)
@@ -245,8 +245,11 @@
 
 
 def attention_backward(
-    parts, heads, triple, others, mixed, mixed_grad, lse, mask_trunk, mask_group, start, stop, deps=()
+    parts, heads, triple, others, mixed, mixed_grad, lse, mask_trunk, mask_group, start, stop, before=(), deps=()
 ):
+    fixed = 10
+    aliases = {fixed + index: index for index in range(len(before))}
+    deps = tuple(before) + tuple(deps)
     rows = triple.shape[0]
     pairs = triple.shape[1] // (3 * 128)
     extra = others.shape[0]
@@ -269,13 +272,14 @@
             whole(mask_group.shape),
         ]
         + [pl.BlockSpec(memory_space=pl.ANY)] * len(deps),
-        out_specs=[block(rows, 0), block(rows, 0), block(rows, 0), block(extra, 0), block(extra, 0)],
+        out_specs=[block(rows, start)] * 3 + [block(extra, start)] * 2,
+        input_output_aliases=aliases,
         out_shape=[
-            jax.ShapeDtypeStruct((rows, (stop - start) * 128), jnp.bfloat16),
-            jax.ShapeDtypeStruct((rows, (stop - start) * 128), jnp.float32),
-            jax.ShapeDtypeStruct((rows, (stop - start) * 128), jnp.float32),
-            jax.ShapeDtypeStruct((extra, (stop - start) * 128), jnp.bfloat16),
-            jax.ShapeDtypeStruct((extra, (stop - start) * 128), jnp.bfloat16),
+            jax.ShapeDtypeStruct((rows, pairs * 128), jnp.bfloat16),
+            jax.ShapeDtypeStruct((rows, pairs * 128), jnp.bfloat16),
+            jax.ShapeDtypeStruct((rows, pairs * 128), jnp.bfloat16),
+            jax.ShapeDtypeStruct((extra, pairs * 128), jnp.bfloat16),
+            jax.ShapeDtypeStruct((extra, pairs * 128), jnp.bfloat16),
         ],
         scratch_shapes=[
             pltpu.VMEM((TRUNK, 128), jnp.bfloat16),
@@ -326,37 +330,42 @@
 ROW_CHUNK = 640
 
 
-def ffn_kernel(
-    sizes, outs, chunk, scalars, *refs,
-):
-    count = len(sizes)
-    mine, theirs = refs[:count], refs[count : 2 * count]
-    second, second_t, seed, seed_t, bias = refs[2 * count : 2 * count + 5]
-    edge = 2 * count + 8
-    lowered, second_grad, bias_grad = refs[2 * count + 5 : edge]
-    mine_grads, theirs_grads = refs[edge : edge + outs], refs[edge + outs : edge + 2 * outs]
-    up, down, act, wide, up_grad, down_grad = refs[edge + 2 * outs :]
+def ffn_kernel(outs, chunk, scalars, *refs):
+    up_main, down_main, tails, second, seed, bias = refs[:6]
+    lowered, second_grad, bias_grad = refs[6:9]
+    mine_grads, theirs_grads = refs[9 : 9 + outs], refs[9 + outs : 9 + 2 * outs]
+    up, down, act, wide, up_grad, down_grad, second_t, seed_t = refs[9 + 2 * outs :]
     step = pl.program_id(0)
     role = scalars[0]
-
-    def place(first_part, second_part):
-        for index, size in enumerate(sizes):
-            rows = pl.ds(pl.multiple_of(scalars[1 + index], 16), size)
-            up[rows, :] = first_part[index][...]
-            down[rows, :] = second_part[index][...]
-
-    @pl.when(role == 0)
+    is_rest = step == pl.num_programs(0) - 1
+
+    @pl.when(jnp.logical_not(is_rest))
     def _():
-        place(mine, theirs)
-
-    @pl.when(role != 0)
+        height = up_main.shape[2]
+        for index in range(up_main.shape[0]):
+            rows = pl.ds(index * height, height)
+            up[rows, :] = up_main[index, 0]
+            down[rows, :] = down_main[index, 0]
+
+    @pl.when(is_rest)
     def _():
-        place(theirs, mine)
+        height, columns = tails.shape[2], tails.shape[1]
+        rest = FF_BLOCK // columns
+        for index in range(tails.shape[0]):
+            rows = pl.ds(index * height, height)
+            slabs = [tails[index, c].astype(jnp.float32) for c in range(columns)]
+            for shift, target in ((0, up), (rest, down)):
+                joined = jnp.concatenate([slab[:, shift : shift + rest] for slab in slabs], axis=1)
+                target[rows, :] = joined.astype(jnp.bfloat16)
 
     @pl.when(step == 0)
     def _():
         lowered[...] = jnp.zeros_like(lowered)
         second_grad[...] = jnp.zeros_like(second_grad)
+        for start in range(0, second.shape[0], 128):
+            rows = pl.ds(start, 128)
+            second_t[:, rows] = second[rows, :].T
+            seed_t[:, rows] = seed[rows, :].T
 
     total = jnp.zeros((1, FF_BLOCK), jnp.float32)
     for start in range(0, second.shape[0], chunk):
@@ -392,23 +401,33 @@
         deliver(down_grad, up_grad)
 
 
-def feed_forward(scalars, mine, theirs, second, seed, bias, outs):
+def feed_forward(scalars, main, second, seed, bias, outs):
     rows, width = second.shape
-    hidden = mine[0].shape[1]
-    sizes = tuple(piece.shape[0] for piece in mine)
-    piece_specs = [pl.BlockSpec((size, FF_BLOCK), lambda j, s: (0, j)) for size in sizes]
+    hidden = bias.shape[0]
+    last = hidden // FF_BLOCK - 2
+    per = (last + 1) // main.shape[1]
+
+    def main_spec(shift):
+        def index(j, s):
+            j = jnp.minimum(j, last)
+            return (0, j // per, 0, j % per + shift)
+
+        return pl.BlockSpec((main.shape[0], 1, main.shape[2], FF_BLOCK), index)
+
+    tail_spec = pl.BlockSpec(main.shape[:3] + (128,), lambda j, s: (0, 0, 0, 4 * per))
     whole = lambda shape: pl.BlockSpec(shape, lambda j, s: (0, 0))
     grad_spec = pl.BlockSpec((width // outs, FF_BLOCK), lambda j, s: (0, j))
     grad_shape = jax.ShapeDtypeStruct((width // outs, hidden), jnp.bfloat16)
     line = pl.BlockSpec((1, FF_BLOCK), lambda j, s: (0, j))
     chunk = ROW_CHUNK if rows % ROW_CHUNK == 0 else rows // 2
     return pl.pallas_call(
-        partial(ffn_kernel, sizes, outs, chunk),
+        partial(ffn_kernel, outs, chunk),
         grid_spec=pltpu.PrefetchScalarGridSpec(
             num_scalar_prefetch=1,
             grid=(hidden // FF_BLOCK,),
-            in_specs=piece_specs * 2 + [
-                whole((rows, width)), whole((width, rows)), whole((rows, width)), whole((width, rows)), line,
+            in_specs=[
+                main_spec(0), main_spec(per), tail_spec,
+                whole((rows, width)), whole((rows, width)), line,
             ],
             out_specs=[whole((rows, width)), whole((rows, width)), line] + [grad_spec] * (2 * outs),
             scratch_shapes=[
@@ -418,6 +437,8 @@
                 pltpu.VMEM((rows, FF_BLOCK), jnp.bfloat16),
                 pltpu.VMEM((width, FF_BLOCK), jnp.bfloat16),
                 pltpu.VMEM((width, FF_BLOCK), jnp.bfloat16),
+                pltpu.VMEM((width, rows), jnp.bfloat16),
+                pltpu.VMEM((width, rows), jnp.bfloat16),
             ],
         ),
         out_shape=[
@@ -432,7 +453,594 @@
             transcendentals=rows * hidden,
         ),
         name="feed_forward",
-    )(scalars, *mine, *theirs, second, second.T, seed, seed.T, bias.reshape(1, hidden))
+    )(scalars, main, main, main, second, seed, bias.reshape(1, hidden))
+
+
+MESH = pl.DeviceIdType.MESH
+HOLD = pl.BlockSpec(memory_space=pl.ANY)
+
+
+def greet(peers):
+    barrier = pltpu.get_barrier_semaphore()
+    for peer in peers:
+        pl.semaphore_signal(barrier, inc=1, device_id=peer, device_id_type=MESH)
+    pl.semaphore_wait(barrier, len(peers))
+
+
+def remote(source, target, send, receive, device):
+    return pltpu.make_async_remote_copy(
+        src_ref=source, dst_ref=target, send_sem=send, recv_sem=receive,
+        device_id=device, device_id_type=MESH,
+    )
+
+
+def chunk_home(chunk):
+    block = chunk // 2
+    turn = block % 4
+    in_trunk = chunk < 16
+    owner = jnp.where(in_trunk, ((turn + 1) // 2) % 2, (chunk - 16) // 12)
+    spot = jnp.where(
+        in_trunk, 2 * (2 * (block // 4) + turn // 2) + chunk % 2, 8 + (chunk - 16) % 12
+    )
+    return owner, spot
+
+
+def start_kernel(grain, pack, later_pack, value, full, rows, later_out, z_send, z_recv, r_send, r_recv, c_send, c_recv,
+                 x_send, x_recv, own_sem, later_sem):
+    row, col = lax.axis_index("row"), lax.axis_index("col")
+    z, core = col // 2, col % 2
+    at = lambda r, c: (r, c)
+    peers = [at(row, (col + shift) % 8) for shift in range(1, 8)] + [at(row ^ 1, col), at(row ^ 2, col)]
+    greet(peers)
+    later_copy = pltpu.make_async_copy(later_pack, later_out, later_sem)
+    later_copy.start()
+    here = full.at[core, row, z]
+    own = pltpu.make_async_copy(pack, here, own_sem)
+    own.start()
+    sends = []
+    for d in range(1, 4):
+        copy = remote(pack, here, z_send.at[d - 1], z_recv.at[d - 1], at(row, (z ^ d) * 2 + core))
+        copy.start()
+        sends.append(copy)
+    own.wait()
+    for copy in sends:
+        copy.wait_recv()
+    later = []
+
+    def pass_on(index, ref, device, send=r_send, receive=r_recv):
+        copy = remote(ref, ref, send.at[index], receive.at[index], device)
+        copy.start()
+        later.append(copy)
+        return copy
+
+    beside = pass_on(0, full.at[core, row], at(row ^ 1, col))
+    below = pass_on(1, full.at[core, row], at(row ^ 2, col))
+    swaps = [pass_on(0, full.at[core, row], at(row, col ^ 1), c_send, c_recv)]
+
+    each = value.shape[1] // grain
+
+    def each_chunk(act_remote, act_own):
+        for m in range(4):
+            for i in range(each):
+                owner, spot = chunk_home(col * each + i)
+                source = value.at[m, pl.ds(i * grain, grain), :]
+                target = rows.at[pl.ds(pl.multiple_of(spot * grain, grain), grain), :]
+                same = jnp.logical_and(z == m, owner == core)
+                index = m * each + i
+
+                @pl.when(jnp.logical_not(same))
+                def _():
+                    act_remote(
+                        remote(source, target, x_send.at[index], x_recv, at(row, 2 * m + owner))
+                    )
+
+                if act_own:
+
+                    @pl.when(same)
+                    def _():
+                        pltpu.make_async_copy(source, target, x_recv).start()
+
+    each_chunk(lambda copy: copy.start(), True)
+    beside.wait_recv()
+    far_a = pass_on(2, full.at[core, row ^ 1, pl.ds(0, 2)], at(row ^ 2, col))
+    swaps.append(pass_on(1, full.at[core, row ^ 1], at(row, col ^ 1), c_send, c_recv))
+    below.wait_recv()
+    far_b = pass_on(3, full.at[core, row ^ 2, pl.ds(2, 2)], at(row ^ 1, col))
+    swaps.append(pass_on(2, full.at[core, row ^ 2], at(row, col ^ 1), c_send, c_recv))
+    far_a.wait_recv()
+    far_b.wait_recv()
+    swaps.append(pass_on(3, full.at[core, row ^ 3], at(row, col ^ 1), c_send, c_recv))
+    for copy in swaps:
+        copy.wait_recv()
+    pltpu.make_async_copy(rows, rows, x_recv).wait()
+    later_copy.wait()
+    for copy in sends + later:
+        copy.wait_send()
+    each_chunk(lambda copy: copy.wait_send(), False)
+
+
+def start_exchange(pack, later_pack, value, count):
+    grain = 64
+    height, lanes = pack.shape
+    copies = 4 * (value.shape[1] // grain)
+    dma = lambda n: pltpu.SemaphoreType.DMA((n,))
+    return pl.pallas_call(
+        partial(start_kernel, grain),
+        in_specs=[HOLD] * 3,
+        out_specs=[HOLD] * 3,
+        out_shape=[
+            jax.ShapeDtypeStruct((2, 4, 4, height, lanes), pack.dtype),
+            jax.ShapeDtypeStruct((count, value.shape[2]), value.dtype),
+            jax.ShapeDtypeStruct(later_pack.shape, later_pack.dtype),
+        ],
+        scratch_shapes=[
+            dma(3), dma(3), dma(4), dma(4), dma(4), dma(4), dma(copies),
+            pltpu.SemaphoreType.DMA, pltpu.SemaphoreType.DMA, pltpu.SemaphoreType.DMA,
+        ],
+        compiler_params=pltpu.CompilerParams(collective_id=0, has_side_effects=True),
+        cost_estimate=pl.CostEstimate(flops=100_000_000_000, bytes_accessed=0, transcendentals=0),
+        name="start_exchange",
+    )(pack, later_pack, value)
+
+
+def end_kernel(
+    grain, grads, small, rows, *refs,
+):
+    final, small_out, tokens, mine, swapped, far, beside, below, tail, small_col, small_row, part = refs[-26:-14]
+    own_sem, c_send, c_recv, r_send, r_recv, z_send, z_recv, s_send, s_recv, t_send, t_recv, _, x_send, x_recv = refs[-14:]
+    row, col = lax.axis_index("row"), lax.axis_index("col")
+    z, core = col // 2, col % 2
+    at = lambda r, c: (r, c)
+    peers = [at(row, (col + shift) % 8) for shift in range(1, 8)]
+    peers += [at(row ^ d, col) for d in range(1, 4)]
+    greet(peers)
+    own = pltpu.make_async_copy(grads.at[core], mine, own_sem)
+    own.start()
+    sends = []
+    for d in (3, 1, 2, 0):
+        copy = remote(
+            grads.at[1 - core, row ^ d], swapped.at[row ^ d], c_send.at[d], c_recv.at[d], at(row, col ^ 1)
+        )
+        copy.start()
+        sends.append(copy)
+    for shift in range(1, 8):
+        copy = remote(
+            small, small_col.at[col], s_send.at[shift - 1], s_recv.at[7 - shift], at(row, (col + shift) % 8)
+        )
+        copy.start()
+        sends.append(copy)
+    small_col[col] = small[...]
+    own.wait()
+    f32 = jnp.float32
+    each = tokens.shape[1] // grain
+
+    def each_chunk(act_remote, act_own):
+        for local in range(rows.shape[0] // grain):
+            pair = local // 2
+            turn = 4 * (pair // 2) + (core if pair % 2 == 0 else 3 - core)
+            chunk = 2 * turn + local % 2 if local < 8 else 16 + 12 * core + local - 8
+            shard = chunk // each
+            source = rows.at[pl.ds(local * grain, grain), :]
+            start = pl.multiple_of((chunk % each) * grain, grain)
+            target = tokens.at[z, pl.ds(start, grain), :]
+
+            @pl.when(shard != col)
+            def _():
+                act_remote(remote(source, target, x_send.at[local], x_recv, at(row, shard)))
+
+            if act_own:
+
+                @pl.when(shard == col)
+                def _():
+                    pltpu.make_async_copy(source, target, x_recv).start()
+
+    each_chunk(lambda copy: copy.start(), True)
+
+    def add(target, source):
+        target[...] = (target[...].astype(f32) + source[...].astype(f32)).astype(target.dtype)
+
+    def add_swapped(position):
+        sends[position].wait_recv()
+        d = (3, 1, 2, 0)[position]
+        for q in range(4):
+            add(mine.at[row ^ d, q], swapped.at[row ^ d, q])
+
+    def send(index, source, target, device):
+        copy = remote(source, target, r_send.at[index], r_recv.at[index], device)
+        copy.start()
+        sends.append(copy)
+        return copy
+
+    add_swapped(0)
+    far_a = send(0, mine.at[row ^ 3, pl.ds(0, 2)], far.at[pl.ds(0, 2)], at(row ^ 2, col))
+    far_b = send(1, mine.at[row ^ 3, pl.ds(2, 2)], far.at[pl.ds(2, 2)], at(row ^ 1, col))
+    add_swapped(1)
+    x_b = send(2, mine.at[row ^ 1, pl.ds(2, 2)], beside.at[pl.ds(2, 2)], at(row ^ 1, col))
+    add_swapped(2)
+    y_a = send(3, mine.at[row ^ 2, pl.ds(0, 2)], below.at[pl.ds(0, 2)], at(row ^ 2, col))
+    add_swapped(3)
+    for shift in range(1, 8):
+        sends[3 + shift].wait_recv()
+    part[...] = small_col[0]
+    for c in range(1, 8):
+        part[...] += small_col[c]
+    rounds = []
+    for d in range(1, 4):
+        copy = remote(part, small_row.at[row], t_send.at[d - 1], t_recv.at[d - 1], at(row ^ d, col))
+        copy.start()
+        rounds.append(copy)
+    small_row[row] = part[...]
+    far_a.wait_recv()
+    for q in (0, 1):
+        add(mine.at[row ^ 1, q], far.at[q])
+    x_a = send(4, mine.at[row ^ 1, pl.ds(0, 2)], beside.at[pl.ds(0, 2)], at(row ^ 1, col))
+    far_b.wait_recv()
+    for q in (2, 3):
+        add(mine.at[row ^ 2, q], far.at[q])
+    y_b = send(5, mine.at[row ^ 2, pl.ds(2, 2)], below.at[pl.ds(2, 2)], at(row ^ 2, col))
+    for copy in (x_b, y_a, x_a, y_b):
+        copy.wait_recv()
+
+    def total(q):
+        return (
+            mine[row, q].astype(f32) + beside[q].astype(f32) + below[q].astype(f32)
+        )
+
+    lasts = []
+    for d in range(1, 4):
+        q = z ^ d
+        mine[row, q] = total(q).astype(mine.dtype)
+        copy = remote(
+            mine.at[row, q], tail.at[d - 1], z_send.at[d - 1], z_recv.at[d - 1], at(row, q * 2 + core)
+        )
+        copy.start()
+        lasts.append(copy)
+    result = total(z)
+    for d in range(1, 4):
+        lasts[d - 1].wait_recv()
+        result = result + tail[d - 1].astype(f32)
+    final[...] = result
+    for copy in rounds:
+        copy.wait_recv()
+    pltpu.make_async_copy(tokens, tokens, x_recv).wait()
+    each_chunk(lambda copy: copy.wait_send(), False)
+    small_out[...] = small_row[0] + small_row[1] + small_row[2] + small_row[3]
+    for copy in sends + lasts + rounds:
+        copy.wait_send()
+
+
+def end_exchange(grads, small, rows, shape, deps):
+    grain = 64
+    height, lanes = grads.shape[3:]
+    slab = lambda *n: pltpu.VMEM(n + (height, lanes), grads.dtype)
+    dma = lambda n: pltpu.SemaphoreType.DMA((n,))
+    return pl.pallas_call(
+        partial(end_kernel, grain),
+        in_specs=[HOLD, pl.BlockSpec(memory_space=pltpu.VMEM), HOLD] + [HOLD] * len(deps),
+        out_specs=[pl.BlockSpec(memory_space=pltpu.VMEM)] * 2 + [HOLD],
+        out_shape=[
+            jax.ShapeDtypeStruct((height, lanes), jnp.float32),
+            jax.ShapeDtypeStruct(small.shape, jnp.float32),
+            jax.ShapeDtypeStruct(shape, rows.dtype),
+        ],
+        scratch_shapes=[
+            slab(4, 4), slab(4, 4), slab(4), slab(4), slab(4), slab(3),
+            pltpu.VMEM((8,) + small.shape, jnp.float32), pltpu.VMEM((4,) + small.shape, jnp.float32),
+            pltpu.VMEM(small.shape, jnp.float32),
+            pltpu.SemaphoreType.DMA, dma(4), dma(4), dma(6), dma(6), dma(3), dma(3),
+            dma(7), dma(7), dma(3), dma(3), dma(1), dma(rows.shape[0] // grain), pltpu.SemaphoreType.DMA,
+        ],
+        compiler_params=pltpu.CompilerParams(
+            collective_id=1, has_side_effects=True, vmem_limit_bytes=40 * 1024 * 1024
+        ),
+        cost_estimate=pl.CostEstimate(flops=100_000_000_000, bytes_accessed=0, transcendentals=0),
+        name="end_exchange",
+    )(grads, small, rows, *deps)
+
+
+def lane_runs(width, padded, columns, qkv_cols, out_cols):
+    runs = []
+    for c in range(columns):
+        start = c * qkv_cols
+        while start < (c + 1) * qkv_cols:
+            third = start // width
+            stop = min((c + 1) * qkv_cols, (third + 1) * width)
+            runs.append((0, third * padded + start - third * width, c, start - c * qkv_cols, stop - start))
+            start = stop
+        runs.append((1, c * out_cols, c, qkv_cols, out_cols))
+    return runs
+
+
+def assemble_kernel(runs, width, padded, full, triple, out):
+    step = pl.program_id(0)
+    height = full.shape[3]
+    columns = 2 * full.shape[2]
+    slabs = [full[c % 2, 0, c // 2].astype(jnp.float32) for c in range(columns)]
+    piece = lambda run: slabs[run[2]][:, run[3] : run[3] + run[4]]
+    gap = jnp.zeros((height, padded - width), jnp.float32)
+
+    def line(which, third):
+        low, high = third * padded, third * padded + padded
+        chosen = [r for r in runs if r[0] == which and low <= r[1] < high]
+        return jnp.concatenate([piece(r) for r in chosen] + [gap], axis=1).astype(triple.dtype)
+
+    for third in range(3):
+        triple[:, third * padded : (third + 1) * padded] = line(0, third)
+
+    @pl.when(step == 0)
+    def _():
+        out[width:, :] = jnp.zeros((padded - width, padded), out.dtype)
+
+    out[pl.ds(pl.multiple_of(step * height, 16), height), :] = line(1, 0)
+
+
+def assemble(full, width, padded, qkv_cols):
+    height, lanes = full.shape[3:]
+    runs = lane_runs(width, padded, 2 * full.shape[2], qkv_cols, lanes - qkv_cols)
+    return pl.pallas_call(
+        partial(assemble_kernel, runs, width, padded),
+        grid=(full.shape[1],),
+        in_specs=[pl.BlockSpec((2, 1, full.shape[2], height, lanes), lambda r: (0, r, 0, 0, 0))],
+        out_specs=[
+            pl.BlockSpec((height, 3 * padded), lambda r: (r, 0)),
+            pl.BlockSpec((padded, padded), lambda r: (0, 0)),
+        ],
+        out_shape=[
+            jax.ShapeDtypeStruct((width, 3 * padded), full.dtype),
+            jax.ShapeDtypeStruct((padded, padded), full.dtype),
+        ],
+        compiler_params=pltpu.CompilerParams(vmem_limit_bytes=48 * 1024 * 1024),
+        cost_estimate=pl.CostEstimate(flops=12_000_000_000, bytes_accessed=0, transcendentals=0),
+        name="assemble_weights",
+    )(full)
+
+
+def divide_kernel(runs, triple, out, full):
+    wide = triple[...].astype(jnp.float32)
+    last = out[...].astype(jnp.float32)
+    for c in range(2 * full.shape[2]):
+        parts = [
+            (wide, last)[r[0]][:, r[1] : r[1] + r[4]] for r in runs if r[2] == c
+        ]
+        full[c % 2, 0, c // 2] = jnp.concatenate(parts, axis=1).astype(full.dtype)
+
+
+def divide(triple, out, width, padded, qkv_cols, out_cols, columns, rows):
+    height, lanes = width // rows, qkv_cols + out_cols
+    runs = lane_runs(width, padded, columns, qkv_cols, out_cols)
+    return pl.pallas_call(
+        partial(divide_kernel, runs),
+        grid=(rows,),
+        in_specs=[
+            pl.BlockSpec((height, 3 * padded), lambda r: (r, 0)),
+            pl.BlockSpec((height, out.shape[1]), lambda r: (r, 0)),
+        ],
+        out_specs=pl.BlockSpec((2, 1, columns // 2, height, lanes), lambda r: (0, r, 0, 0, 0)),
+        out_shape=jax.ShapeDtypeStruct((2, rows, columns // 2, height, lanes), jnp.bfloat16),
+        compiler_params=pltpu.CompilerParams(vmem_limit_bytes=48 * 1024 * 1024),
+        cost_estimate=pl.CostEstimate(flops=12_000_000_000, bytes_accessed=0, transcendentals=0),
+        name="divide_gradients",
+    )(triple, out)
+
+
+def finish_kernel(own_trunk, dq, dk, dv, other_k, other_v, *refs):
+    total, sums = refs[-2:]
+    step = pl.program_id(0)
+    each = pl.num_programs(0) // 3
+
+    def deliver(value):
+        total[...] = value
+        sums[...] = jnp.sum(value.astype(jnp.float32), axis=0, keepdims=True)
+
+    @pl.when(step < each)
+    def _():
+        deliver(dq[...])
+
+    for index, (near, far) in enumerate(((dk, other_k), (dv, other_v))):
+
+        @pl.when(step // each == index + 1)
+        def _():
+            value = near[:own_trunk, :].astype(jnp.float32)
+            for start in range(0, far.shape[0], own_trunk):
+                value = value + far[start : start + own_trunk, :].astype(jnp.float32)
+            deliver(jnp.concatenate([value.astype(total.dtype), near[own_trunk:, :]], axis=0))
+
+
+def finish_gradients(own_trunk, dq, dk, dv, other_k, other_v, deps):
+    rows, padded = dq.shape
+    block = 384
+    each = padded // block
+
+    def spec(count, third):
+        return pl.BlockSpec((count, block), lambda j: (0, jnp.clip(j - third * each, 0, each - 1)))
+
+    return pl.pallas_call(
+        partial(finish_kernel, own_trunk),
+        grid=(3 * each,),
+        in_specs=[
+            spec(rows, 0), spec(rows, 1), spec(rows, 2), spec(other_k.shape[0], 1), spec(other_v.shape[0], 2),
+        ]
+        + [HOLD] * len(deps),
+        out_specs=[
+            pl.BlockSpec((rows, block), lambda j: (0, j)), pl.BlockSpec((1, block), lambda j: (0, j)),
+        ],
+        out_shape=[
+            jax.ShapeDtypeStruct((rows, 3 * padded), jnp.bfloat16),
+            jax.ShapeDtypeStruct((1, 3 * padded), jnp.float32),
+        ],
+        compiler_params=pltpu.CompilerParams(vmem_limit_bytes=48 * 1024 * 1024),
+        cost_estimate=pl.CostEstimate(flops=8_000_000_000, bytes_accessed=0, transcendentals=0),
+        name="finish_gradients",
+    )(dq, dk, dv, other_k, other_v, *deps)
+
+
+def norm_parts(value):
+    center = value - jnp.mean(value, axis=-1, keepdims=True)
+    scale = lax.rsqrt(jnp.mean(center * center, axis=-1, keepdims=True) + 1e-05)
+    return center * scale, scale
+
+
+def norm_back(grad, value, gain):
+    unit, scale = norm_parts(value)
+    scaled = grad * gain
+    back = scaled - jnp.mean(scaled, axis=-1, keepdims=True)
+    back = scale * (back - unit * jnp.mean(scaled * unit, axis=-1, keepdims=True))
+    return back, jnp.sum(grad * unit, axis=0, keepdims=True), jnp.sum(grad, axis=0, keepdims=True)
+
+
+def out_kernel(mixed, weight, bias, rows, gain, shift, middle, second):
+    width = rows.shape[1]
+    attended = dot_nn(mixed[...], weight[...])[:, :width] + bias[...]
+    total = rows[...].astype(jnp.float32) + attended.astype(jnp.bfloat16).astype(jnp.float32)
+    middle[...] = total
+    unit, _ = norm_parts(total)
+    second[...] = (unit * gain[...] + shift[...]).astype(jnp.bfloat16)
+
+
+def by_rows(kernel, name, count, chunked, fixed, outs, sums=(), scratch=(), flops=0):
+    chunk = count // 5
+    block = lambda width: pl.BlockSpec((chunk, width), lambda i: (i, 0))
+    whole = lambda shape: pl.BlockSpec(shape, lambda i: (0,) * len(shape))
+    return pl.pallas_call(
+        kernel,
+        grid=(5,),
+        in_specs=[block(v.shape[1]) for v in chunked] + [whole(v.shape) for v in fixed],
+        out_specs=[block(width) for width, _ in outs] + [whole(shape) for shape, _ in sums],
+        out_shape=[jax.ShapeDtypeStruct((count, width), dtype) for width, dtype in outs]
+        + [jax.ShapeDtypeStruct(shape, dtype) for shape, dtype in sums],
+        scratch_shapes=list(scratch),
+        compiler_params=pltpu.CompilerParams(vmem_limit_bytes=56 * 1024 * 1024),
+        cost_estimate=pl.CostEstimate(flops=flops, bytes_accessed=0, transcendentals=0),
+        name=name,
+    )(*chunked, *fixed)
+
+
+def project_out(mixed, rows, weight, bias, gain, shift):
+    width = rows.shape[1]
+
+    def kernel(mixed, rows, weight, bias, gain, shift, middle, second):
+        out_kernel(mixed, weight, bias, rows, gain, shift, middle, second)
+
+    line = lambda v: v.reshape(1, width)
+    return by_rows(
+        kernel, "project_out", rows.shape[0], (mixed, rows), (weight, line(bias), line(gain), line(shift)),
+        ((width, jnp.float32), (width, jnp.bfloat16)), flops=12_000_000_000,
+    )
+
+
+def middle_kernel(second_grad, lowered, middle, seed, mixed, weight, gain, down_bias,
+                  result, middle_grad, mixed_grad, sums, out_grad, total):
+    step = pl.program_id(0)
+    width = middle.shape[1]
+    value, up = middle[...], seed[...].astype(jnp.float32)
+    result[...] = (value + lowered[...] + down_bias[...]).astype(jnp.bfloat16)
+    back, gain_sum, shift_sum = norm_back(second_grad[...], value, gain[...])
+    grad = up + back
+    middle_grad[...] = grad
+    low = grad.astype(jnp.bfloat16)
+    mixed_grad[...] = dot_nt(low, weight[:, :width]).astype(jnp.bfloat16)
+    part = dot_tn(mixed[...], low)
+    low_sum = jnp.sum(low.astype(jnp.float32), axis=0, keepdims=True)
+    up_sum = jnp.sum(up, axis=0, keepdims=True)
+    lines = jnp.concatenate([low_sum, gain_sum, shift_sum, up_sum], axis=0)
+
+    @pl.when(step == 0)
+    def _():
+        sums[...] = lines
+        total[...] = part
+
+    @pl.when(step > 0)
+    def _():
+        sums[...] += lines
+        total[...] += part
+
+    @pl.when(step == pl.num_programs(0) - 1)
+    def _():
+        out_grad[:, :width] = total[:width, :].astype(jnp.bfloat16)
+        out_grad[:, width:] = jnp.zeros((width, out_grad.shape[1] - width), jnp.bfloat16)
+
+
+def middle_back(second_grad, lowered, middle, seed, mixed, weight, gain, down_bias):
+    rows, width = middle.shape
+    padded = weight.shape[0]
+    line = lambda v: v.reshape(1, width)
+    return by_rows(
+        middle_kernel, "middle_back", rows, (second_grad, lowered, middle, seed, mixed),
+        (weight, line(gain), line(down_bias)),
+        ((width, jnp.bfloat16), (width, jnp.float32), (padded, jnp.bfloat16)),
+        (((4, width), jnp.float32), ((width, padded), jnp.bfloat16)),
+        (pltpu.VMEM((padded, width), jnp.float32),), flops=25_000_000_000,
+    )
+
+
+def first_kernel(triple_grad, rows, middle_grad, weight, gain, input_grad, sums):
+    step = pl.program_id(0)
+    grad = dot_nt(triple_grad[...], weight[...])
+    back, gain_sum, shift_sum = norm_back(grad, rows[...].astype(jnp.float32), gain[...])
+    input_grad[...] = (middle_grad[...] + back).astype(jnp.bfloat16)
+    lines = jnp.concatenate([gain_sum, shift_sum], axis=0)
+
+    @pl.when(step == 0)
+    def _():
+        sums[...] = lines
+
+    @pl.when(step > 0)
+    def _():
+        sums[...] += lines
+
+
+def first_back(triple_grad, rows, middle_grad, weight, gain):
+    count, width = rows.shape
+    return by_rows(
+        first_kernel, "first_back", count, (triple_grad, rows, middle_grad), (weight, gain.reshape(1, width)),
+        ((width, jnp.bfloat16),), (((2, width), jnp.float32),), flops=25_000_000_000,
+    )
+
+
+def blocks_kernel(rest, core, total, other, total_tail, other_tail, out):
+    quarter = pl.program_id(0)
+    main = total.shape[1]
+    out[0, :, :main] = total[...]
+    out[0, :, main : 2 * main] = other[...]
+    for shard in range(8):
+
+        @pl.when(2 * quarter + core[0] == shard)
+        def _():
+            cut = slice(shard * rest, (shard + 1) * rest)
+            out[0, :, 2 * main : 2 * main + rest] = total_tail[:, cut]
+            out[0, :, 2 * main + rest :] = other_tail[:, cut]
+
+
+def pair_blocks(core, total, other, main, rest):
+    rows = total.shape[0]
+    spec = pl.BlockSpec((rows, main), lambda q, s: (0, 2 * q + s[0]))
+    tail = pl.BlockSpec((rows, 8 * rest), lambda q, s: (0, main // rest))
+    return pl.pallas_call(
+        partial(blocks_kernel, rest),
+        grid_spec=pltpu.PrefetchScalarGridSpec(
+            num_scalar_prefetch=1,
+            grid=(4,),
+            in_specs=[spec, spec, tail, tail],
+            out_specs=pl.BlockSpec((1, rows, 2 * (main + rest)), lambda q, s: (q, 0, 0)),
+        ),
+        out_shape=jax.ShapeDtypeStruct((4, rows, 2 * (main + rest)), total.dtype),
+        cost_estimate=pl.CostEstimate(flops=5_000_000_000, bytes_accessed=0, transcendentals=0),
+        name="pair_blocks",
+    )(core, total, other, total, other)
+
+
+def after(value, *deps):
+    def kernel(*refs):
+        pass
+
+    return pl.pallas_call(
+        kernel,
+        in_specs=[HOLD] * (1 + len(deps)),
+        out_specs=HOLD,
+        out_shape=jax.ShapeDtypeStruct(value.shape, value.dtype),
+        input_output_aliases={0: 0},
+        name="after",
+    )(value, *deps)
 
 
 def layer_norm(value, gain, bias):
@@ -543,8 +1151,8 @@
         ]
         return lax.all_to_all(value, "col", 0, 0, axis_index_groups=groups, tiled=True)
 
-    def to_tree_sources(self, value):
-        mine = self.swap_quarters(value).reshape(self.micro * self.length, value.shape[2])
+    def tree_sources(self, value):
+        mine = value.reshape(self.micro * self.length, value.shape[2])
         return [mine] + [lax.ppermute(mine, "col", self.part_perm(e)) for e in range(1, self.parts)]
 
     def to_tree(self, sources):
@@ -671,90 +1279,10 @@
     return (base + beside + below).astype(jnp.bfloat16)
 
 
-def column_scatter(place, pick):
-    total = pick(0)
-    for d in range(1, place.micro):
-        total = total + lax.ppermute(
-            pick(d).astype(jnp.bfloat16), "col", place.quarter_perm(d)
-        ).astype(jnp.float32)
-    return total
-
-
-def sum_all(values):
-    sizes = [v.shape[0] for v in values]
-    flat = jnp.concatenate(values)
-    flat = jnp.pad(flat, (0, -flat.shape[0] % 1024)).reshape(-1, 128)
-    for axis in ("col", "row"):
-        size = lax.axis_size(axis)
-        shift = 1
-        while shift < size:
-            flat = flat + lax.ppermute(flat, axis, [(i, i ^ shift) for i in range(size)])
-            shift *= 2
-    flat = flat.reshape(-1)
-    out, start = [], 0
-    for size in sizes:
-        out.append(flat[start : start + size])
-        start += size
-    return out
-
-
-def assemble_kernel(sizes, edge, scalars, *refs):
-    count = len(sizes)
-    mine, theirs = refs[:count], refs[count : 2 * count]
-    triple, out = refs[2 * count :]
-    step = pl.program_id(0)
-    use_mine = (step < edge) == (scalars[0] == 0)
-    total = sum(sizes)
-
-    def fill(target, pieces):
-        for index, size in enumerate(sizes):
-            rows = pl.ds(pl.multiple_of(scalars[1 + index], 16), size)
-            target[rows, :] = pieces[index][...]
-
-    for own in (True, False):
-        for low in (True, False):
-
-            @pl.when(jnp.logical_and(use_mine == own, (step < edge + edge // 2) == low))
-            def _():
-                fill(triple if low else out, mine if own else theirs)
-
-    @pl.when(step >= edge + edge // 2)
-    def _():
-        out[total:, :] = jnp.zeros((out.shape[0] - total, out.shape[1]), out.dtype)
-
-
-def assemble(scalars, mine, theirs, padded):
-    block = 384
-    edge = 2 * padded // block
-    sizes = tuple(piece.shape[0] for piece in mine)
-    width = sum(sizes)
-
-    def source(own):
-        def index(j, s):
-            first = (s[0] == 0) if own else (s[0] != 0)
-            return (0, jnp.where(first, jnp.minimum(j, edge - 1), jnp.maximum(j - edge, 0)))
-
-        return [pl.BlockSpec((size, block), index) for size in sizes]
-
-    return pl.pallas_call(
-        partial(assemble_kernel, sizes, edge),
-        grid_spec=pltpu.PrefetchScalarGridSpec(
-            num_scalar_prefetch=1,
-            grid=(2 * edge,),
-            in_specs=source(True) + source(False),
-            out_specs=[
-                pl.BlockSpec((width, block), lambda j, s: (0, jnp.minimum(j, 3 * edge // 2 - 1))),
-                pl.BlockSpec((padded, block), lambda j, s: (0, jnp.maximum(j - 3 * edge // 2, 0))),
-            ],
-        ),
-        out_shape=[
-            jax.ShapeDtypeStruct((width, 3 * padded), jnp.bfloat16),
-            jax.ShapeDtypeStruct((padded, padded), jnp.bfloat16),
-        ],
-        compiler_params=pltpu.CompilerParams(vmem_limit_bytes=48 * 1024 * 1024),
-        cost_estimate=pl.CostEstimate(flops=0, bytes_accessed=16 * width * padded, transcendentals=0),
-        name="assemble_weights",
-    )(scalars, *mine, *theirs)
+def pack_pair(w_up, w_down):
+    main = w_up.shape[1] // 256 * 256
+    down = w_down.T
+    return jnp.concatenate([w_up[:, :main], down[:, :main], w_up[:, main:], down[:, main:]], axis=1)
 
 
 class QuickWeights:
@@ -764,38 +1292,27 @@
         self.cols = place.columns
         self.width = w_out.shape[1] * self.cols
         self.qkv_cols, self.out_cols, self.up_cols = w_qkv.shape[1], w_out.shape[1], w_up.shape[1]
-        self.main = self.up_cols // 256 * 256
-        self.rest = self.up_cols - self.main
-        starts = row_starts(self.rows)
+        self.main = main = self.up_cols // 256 * 256
+        self.rest = rest = self.up_cols - main
         self.role = place.part
-        self.scalars = jnp.stack([self.role] + starts).astype(jnp.int32)
-        pad = padded - self.width
-
-        pack = jnp.concatenate([w_qkv, w_out], axis=1)
-        full = lax.all_gather(pack, "col", axis=0, tiled=False).transpose(1, 0, 2)
-        qkv = full[:, :, : self.qkv_cols].reshape(self.rows, 3, self.width)
-        out = full[:, :, self.qkv_cols :].reshape(self.rows, 1, self.width)
-        four = jnp.pad(jnp.concatenate([qkv, out], axis=1), ((0, 0), (0, 0), (0, pad)))
-        mine = jnp.where(self.role == 0, four[:, :2], four[:, 2:]).reshape(self.rows, 2 * padded)
-        mine = row_gather(mine)
-        theirs = [core_swap(place, piece) for piece in mine]
-        self.triple, self.out = assemble(self.scalars, mine, theirs, padded)
-
-        main = self.main
-        down = w_down.T
-        pack = jnp.concatenate([w_up[:, :main], down[:, :main], w_up[:, main:], down[:, main:]], axis=1)
-        full = lax.all_gather(pack, "col", axis=0, tiled=False)
-        rest = self.rest
-
-        def role_part(role):
-            body = full[:, :, role * main : (role + 1) * main].transpose(1, 0, 2)
-            tail = full[:, :, 2 * main + role * rest : 2 * main + (role + 1) * rest].transpose(1, 0, 2)
-            return jnp.concatenate(
-                [body.reshape(self.rows, self.cols * main), tail.reshape(self.rows, self.cols * rest)], axis=1
-            )
-
-        self.mine = row_gather(jnp.where(self.role == 0, role_part(0), role_part(1)))
-        self.theirs = [core_swap(place, piece) for piece in self.mine]
+        self.scalars = jnp.stack([self.role] + row_starts(self.rows)).astype(jnp.int32)
+        self.pack = pack_pair(w_up, w_down)
+
+    def start(self, w_qkv, w_out, value):
+        full, rows, pack = start_exchange(
+            jnp.concatenate([w_qkv, w_out], axis=1), self.pack, value, self.place.count
+        )
+        pair = lax.all_gather(pack, BOTH, axis=0, tiled=False)
+        self.pair = pair.reshape(lax.axis_size("row"), self.cols, self.rows, 2 * self.up_cols)
+        self.triple, self.out = assemble(full, self.width, self.padded, self.qkv_cols)
+        return rows
+
+    def end(self, triple_grad, out_grad, small, rows, shape, deps):
+        blocks = divide(
+            triple_grad, out_grad, self.width, self.padded, self.qkv_cols, self.out_cols, self.cols, 4
+        )
+        final, summed, tokens = end_exchange(blocks, small, rows, shape, deps)
+        return final[:, : self.qkv_cols], final[:, self.qkv_cols :], summed, tokens
 
     def bias_order(self, bias):
         blocks = bias.reshape(self.cols, self.up_cols)
@@ -807,55 +1324,14 @@
             [grad[:edge].reshape(self.cols, self.main), grad[edge:].reshape(self.cols, self.rest)], axis=1
         ).reshape(-1)
 
-    def pair_total(self, total):
-        place = self.place
-        other = core_swap(place, total)
-        edge = self.cols * self.main
-
-        def pick(d):
-            shard = (place.quarter ^ d) * place.parts + place.part
-            out = []
-            for start, size in ((0, self.main), (edge, self.rest)):
-                for value in (total, other):
-                    out.append(lax.dynamic_slice_in_dim(value, start + shard * size, size, 1))
-            return jnp.concatenate(out, axis=1).astype(jnp.float32)
-
-        final = column_scatter(place, pick)
+    def pair_final(self, parts):
+        final = jnp.sum(parts.astype(jnp.float32), axis=0)
         main, rest = self.main, self.rest
         own = jnp.concatenate([final[:, :main], final[:, 2 * main : 2 * main + rest]], axis=1)
         far = jnp.concatenate([final[:, main : 2 * main], final[:, 2 * main + rest :]], axis=1)
         up = jnp.where(self.role == 0, own, far)
         down = jnp.where(self.role == 0, far, own)
         return up, down.T
-
-    def first_pieces(self, triple_grad, out_grad):
-        padded, rows = self.padded, self.rows
-        low = triple_grad[:, : 2 * padded]
-        high = jnp.concatenate([triple_grad[:, 2 * padded :], out_grad], axis=1)
-        mine = jnp.where(self.role == 0, low, high)
-        theirs = jnp.where(self.role == 0, high, low)
-        me = lax.axis_index("row")
-        cut = lambda value: [
-            lax.dynamic_slice_in_dim(value, (me ^ d) * rows, rows, 0) for d in range(4)
-        ]
-        return cut(mine), cut(theirs)
-
-    def first_total(self, total):
-        place, padded, width = self.place, self.padded, self.width
-        other = core_swap(place, total)
-        low = jnp.where(self.role == 0, total, other).reshape(self.rows, 2, padded)
-        high = jnp.where(self.role == 0, other, total).reshape(self.rows, 2, padded)
-        four = jnp.concatenate([low, high], axis=1)[:, :, :width]
-        qkv = four[:, :3].reshape(self.rows, self.cols, self.qkv_cols)
-        out = four[:, 3].reshape(self.rows, self.cols, self.out_cols)
-        blocks = jnp.concatenate([qkv, out], axis=2).transpose(1, 0, 2)
-
-        def pick(d):
-            shard = (place.quarter ^ d) * place.parts + place.part
-            return lax.dynamic_index_in_dim(blocks, shard, 0, keepdims=False).astype(jnp.float32)
-
-        final = column_scatter(place, pick)
-        return final[:, : self.qkv_cols], final[:, self.qkv_cols :]
 
 
 class PlainWeights:
@@ -868,18 +1344,31 @@
             width, 3 * padded
         )
         self.out = jnp.pad(out, ((0, pad), (0, pad)))
-        self.mine = [plain_gather(w_up)]
-        self.theirs = [plain_gather(w_down.T)]
+        self.rows, self.cols, self.up_cols = w_qkv.shape[0], place.columns, w_up.shape[1]
+        self.main = self.up_cols // 256 * 256
+        self.rest = self.up_cols - self.main
+        full = lax.all_gather(pack_pair(w_up, w_down), BOTH, axis=0, tiled=False)
+        full = full.reshape(lax.axis_size("row"), self.cols, self.rows, 2 * self.up_cols)
+        self.pair = full.transpose(1, 0, 2, 3).reshape(1, self.cols, width, 2 * self.up_cols)
         self.scalars = jnp.zeros((2,), jnp.int32)
 
     def bias_order(self, bias):
-        return bias
+        blocks = bias.reshape(self.cols, self.up_cols)
+        return jnp.concatenate([blocks[:, : self.main].reshape(-1), blocks[:, self.main :].reshape(-1)])
 
     def bias_back(self, grad):
-        return grad
+        edge = self.cols * self.main
+        return jnp.concatenate(
+            [grad[:edge].reshape(self.cols, self.main), grad[edge:].reshape(self.cols, self.rest)], axis=1
+        ).reshape(-1)
+
+    def natural(self, grad):
+        edge = self.cols * self.main
+        cut = lambda value: value.reshape(grad.shape[0], self.cols, -1)
+        return jnp.concatenate([cut(grad[:, :edge]), cut(grad[:, edge:])], axis=2).reshape(grad.shape)
 
     def scatter_pair(self, mine, theirs):
-        return plain_scatter(mine), plain_scatter(theirs).T
+        return plain_scatter(self.natural(mine)), plain_scatter(self.natural(theirs)).T
 
     def scatter_first(self, triple_grad, out_grad):
         width, padded = self.width, self.padded
@@ -907,14 +1396,19 @@
     f32, bf16 = jnp.float32, jnp.bfloat16
 
     quick = lax.axis_size("row") == 4 and parts == 2 and w_qkv.shape[0] == 272
-    weights = (QuickWeights if quick else PlainWeights)(place, w_qkv, w_out, w_up, w_down, padded)
+    if quick:
+        weights = QuickWeights(place, w_qkv, w_out, w_up, w_down, padded)
+        rows_low = weights.start(w_qkv, w_out, block_input)
+    else:
+        weights = PlainWeights(place, w_qkv, w_out, w_up, w_down, padded)
+        rows_low = place.to_tree(place.tree_sources(place.swap_quarters(block_input)))
+    rows_in = rows_low.astype(f32)
 
     own_ids = lax.dynamic_index_in_dim(paths[0], place.quarter, 0, keepdims=False)
     parent_ids = lax.dynamic_index_in_dim(paths[1], place.quarter, 0, keepdims=False)
     mask_trunk, mask_group = place.masks(own_ids, parent_ids)
 
-    rows_in = place.to_tree(place.to_tree_sources(block_input)).astype(f32)
-    seed_rows = place.to_tree(place.to_tree_sources(cotangent))
+    seed_moved = place.swap_quarters(cotangent)
 
     q_scale = HEAD_DIM**-0.5 * LOG2E
     triple_bias = jnp.concatenate(
@@ -927,44 +1421,27 @@
     others = jnp.concatenate(
         [lax.ppermute(shared, "col", place.part_perm(e)) for e in range(1, parts)], axis=0
     )
-    forward_cuts, backward_cuts = cuts_of(pairs, 3), cuts_of(pairs, 4)
-    mixed, lse = [], []
-    for start, stop in forward_cuts:
-        one, two = attention_forward(
-            parts, heads, triple, others, mask_trunk, mask_group, start, stop
-        )
-        mixed.append(one)
-        lse.append(two)
-    mixed, lse = jnp.concatenate(mixed, axis=1), jnp.concatenate(lse, axis=1)
-    out_weight = weights.out[:, :width]
-    attended = (dot_nn(mixed, out_weight) + out_bias).astype(bf16)
-    middle = rows_in + attended.astype(f32)
-    second = layer_norm(middle, ln2_gain, ln2_bias).astype(bf16)
-    seed = seed_rows.astype(f32)
+    mixed, lse = attention_forward(parts, heads, triple, others, mask_trunk, mask_group, 0, pairs)
+    seed_rows = place.to_tree(place.tree_sources(after(seed_moved, mixed)))
+    middle, second = project_out(mixed, rows_low, weights.out, out_bias, ln2_gain, ln2_bias)
     outs = 4 if quick else 1
     lowered, second_grad, up_bias_grad, *pair_grads = feed_forward(
-        weights.scalars, weights.mine, weights.theirs, second, seed_rows, weights.bias_order(up_bias), outs
+        weights.scalars, weights.pair, second, seed_rows, weights.bias_order(up_bias), outs
     )
     pair_mine, pair_theirs = pair_grads[:outs], pair_grads[outs:]
     up_bias_grad = weights.bias_back(up_bias_grad.reshape(-1))
-    result = (middle + lowered + down_bias).astype(bf16)
-
-    down_bias_grad = jnp.sum(seed, axis=0)
-    norm_grad, gain_two, shift_two = jax.vjp(layer_norm, middle, ln2_gain, ln2_bias)[1](second_grad)
-    middle_grad = seed + norm_grad
-    attended_grad = middle_grad.astype(bf16)
-    out_bias_grad = jnp.sum(attended_grad.astype(f32), axis=0)
-    out_weight_grad = dot_tn(mixed, attended_grad)[:width].astype(bf16)
-    mixed_grad = dot_nt(attended_grad, out_weight).astype(bf16)
-    early = sum_all([out_bias_grad, gain_two, shift_two, up_bias_grad, down_bias_grad])
+    result, middle_grad, mixed_grad, sums, out_padded = middle_back(
+        second_grad, lowered, middle, seed_rows, mixed, weights.out, ln2_gain, down_bias
+    )
+    out_bias_grad, gain_two, shift_two, down_bias_grad = sums[0], sums[1], sums[2], sums[3]
 
     turned = jnp.swapaxes(mask_trunk, 1, 2), jnp.swapaxes(mask_group, 1, 2)
     result_sources = place.from_tree_sources(result)
     if quick:
         pair_swapped = {d: core_swap(place, pair_theirs[d]) for d in (3, 1, 2, 0)}
         sums = far_sums(pair_mine, pair_swapped)
-    grads = []
-    for index, (start, stop) in enumerate(backward_cuts):
+    grads = ()
+    for index, (start, stop) in enumerate(cuts_of(pairs, 4)):
         deps = ()
         if quick and index == 0:
             deps = sums
@@ -980,44 +1457,58 @@
         if quick and index == 3:
             total = row_total(pair_mine, pair_swapped, received, last)
             deps = (total,)
-        grads.append(
-            attention_backward(
-                parts, heads, triple, others, mixed, mixed_grad, lse, *turned, start, stop, deps
-            )
+        grads = attention_backward(
+            parts, heads, triple, others, mixed, mixed_grad, lse, *turned, start, stop, grads, deps
         )
+    deps = ()
     if quick:
-        up_grad, down_grad = weights.pair_total(total)
+        blocks = pair_blocks(
+            place.part.reshape(1).astype(jnp.int32), total, core_swap(place, total), weights.main, weights.rest
+        )
+        pair_parts = place.swap_quarters(blocks)
+        deps = (blocks,)
     else:
         up_grad, down_grad = weights.scatter_pair(pair_mine[0], pair_theirs[0])
-    dq, dk, dv, dko, dvo = (jnp.concatenate(part, axis=1) for part in zip(*grads))
-    both = jnp.concatenate([dko, dvo], axis=1)
-    key_value = jnp.concatenate([dk, dv], axis=1)
-    for e in range(1, parts):
-        block = both[(e - 1) * own_trunk : e * own_trunk]
-        key_value = key_value.at[:own_trunk].add(
-            lax.ppermute(block, "col", place.part_perm(e)).astype(f32)
+    dq, dk, dv, dko, dvo = grads
+    other_k, other_v = (
+        jnp.concatenate(
+            [
+                lax.ppermute(part[(e - 1) * own_trunk : e * own_trunk], "col", place.part_perm(e))
+                for e in range(1, parts)
+            ],
+            axis=0,
         )
-    triple_grad = jnp.concatenate([dq, key_value.astype(bf16)], axis=1)
-    first_grad = dot_nt(triple_grad, weights.triple)
-    q_bias_grad = jnp.sum(triple_grad[:, :width].astype(f32), axis=0)
-    v_bias_grad = jnp.sum(triple_grad[:, 2 * padded : 2 * padded + width].astype(f32), axis=0)
-    norm_grad, gain_one, shift_one = jax.vjp(layer_norm, rows_in, ln1_gain, ln1_bias)[1](first_grad)
-    input_grad = (middle_grad + norm_grad).astype(bf16)
-    input_grad_out = place.swap_quarters(place.from_tree_parts(place.from_tree_sources(input_grad)))
+        for part in (dko, dvo)
+    )
+    triple_grad, triple_sums = finish_gradients(own_trunk, dq, dk, dv, other_k, other_v, deps)
+    q_bias_grad = triple_sums[0, :width]
+    v_bias_grad = triple_sums[0, 2 * padded : 2 * padded + width]
+    input_grad, sums = first_back(triple_grad, rows_low, middle_grad, weights.triple, ln1_gain)
+    gain_one, shift_one = sums[0], sums[1]
     triple_weight_grad = dot_tn(first, triple_grad).astype(bf16)
-    out_padded = jnp.pad(out_weight_grad, ((0, 0), (0, pad)))
+    small = [
+        gain_one, shift_one, q_bias_grad, v_bias_grad, out_bias_grad, gain_two, shift_two, up_bias_grad,
+        down_bias_grad,
+    ]
     if quick:
-        mine, theirs = weights.first_pieces(triple_weight_grad, out_padded)
-        swapped = {d: core_swap(place, theirs[d]) for d in (3, 1, 2, 0)}
-        received = far_sends(far_sums(mine, swapped))
-        last = near_sends(near_sums(mine, swapped, received))
-        qkv_grad, out_grad = weights.first_total(row_total(mine, swapped, received, last))
+        up_grad, down_grad = weights.pair_final(pair_parts)
+        flat = jnp.concatenate(small)
+        flat = jnp.pad(flat, (0, -flat.shape[0] % 1024)).reshape(-1, 128)
+        qkv_grad, out_grad, flat, input_grad_out = weights.end(
+            triple_weight_grad, out_padded, flat, input_grad, block_input.shape, (up_grad, down_grad)
+        )
+        edges = np.cumsum([0] + [v.shape[0] for v in small])
+        flat = flat.reshape(-1)
+        small = [flat[low:high] for low, high in zip(edges[:-1], edges[1:])]
     else:
         qkv_grad, out_grad = weights.scatter_first(triple_weight_grad, out_padded)
-    late = sum_all([gain_one, shift_one, q_bias_grad, v_bias_grad])
+        small = lax.psum(small, BOTH)
+        input_grad_out = place.swap_quarters(
+            place.from_tree_parts(place.from_tree_sources(input_grad))
+        )
     return (
-        result_out, input_grad_out, late[0], late[1], qkv_grad, late[2], late[3],
-        out_grad, early[0], early[1], early[2], up_grad, early[3], down_grad, early[4],
+        result_out, input_grad_out, small[0], small[1], qkv_grad, small[2], small[3],
+        out_grad, small[4], small[5], small[6], up_grad, small[7], down_grad, small[8],
     )
 
 

time: 1160 us -> 859 us (0.74)
  waiting for transfers between devices: 319 us -> 41.7 us
  Pallas kernels: 356 us -> 629 us
  local copies, waits for them, and re-layouts: 212 us -> 68.8 us
  other arithmetic: 123 us -> 34.9 us
  starting transfers between devices: 69 us -> 28.8 us
  matrix products: 60.7 us -> 31.9 us
    pallas_call x2 -> x11, Pallas kernels: 139 us -> 420 us  [the longest x1 128 us: feed_forward(): pl.pallas_call(partial(ffn_kernel, outs, chunk), grid_spec=pltpu.Prefetch...]
    ppermute x19 -> x3, waiting for transfers between devices: 144 us -> 0.01 us  [the longest x2 0.01 us: local(): lax.ppermute(part[(e - 1) * own_trunk:e * own_trunk], 'col', place.part_p...]
    ppermute x20 -> x6, waiting for transfers between devices: 73.1 us -> 0.02 us  [across(): lax.ppermute(value, 'row', [(r, r ^ shift) for r in range(lax.axis_size('...]
    all_gather x2 -> x1, waiting for transfers between devices: 70 us -> 0.01 us  [start(): pair = lax.all_gather(pack, BOTH, axis=0, tiled=False)]
    unnamed x258 -> x113, local copies, waits for them, and re-layouts: 68 us -> 23.9 us
    slice x26 -> x14, local copies, waits for them, and re-layouts: 38.9 us -> 6.3 us  [the longest x2 1.38 us: local(): small = [flat[low:high] for low, high in zip(edges[:-1], edges[1:])]]
    reduce_sum x7 -> x1, other arithmetic: 28.7 us -> 2.24 us  [pair_final(): final = jnp.sum(parts.astype(jnp.float32), axis=0)]
    dot_general x2 -> x0, matrix products: 24.1 us -> none  [dot_nt(): lax.dot_general(a, b, (((1,), (1,)), ((), ())), preferred_element_type=jn...]
  transfers between devices with their start and end apart: 68 -> 20, of which waited for: 19 -> 1; matrix products, arithmetic and copies ran while one was open for 29% -> 12% of each run, Pallas kernels for 20% -> 35%
where the time goes in v2:
time: 859 us; the launch traced here: 850 us
  Pallas kernels  629 us (73%)
  local copies, waits for them, and re-layouts  68.8 us (8%)
  waiting for transfers between devices  41.7 us (5%)
  other arithmetic  34.9 us (4%)
  matrix products  31.9 us (4%)
  starting transfers between devices  28.8 us (3%)
  between operations  15.4 us (2%)
    pallas_call x4, Pallas kernels, attention_backward(): pl.pallas_call(partial(bwd_kernel, parts, heads, start, len(deps)), grid=...  133 us
    pallas_call x1, Pallas kernels, feed_forward(): pl.pallas_call(partial(ffn_kernel, outs, chunk), grid_spec=pltpu.Prefetch...  128 us
    pallas_call x1, Pallas kernels, end_exchange(): pl.pallas_call(partial(end_kernel, grain), in_specs=[HOLD, pl.BlockSpec(m...  107 us
    pallas_call x1, Pallas kernels, start_exchange(): pl.pallas_call(partial(start_kernel, grain), in_specs=[HOLD] * 3, out_spe...  99.2 us
    pallas_call x1, Pallas kernels, attention_forward(): pl.pallas_call(partial(fwd_kernel, parts, heads, start, len(deps)), grid=...  67.9 us
    pallas_call x3, Pallas kernels, by_rows(): pl.pallas_call(kernel, grid=(5,), in_specs=[block(v.shape[1]) for v in ch...  52.9 us
    all_to_all x3, waiting for transfers between devices, swap_quarters(): lax.all_to_all(value, 'col', 0, 0, axis_index_groups=groups, tiled=True)  41.7 us
    unnamed x113, local copies, waits for them, and re-layouts  23.9 us
  transfers between devices with their start and end apart: 20, of which 1 were waited for; matrix products, arithmetic and copies ran while one was open for 12% of the time, Pallas kernels for 35%

profile of v2, /device:TPU:8, one launch (start us, length us, event | category | flops | bytes accessed | tf_op | source)
XLA Modules:
  0.0 850.0 jit_solution(18345723826018468300)
XLA Ops:
  11.0 1.8 pad_maximum_fusion.4.pack
  13.8 99.2 %start_exchange.1 = (bf16[2,4,4,272,544]{4,3,2,1,0:T(8,128)(2,1)}, bf16[1280,1088]{1,0:T(8,128)(2,1)}, bf16[272,1088]{1,0:T(8,128)(2,1)}) custom-call(bf16[272,544]{1,0:T(8,128)(2,1)} %pad_maximum_fusion.4.pack, bf16[272,1088]{1,0:T(8,128)(2,1)} %concatenate.37.later_pack, bf16[4,320,1088]{2,1,0:T(8,128)(2,1)} %value.1), custom_call_target="tpu_custom_call" | custom-call | flops 99999997952 | tf_op jit(solution)/shard_map/start_exchange/pallas_call | solution.py:567
  113.1 2.5 convert_reduce_fusion
  116.7 9.0 %assemble_weights.1 = (bf16[1088,3456]{1,0:T(8,128)(2,1)}, bf16[1152,1152]{1,0:T(8,128)(2,1)S(1)}) custom-call(bf16[2,4,4,272,544]{4,3,2,1,0:T(8,128)(2,1)} %get-tuple-element.69.full), custom_call_target="tpu_custom_call" | custom-call | flops 12000000000 | tf_op jit(solution)/shard_map/assemble_weights/pallas_call | solution.py:780
  125.8 16.3 %fusion.1.q_ref.k_ref.v_ref = bf16[1280,3456]{1,0:T(8,128)(2,1)S(1)} fusion(bf16[1088,3456]{1,0:T(8,128)(2,1)} %get-tuple-element.70.weight, f32[3456]{0:T(1024)S(1)} %select_maximum_fusion, f32[3456]{0:T(1024)S(1)} %copy-done.50, bf16[1280,1088]{1,0:T(8,128)(2,1)S(1)} %copy-done.15, f32[1088]{0:T(1024)S(1)} %copy-done.47, f32[1088]{0:T(1024)S(1)} %copy-done.36, ...), kind=kOutput, calls=%fused_computation.5 | convolution fusion | flops 9647554560 | bytes 19199488 | tf_op jit(solution)/shard_map/dot_general | solution.py:21
  142.1 1.7 slice.228
  143.7 2.5 copy-done.23
  146.2 5.8 all-to-all-start
  152.6 1.6 fusion.21
  154.2 2.8 copy.75.mg_ref
  159.5 2.5 copy.74.mt_ref
  164.6 67.9 %attention_forward.1 = (bf16[1280,1152]{1,0:T(8,128)(2,1)}, f32[1280,1152]{1,0:T(8,128)}) custom-call(bf16[1280,3456]{1,0:T(8,128)(2,1)} %copy-done.23, bf16[1280,3456]{1,0:T(8,128)(2,1)} %copy-done.23, bf16[1280,3456]{1,0:T(8,128)(2,1)} %copy-done.23, bf16[512,2304]{1,0:T(8,128)(2,1)} %collective-permute-done.ko_ref.vo_ref, ...), custom_call_target="tpu_custom_call" | custom-call | flops 78336000000 | bytes 23040000 | tf_op jit(solution)/shard_map/attention_forward/pallas_call | solution.py:111
  232.5 41.7 %all-to-all-done.refs_0_ = bf16[4,320,1088]{2,1,0:T(8,128)(2,1)S(1)} async-done(((bf16[4,320,1088]{2,1,0:T(8,128)(2,1)}), bf16[4,320,1088]{2,1,0:T(8,128)(2,1)S(1)}, u32[]{:S(2)}, u32[]{:S(2)}) %all-to-all-start) | async-done | bytes 2785312 | tf_op jit(solution)/shard_map/all_to_all | solution.py:1152
  274.1 1.6 copy-done
  275.9 5.4 copy.76
  287.9 10.4 %project_out.1 = (f32[1280,1088]{1,0:T(8,128)}, bf16[1280,1088]{1,0:T(8,128)(2,1)}) custom-call(bf16[1280,1152]{1,0:T(8,128)(2,1)} %get-tuple-element.71.mixed.refs_1_.o_ref, bf16[1280,1088]{1,0:T(8,128)(2,1)} %get-tuple-element.68.rows, bf16[1152,1152]{1,0:T(8,128)(2,1)} %copy-done.11, f32[1,1088]{1,0:T(1,128)} %reshape.570.bias, f32[1,1088]{1,0:T(1,128)} %reshape.571.gain, ...), custom_call_target="tpu_custom_call" | custom-call | flops 12000000000 | tf_op jit(solution)/shard_map/project_out/pallas_call | solution.py:904
  298.4 5.5 copy.77.refs_1_
  303.9 3.1 spread_rows.1.refs_4_.seed
  307.0 1.6 copy-done.3
  308.6 127.8 %feed_forward.1 = (f32[1280,1088]{1,0:T(8,128)}, f32[1280,1088]{1,0:T(8,128)}, f32[1,4352]{1,0:T(1,128)}, bf16[272,4352]{1,0:T(8,128)(2,1)}, bf16[272,4352]{1,0:...) custom-call(s32[6]{0:T(128)} %stack.46.scalars, ...), custom_call_target="tpu_custom_call" | custom-call | flops 145458462720 | bytes 65732608 | tf_op jit(solution)/shard_map/feed_forward/pallas_call | solution.py:423
  438.4 22.3 %middle_back.1 = (bf16[1280,1088]{1,0:T(8,128)(2,1)}, f32[1280,1088]{1,0:T(8,128)}, bf16[1280,1152]{1,0:T(8,128)(2,1)}, f32[4,1088]{1,0:T(4,128)}, bf16[1088,1152]{1,0:T(8,128)(2,1)}) custom-call(f32[1280,1088]{1,0:T(8,128)} %get-tuple-element.74.second_grad, f32[1280,1088]{1,0:T(8,128)} %get-tuple-element.75.lowered, ...), custom_call_target="tpu_custom_call" | custom-call | flops 24999999488 | tf_op jit(solution)/shard_map/middle_back/pallas_call | solution.py:904
  460.7 5.4 copy.78
  466.1 3.0 add_convert_fusion.6.refs_1_
  470.7 2.7 add_convert_fusion.3.refs_0_
  474.8 2.7 add_convert_fusion.2.refs_3_
  478.1 2.8 add_convert_fusion.5.refs_2_
  480.9 31.4 %attention_backward.4 = (bf16[1280,1152]{1,0:T(8,128)(2,1)}, bf16[1280,1152]{1,0:T(8,128)(2,1)}, bf16[1280,1152]{1,0:T(8,128)(2,1)}, bf16[512,1152]{1,0:T(8,128)(2,1)}, bf16[512,1152]{1,0:T(8,128)(2,1)}) custom-call(bf16[1280,3456]{1,0:T(8,128)(2,1)} %copy-done.23, bf16[1280,3456]{1,0:T(8,128)(2,1)} %copy-done.23, bf16[1280,3456]{1,0:T(8,128)(2,1)} %copy-done.23, ...), custom_call_target="tpu_custom_call" | custom-call | flops 31232000000 | bytes 46080000 | tf_op jit(solution)/shard_map/attention_backward/pallas_call | solution.py:259
  513.1 5.5 copy.79.refs_1_
  518.5 4.4 collect_rows.1
  523.0 8.8 %all-to-all-start.1 = ((bf16[4,320,1088]{2,1,0:T(8,128)(2,1)}), bf16[4,320,1088]{2,1,0:T(8,128)(2,1)S(1)}, u32[]{:S(2)}, u32[]{:S(2)}) async-start(bf16[4,320,1088]{2,1,0:T(8,128)(2,1)} %bitcast.16.refs_5_), calls=%async_computation.1 | async-start | bytes 5898240 | tf_op jit(solution)/shard_map/all_to_all | solution.py:1152
  531.8 3.5 add_convert_fusion.4.refs_7_
  536.5 3.2 add_convert_fusion.1.refs_6_
  541.0 31.4 %attention_backward.5 = (bf16[1280,1152]{1,0:T(8,128)(2,1)}, bf16[1280,1152]{1,0:T(8,128)(2,1)}, bf16[1280,1152]{1,0:T(8,128)(2,1)}, bf16[512,1152]{1,0:T(8,128)(2,1)}, bf16[512,1152]{1,0:T(8,128)(2,1)}) custom-call(bf16[1280,3456]{1,0:T(8,128)(2,1)} %copy-done.23, ...), custom_call_target="tpu_custom_call", output_to_operand_aliasing={{0}: (10, {}), {1}: (11, {}), {2}: (12, {}), {3}: (13, {}),... | custom-call | flops 31232000000 | bytes 46080000 | tf_op jit(solution)/shard_map/attention_backward/pallas_call | solution.py:259
  572.4 45.3 %attention_backward.6 = (bf16[1280,1152]{1,0:T(8,128)(2,1)}, bf16[1280,1152]{1,0:T(8,128)(2,1)}, bf16[1280,1152]{1,0:T(8,128)(2,1)}, bf16[512,1152]{1,0:T(8,128)(2,1)}, bf16[512,1152]{1,0:T(8,128)(2,1)}) custom-call(bf16[1280,3456]{1,0:T(8,128)(2,1)} %copy-done.23, ...), custom_call_target="tpu_custom_call", output_to_operand_aliasing={{0}: (10, {}), {1}: (11, {}), {2}: (12, {}), {3}: (13, {}),... | custom-call | flops 46848000000 | bytes 46080000 | tf_op jit(solution)/shard_map/attention_backward/pallas_call | solution.py:259
  617.8 4.0 add_convert_fusion.refs_5_.total.total_tail
  621.8 24.7 %attention_backward.7 = (bf16[1280,1152]{1,0:T(8,128)(2,1)}, bf16[1280,1152]{1,0:T(8,128)(2,1)}, bf16[1280,1152]{1,0:T(8,128)(2,1)}, bf16[512,1152]{1,0:T(8,128)(2,1)}, bf16[512,1152]{1,0:T(8,128)(2,1)}) custom-call(bf16[1280,3456]{1,0:T(8,128)(2,1)} %copy-done.23, ...), custom_call_target="tpu_custom_call", output_to_operand_aliasing={{0}: (10, {}), {1}: (11, {}), {2}: (12, {}), {3}: (13, {}),... | custom-call | flops 31232000000 | bytes 46080000 | tf_op jit(solution)/shard_map/attention_backward/pallas_call | solution.py:259
  648.0 1.6 copy-done.17
  649.6 4.3 pair_blocks.1.refs_0_
  653.9 5.5 all-to-all-start.2
  659.4 11.3 %finish_gradients.1 = (bf16[1280,3456]{1,0:T(8,128)(2,1)}, f32[1,3456]{1,0:T(1,128)S(1)}) custom-call(bf16[1280,1152]{1,0:T(8,128)(2,1)} %get-tuple-element.103.dq, bf16[1280,1152]{1,0:T(8,128)(2,1)} %get-tuple-element.104.dk, bf16[1280,1152]{1,0:T(8,128)(2,1)} %get-tuple-element.105.dv, bf16[512,1152]{1,0:T(8,128)(2,1)} %collective-permute-done.13.other_k, ...), custom_call_target="tpu_custom_call" | custom-call | flops 8000000000 | tf_op jit(solution)/shard_map/finish_gradients/pallas_call | solution.py:857
  670.7 20.2 %first_back.1 = (bf16[1280,1088]{1,0:T(8,128)(2,1)}, f32[2,1088]{1,0:T(2,128)}) custom-call(bf16[1280,3456]{1,0:T(8,128)(2,1)} %get-tuple-element.108.triple_grad, bf16[1280,1088]{1,0:T(8,128)(2,1)} %get-tuple-element.68.rows, f32[1280,1088]{1,0:T(8,128)} %get-tuple-element.110.middle_grad, bf16[1088,3456]{1,0:T(8,128)(2,1)} %get-tuple-element.70.weight, ...), custom_call_target="tpu_custom_call" | custom-call | flops 24999999488 | tf_op jit(solution)/shard_map/first_back/pallas_call | solution.py:904
  691.9 15.6 %convolution_convert_fusion.triple = bf16[1088,3456]{1,0:T(8,128)(2,1)} fusion(bf16[1280,3456]{1,0:T(8,128)(2,1)} %get-tuple-element.108.triple_grad, bf16[1280,1088]{1,0:T(8,128)(2,1)S(1)} %copy-done.16, f32[1088]{0:T(1024)S(1)} %copy-done.48, f32[1088]{0:T(1024)S(1)} %copy-done.37, f32[1280]{0:T(1024)S(1)} %copy-done.39, f32[1280]{0:T(1024)S(1)} %copy-done.26), kind=kOutput, calls=%fused_computation.6 | convolution fusion | flops 9638043648 | bytes 19171840 | tf_op jit(solution)/shard_map/dot_general | solution.py:29
  707.5 9.1 %divide_gradients.1.grads = bf16[2,4,4,272,544]{4,3,2,1,0:T(8,128)(2,1)} custom-call(bf16[1088,3456]{1,0:T(8,128)(2,1)} %convolution_convert_fusion.triple, bf16[1088,1152]{1,0:T(8,128)(2,1)S(1)} %copy-done.10), custom_call_target="tpu_custom_call" | custom-call | flops 12000000000 | tf_op jit(solution)/shard_map/divide_gradients/pallas_call | solution.py:811
  716.6 2.2 convert_reduce_fusion.1
  722.4 2.1 copy-done.12
  724.5 106.9 %end_exchange.1 = (f32[272,544]{1,0:T(8,128)S(1)}, f32[104,128]{1,0:T(8,128)S(1)}, bf16[4,320,1088]{2,1,0:T(8,128)(2,1)S(1)}) custom-call(bf16[2,4,4,272,544]{4,3,2,1,0:T(8,128)(2,1)} %divide_gradients.1.grads, f32[104,128]{1,0:T(8,128)S(1)} %pad_bitcast_fusion.small, bf16[1280,1088]{1,0:T(8,128)(2,1)S(1)} %copy-done.12, f32[272,544]{1,0:T(8,128)S(1)} %copy.84.refs_0_, ...), custom_call_target="tpu_custom_call" | custom-call | flops 99999997952 | tf_op jit(solution)/shard_map/end_exchange/pallas_call | solution.py:717
  837.3 3.8 copy.111
  841.1 1.6 copy.112
  (209 shorter events, 39.0 us)
Async XLA Ops:
  7.2 301.4 %all-gather.3.cloned.1.call-start = ((), (), s32[]{:S(2)}) async-start(), calls=%async_computation.3 | async-start | bytes 20680704 | tf_op jit(solution)/shard_map/all_gather | solution.py:1305
  13.8 99.2 %copy-start.31 = (f32[1088]{0:T(1024)S(1)}, f32[1088]{0:T(1024)}, u32[]{:S(2)}) copy-start(f32[1088]{0:T(1024)} %param.30) | copy-start | bytes 13060
  13.8 99.3 %copy-start.30 = (f32[1088]{0:T(1024)S(1)}, f32[1088]{0:T(1024)}, u32[]{:S(2)}) copy-start(f32[1088]{0:T(1024)} %param.31) | copy-start | bytes 13060
  115.7 10.0 %copy-start.25 = (f32[1280]{0:T(1024)}, f32[1280]{0:T(1024)S(1)}, u32[]{:S(2)}) copy-start(f32[1280]{0:T(1024)S(1)} %broadcast_multiply_fusion.1) | copy-start | bytes 15364
  116.7 9.0 %copy-start.38 = (f32[1280]{0:T(1024)}, f32[1280]{0:T(1024)S(1)}, u32[]{:S(2)}) copy-start(f32[1280]{0:T(1024)S(1)} %add_rsqrt_fusion) | copy-start | bytes 15364
  116.7 9.0 %copy-start.36 = (f32[1088]{0:T(1024)S(1)}, f32[1088]{0:T(1024)}, u32[]{:S(2)}) copy-start(f32[1088]{0:T(1024)} %param.27) | copy-start | bytes 13060
  116.7 9.0 %copy-start.47 = (f32[1088]{0:T(1024)S(1)}, f32[1088]{0:T(1024)}, u32[]{:S(2)}) copy-start(f32[1088]{0:T(1024)} %param.28) | copy-start | bytes 13060
  116.7 9.0 %copy-start.50 = (f32[3456]{0:T(1024)S(1)}, f32[3456]{0:T(1024)}, u32[]{:S(2)}) copy-start(f32[3456]{0:T(1024)} %constant.174.clone.1) | copy-start | bytes 41476
  125.7 16.3 %copy-start.11 = (bf16[1152,1152]{1,0:T(8,128)(2,1)}, bf16[1152,1152]{1,0:T(8,128)(2,1)S(1)}, u32[]{:S(2)}) copy-start(bf16[1152,1152]{1,0:T(8,128)(2,1)S(1)} %get-tuple-element.72.weight) | copy-start | bytes 7962628
  146.2 15.8 %collective-permute-start = (bf16[512,2304]{1,0:T(8,128)(2,1)}, bf16[512,2304]{1,0:T(8,128)(2,1)}, u32[]{:S(2)}, u32[]{:S(2)}) collective-permute-start(bf16[512,2304]{1,0:T(8,128)(2,1)} %slice.228), channel_id=1, source_target_pairs={{0,1},{1,0},{2,3},{3,2},{4,5},{5,4},{6,7},{7,6},{8,9},{9,8},{10,11... | collective-permute-start | bytes 7077896 | tf_op jit(solution)/shard_map/ppermute | solution.py:1422
  146.2 127.9 %all-to-all-start = ((bf16[4,320,1088]{2,1,0:T(8,128)(2,1)}), bf16[4,320,1088]{2,1,0:T(8,128)(2,1)S(1)}, u32[]{:S(2)}, u32[]{:S(2)}) async-start(bf16[4,320,1088]{2,1,0:T(8,128)(2,1)} %param.40), calls=%async_computation | async-start | bytes 5898240 | tf_op jit(solution)/shard_map/all_to_all | solution.py:1152
  275.8 8.1 copy-start.44
  275.8 8.1 copy-start.14
  275.8 8.8 %copy-start.13 = (s32[40]{0:T(128)S(1)}, s32[40]{0:T(128)}, u32[]{:S(2)}) copy-start(s32[40]{0:T(128)} %constant.192.clone) | copy-start | bytes 484
  275.9 10.0 %copy-start.49 = (s32[2,40]{1,0:T(2,128)S(1)}, s32[2,40]{1,0:T(2,128)}, u32[]{:S(2)}) copy-start(s32[2,40]{1,0:T(2,128)} %constant.185.clone) | copy-start | bytes 964
  275.9 10.0 %copy-start.41 = (s32[40]{0:T(128)S(1)}, s32[40]{0:T(128)}, u32[]{:S(2)}) copy-start(s32[40]{0:T(128)} %constant.186.clone) | copy-start | bytes 484
  275.9 10.0 %copy-start.42 = (s32[40]{0:T(128)S(1)}, s32[40]{0:T(128)}, u32[]{:S(2)}) copy-start(s32[40]{0:T(128)} %constant.187.clone) | copy-start | bytes 484
  275.9 10.0 %copy-start.43 = (s32[40]{0:T(128)S(1)}, s32[40]{0:T(128)}, u32[]{:S(2)}) copy-start(s32[40]{0:T(128)} %constant.188.clone) | copy-start | bytes 484
  281.3 17.0 %collective-permute-start.1 = (bf16[1280,1088]{0,1:T(8,128)(2,1)}, bf16[1280,1088]{0,1:T(8,128)(2,1)}, u32[]{:S(2)}, u32[]{:S(2)}) collective-permute-start(bf16[1280,1088]{0,1:T(8,128)(2,1)} %copy.76), channel_id=1, source_target_pairs={{0,1},{1,0},{2,3},{3,2},{4,5},{5,4},{6,7},{7,6},{8,9},{9,8},{10,11... | collective-permute-start | bytes 8355848 | tf_op jit(solution)/shard_map/ppermute | solution.py:1156
  308.6 127.9 %copy-start.40 = (s32[20]{0:T(128)S(1)}, s32[20]{0:T(128)}, u32[]{:S(2)}) copy-start(s32[20]{0:T(128)} %gather_fusion.1) | copy-start | bytes 244
  308.6 127.9 %copy-start.46 = (s32[20,1]{0,1:T(1,128)S(1)}, s32[20,1]{0,1:T(1,128)}, u32[]{:S(2)}) copy-start(s32[20,1]{0,1:T(1,128)} %xor_bitcast_fusion) | copy-start | bytes 244
  308.6 127.9 %copy-start.35 = (f32[1088]{0:T(1024)S(1)}, f32[1088]{0:T(1024)}, u32[]{:S(2)}) copy-start(f32[1088]{0:T(1024)} %param.39) | copy-start | bytes 13060
  436.4 29.7 %collective-permute-start.3 = (bf16[272,4352]{1,0:T(8,128)(2,1)}, bf16[272,4352]{1,0:T(8,128)(2,1)}, u32[]{:S(2)}, u32[]{:S(2)}) collective-permute-start(bf16[272,4352]{1,0:T(8,128)(2,1)} %get-tuple-element.81), channel_id=1, source_target_pairs={{0,1},{1,0},{2,3},{3,2},{4,5},{5,4},{6,7},{7,6},{8,9},{9,8},{10,11... | collective-permute-start | bytes 7102472 | tf_op jit(solution)/shard_map/ppermute | solution.py:1249
  437.4 36.0 %collective-permute-start.5 = (bf16[272,4352]{1,0:T(8,128)(2,1)}, bf16[272,4352]{1,0:T(8,128)(2,1)}, u32[]{:S(2)}, u32[]{:S(2)}) collective-permute-start(bf16[272,4352]{1,0:T(8,128)(2,1)} %get-tuple-element.85), channel_id=1, source_target_pairs={{0,1},{1,0},{2,3},{3,2},{4,5},{5,4},{6,7},{7,6},{8,9},{9,8},{10,11... | collective-permute-start | bytes 7102472 | tf_op jit(solution)/shard_map/ppermute | solution.py:1249
  437.9 39.7 %collective-permute-start.4 = (bf16[272,4352]{1,0:T(8,128)(2,1)}, bf16[272,4352]{1,0:T(8,128)(2,1)S(1)}, u32[]{:S(2)}, u32[]{:S(2)}) collective-permute-start(bf16[272,4352]{1,0:T(8,128)(2,1)} %get-tuple-element.83), channel_id=1, source_target_pairs={{0,1},{1,0},{2,3},{3,2},{4,5},{5,4},{6,7},{7,6},{8,9},{9,8},{10,11... | collective-permute-start | bytes 7102472 | tf_op jit(solution)/shard_map/ppermute | solution.py:1249
  438.0 179.8 %collective-permute-start.8 = (bf16[272,4352]{1,0:T(8,128)(2,1)}, bf16[272,4352]{1,0:T(8,128)(2,1)}, u32[]{:S(2)}, u32[]{:S(2)}) collective-permute-start(bf16[272,4352]{1,0:T(8,128)(2,1)} %get-tuple-element.102), channel_id=1, source_target_pairs={{0,1},{1,0},{2,3},{3,2},{4,5},{5,4},{6,7},{7,6},{8,9},{9,8},{10,11... | collective-permute-start | bytes 7102472 | tf_op jit(solution)/shard_map/ppermute | solution.py:1249
  466.0 46.3 %collective-permute-start.2 = (bf16[1280,1088]{0,1:T(8,128)(2,1)}, bf16[1280,1088]{0,1:T(8,128)(2,1)}, u32[]{:S(2)}, u32[]{:S(2)}) collective-permute-start(bf16[1280,1088]{0,1:T(8,128)(2,1)} %copy.78), channel_id=1, source_target_pairs={{0,1},{1,0},{2,3},{3,2},{4,5},{5,4},{6,7},{7,6},{8,9},{9,8},{10,11... | collective-permute-start | bytes 8355848 | tf_op jit(solution)/shard_map/ppermute | solution.py:1170
  469.1 62.7 %collective-permute-start.7 = (bf16[128,4352]{1,0:T(8,128)(2,1)}, bf16[128,4352]{1,0:T(8,128)(2,1)}, u32[]{:S(2)}, u32[]{:S(2)}) collective-permute-start(bf16[128,4352]{1,0:T(8,128)(2,1)} %add_convert_fusion.6.refs_1_), channel_id=1, source_target_pairs={{0,8},{8,0},{16,24},{24,16},{1,9},{9,1},{17,25},{25,17},{2,10},{10... | collective-permute-start | bytes 3342344 | tf_op jit(solution)/shard_map/ppermute | solution.py:1233
  473.4 63.1 %collective-permute-start.6 = (bf16[144,4352]{1,0:T(8,128)(2,1)}, bf16[144,4352]{1,0:T(8,128)(2,1)}, u32[]{:S(2)}, u32[]{:S(2)}) collective-permute-start(bf16[144,4352]{1,0:T(8,128)(2,1)} %add_convert_fusion.3.refs_0_), channel_id=1, source_target_pairs={{0,16},{8,24},{16,0},{24,8},{1,17},{9,25},{17,1},{25,9},{2,18},{10... | collective-permute-start | bytes 3760136 | tf_op jit(solution)/shard_map/ppermute | solution.py:1233
  477.5 140.2 %collective-permute-start.11 = (bf16[144,4352]{1,0:T(8,128)(2,1)}, bf16[144,4352]{1,0:T(8,128)(2,1)}, u32[]{:S(2)}, u32[]{:S(2)}) collective-permute-start(bf16[144,4352]{1,0:T(8,128)(2,1)} %add_convert_fusion.2.refs_3_), channel_id=1, source_target_pairs={{0,16},{8,24},{16,0},{24,8},{1,17},{9,25},{17,1},{25,9},{2,18},{10... | collective-permute-start | bytes 3760136 | tf_op jit(solution)/shard_map/ppermute | solution.py:1233
  512.3 105.5 %collective-permute-start.10 = (bf16[128,4352]{1,0:T(8,128)(2,1)}, bf16[128,4352]{1,0:T(8,128)(2,1)}, u32[]{:S(2)}, u32[]{:S(2)}) collective-permute-start(bf16[128,4352]{1,0:T(8,128)(2,1)} %add_convert_fusion.5.refs_2_), channel_id=1, source_target_pairs={{0,8},{8,0},{16,24},{24,16},{1,9},{9,1},{17,25},{25,17},{2,10},{10... | collective-permute-start | bytes 3342344 | tf_op jit(solution)/shard_map/ppermute | solution.py:1233
  523.0 125.1 %all-to-all-start.1 = ((bf16[4,320,1088]{2,1,0:T(8,128)(2,1)}), bf16[4,320,1088]{2,1,0:T(8,128)(2,1)S(1)}, u32[]{:S(2)}, u32[]{:S(2)}) async-start(bf16[4,320,1088]{2,1,0:T(8,128)(2,1)} %bitcast.16.refs_5_), calls=%async_computation.1 | async-start | bytes 5898240 | tf_op jit(solution)/shard_map/all_to_all | solution.py:1152
  535.3 82.4 %collective-permute-start.12 = (bf16[128,4352]{1,0:T(8,128)(2,1)}, bf16[128,4352]{1,0:T(8,128)(2,1)S(1)}, u32[]{:S(2)}, u32[]{:S(2)}) collective-permute-start(bf16[128,4352]{1,0:T(8,128)(2,1)} %add_convert_fusion.4.refs_7_), channel_id=1, source_target_pairs={{0,16},{8,24},{16,0},{24,8},{1,17},{9,25},{17,1},{25,9},{2,18},{10... | collective-permute-start | bytes 3342344 | tf_op jit(solution)/shard_map/ppermute | solution.py:1233
  539.8 78.0 %collective-permute-start.9 = (bf16[144,4352]{1,0:T(8,128)(2,1)}, bf16[144,4352]{1,0:T(8,128)(2,1)S(1)}, u32[]{:S(2)}, u32[]{:S(2)}) collective-permute-start(bf16[144,4352]{1,0:T(8,128)(2,1)} %add_convert_fusion.1.refs_6_), channel_id=1, source_target_pairs={{0,8},{8,0},{16,24},{24,16},{1,9},{9,1},{17,25},{25,17},{2,10},{10... | collective-permute-start | bytes 3760136 | tf_op jit(solution)/shard_map/ppermute | solution.py:1233
  572.4 45.4 %copy-start.18 = (bf16[272,4352]{1,0:T(8,128)(2,1)S(1)}, bf16[272,4352]{1,0:T(8,128)(2,1)}, u32[]{:S(2)}) copy-start(bf16[272,4352]{1,0:T(8,128)(2,1)} %get-tuple-element.101) | copy-start | bytes 7102468
  621.8 26.3 %collective-permute-start.15 = (bf16[272,4352]{1,0:T(8,128)(2,1)}, bf16[272,4352]{1,0:T(8,128)(2,1)}, u32[]{:S(2)}, u32[]{:S(2)}) collective-permute-start(bf16[272,4352]{1,0:T(8,128)(2,1)} %add_convert_fusion.refs_5_.total.total_tail), channel_id=1, source_target_pairs={{0,1},{1,0},{2,3},{3,2},{4,5},{5,4},{6,7},{7,6},{8,9},{9,8},{10,11... | collective-permute-start | bytes 7102472 | tf_op jit(solution)/shard_map/ppermute | solution.py:1249
  621.8 25.3 %copy-start.37 = (f32[1088]{0:T(1024)S(1)}, f32[1088]{0:T(1024)}, u32[]{:S(2)}) copy-start(f32[1088]{0:T(1024)} %param.27) | copy-start | bytes 13060
  621.8 25.9 %copy-start.29 = (f32[1,4352]{1,0:T(1,128)S(1)}, f32[1,4352]{1,0:T(1,128)}, u32[]{:S(2)}) copy-start(f32[1,4352]{1,0:T(1,128)} %get-tuple-element.114) | copy-start | bytes 52228
  621.8 26.2 %copy-start.28 = (f32[4,1088]{1,0:T(4,128)S(1)}, f32[4,1088]{1,0:T(4,128)}, u32[]{:S(2)}) copy-start(f32[4,1088]{1,0:T(4,128)} %get-tuple-element.113) | copy-start | bytes 52228
  646.4 12.9 %collective-permute-start.13 = (bf16[512,1152]{1,0:T(8,128)(2,1)}, bf16[512,1152]{1,0:T(8,128)(2,1)}, u32[]{:S(2)}, u32[]{:S(2)}) collective-permute-start(bf16[512,1152]{1,0:T(8,128)(2,1)} %get-tuple-element.106), channel_id=1, source_target_pairs={{0,1},{1,0},{2,3},{3,2},{4,5},{5,4},{6,7},{7,6},{8,9},{9,8},{10,11... | collective-permute-start | bytes 3538952 | tf_op jit(solution)/shard_map/ppermute | solution.py:1476
  647.0 12.4 %collective-permute-start.14 = (bf16[512,1152]{1,0:T(8,128)(2,1)}, bf16[512,1152]{1,0:T(8,128)(2,1)}, u32[]{:S(2)}, u32[]{:S(2)}) collective-permute-start(bf16[512,1152]{1,0:T(8,128)(2,1)} %get-tuple-element.107), channel_id=1, source_target_pairs={{0,1},{1,0},{2,3},{3,2},{4,5},{5,4},{6,7},{7,6},{8,9},{9,8},{10,11... | collective-permute-start | bytes 3538952 | tf_op jit(solution)/shard_map/ppermute | solution.py:1476
  653.9 62.7 %all-to-all-start.2 = ((bf16[4,272,1088]{2,1,0:T(8,128)(2,1)}), bf16[4,272,1088]{2,1,0:T(8,128)(2,1)}, u32[]{:S(2)}, u32[]{:S(2)}) async-start(bf16[4,272,1088]{2,1,0:T(8,128)(2,1)} %pair_blocks.1.refs_0_), calls=%async_computation.2 | async-start | bytes 5013504 | tf_op jit(solution)/shard_map/all_to_all | solution.py:1152
  670.7 21.2 %copy-start.16 = (bf16[1280,1088]{1,0:T(8,128)(2,1)S(1)}, bf16[1280,1088]{1,0:T(8,128)(2,1)}, u32[]{:S(2)}) copy-start(bf16[1280,1088]{1,0:T(8,128)(2,1)} %get-tuple-element.68.rows) | copy-start | bytes 8355844
  670.7 21.2 %copy-start.26 = (f32[1280]{0:T(1024)S(1)}, f32[1280]{0:T(1024)}, u32[]{:S(2)}) copy-start(f32[1280]{0:T(1024)} %copy-done.25) | copy-start | bytes 15364
  670.7 21.2 %copy-start.39 = (f32[1280]{0:T(1024)S(1)}, f32[1280]{0:T(1024)}, u32[]{:S(2)}) copy-start(f32[1280]{0:T(1024)} %copy-done.38) | copy-start | bytes 15364
  670.7 21.2 %copy-start.48 = (f32[1088]{0:T(1024)S(1)}, f32[1088]{0:T(1024)}, u32[]{:S(2)}) copy-start(f32[1088]{0:T(1024)} %param.28) | copy-start | bytes 13060
  691.9 15.6 %copy-start.10 = (bf16[1088,1152]{1,0:T(8,128)(2,1)S(1)}, bf16[1088,1152]{1,0:T(8,128)(2,1)}, u32[]{:S(2)}) copy-start(bf16[1088,1152]{1,0:T(8,128)(2,1)} %get-tuple-element.109.out) | copy-start | bytes 7520260
  722.3 109.0 %copy-start.9 = (f32[272,544]{1,0:T(8,128)}, f32[272,544]{1,0:T(8,128)S(1)}, u32[]{:S(2)}) copy-start(f32[272,544]{1,0:T(8,128)S(1)} %copy.84.refs_0_) | copy-start | bytes 1775620
  (24 other events, 102.9 us)
Sparse Core Ops, SparseCore 0:
  113.2 177.1 all-gather.2

commit v3 on v2

--- a/solution.py
+++ b/solution.py
@@ -64,7 +64,7 @@
         o_ref[rows, :] += jnp.where(inside, total / turned, 0.0).astype(jnp.bfloat16)
         lse_ref[rows, :] += jnp.where(inside, 0.0, top + jnp.log2(total))
 
-    def head_body(head, carry):
+    def head_body(head):
         inside, hm, _ = lane_masks(head)
         rest = 1 - hm
         va[...] = vt[...] * hm + rest
@@ -83,8 +83,8 @@
                 total += dot_nn(jnp.exp2(s_far - top).astype(jnp.bfloat16), va[:near, :])
             finish(rows, top, total, inside)
 
-        def group_body(group, carry):
-            rows = pl.ds(pl.multiple_of(own + group * GROUP, 128), GROUP)
+        for group in range(groups):
+            rows = pl.ds(own + group * GROUP, GROUP)
             q = q_ref[rows, :] * hm
             s_near = dot_nt(q, k_ref[rows, :]) + mg_ref[group]
             s_far = dot_nt(q, kt[...])
@@ -95,14 +95,15 @@
             total = dot_nn(jnp.exp2(s_near - top).astype(jnp.bfloat16), near)
             total += dot_nn(jnp.exp2(s_far - top).astype(jnp.bfloat16), va[...])
             finish(rows, top, total, inside)
-            return carry
-
-        return lax.fori_loop(0, groups, group_body, carry)
-
-    lax.fori_loop(0, jnp.minimum(2, heads - 2 * pair), head_body, 0)
-
-
-def attention_forward(parts, heads, triple, others, mask_trunk, mask_group, start, stop, deps=()):
+
+    head_body(0)
+    pl.when(2 * pair + 1 < heads)(lambda: head_body(1))
+
+
+def attention_forward(parts, heads, triple, others, mask_trunk, mask_group, start, stop, before=(), deps=()):
+    fixed = 7
+    aliases = {fixed + index: index for index in range(len(before))}
+    deps = tuple(before) + tuple(deps)
     rows = triple.shape[0]
     pairs = triple.shape[1] // (3 * 128)
     extra = others.shape[0]
@@ -121,10 +122,11 @@
             whole(mask_group.shape),
         ]
         + [pl.BlockSpec(memory_space=pl.ANY)] * len(deps),
-        out_specs=[block(rows, 0), block(rows, 0)],
+        out_specs=[block(rows, start)] * 2,
+        input_output_aliases=aliases,
         out_shape=[
-            jax.ShapeDtypeStruct((rows, (stop - start) * 128), jnp.bfloat16),
-            jax.ShapeDtypeStruct((rows, (stop - start) * 128), jnp.float32),
+            jax.ShapeDtypeStruct((rows, pairs * 128), jnp.bfloat16),
+            jax.ShapeDtypeStruct((rows, pairs * 128), jnp.float32),
         ],
         scratch_shapes=[
             pltpu.VMEM((TRUNK, 128), jnp.bfloat16),
@@ -133,7 +135,7 @@
         ],
         compiler_params=pltpu.CompilerParams(vmem_limit_bytes=48 * 1024 * 1024),
         cost_estimate=pl.CostEstimate(
-            flops=(stop - start) * rows * 6_800_000, bytes_accessed=rows * pairs * 2000, transcendentals=0
+            flops=(stop - start) * rows * 5_200_000, bytes_accessed=rows * pairs * 2000, transcendentals=0
         ),
         name="attention_forward",
     )(triple, triple, triple, others, others, mask_trunk, mask_group, *deps)
@@ -154,7 +156,7 @@
     *refs,
 ):
     dq_ref, dk_ref, dv_ref, dko_ref, dvo_ref = refs[extra : extra + 5]
-    kt, vt, ka, va, qa, da, qm, dm, dkt, dvt, dkg, dvg, dqs = refs[extra + 5 :]
+    kt, vt, ka, va, qa, da, qm, dm, dkt, dvt, dkg, dvg, dqs, kat = refs[extra + 5 :]
     pair = start + pl.program_id(0)
     own = TRUNK // parts
     tiles = own // QT
@@ -168,7 +170,7 @@
     dvg[...] = jnp.zeros_like(dvg)
     dqs[...] = jnp.zeros_like(dqs)
 
-    def head_body(head, carry):
+    def head_body(head):
         inside, hm, place = lane_masks(head)
         rest = 1 - hm
         outside = jnp.logical_not(inside)
@@ -177,8 +179,12 @@
         ka[TRUNK:, :] = k_ref[own:, :] * hm + rest
         va[TRUNK:, :] = v_ref[own:, :] * hm + rest
 
-        def prepare(step, carry):
-            rows = pl.ds(pl.multiple_of(step * 128, 128), 128)
+        kat[:, :TRUNK] = (kt[...] * hm).T
+        kat[:, TRUNK:] = (k_ref[own:, :] * hm).T
+
+        part = 256 if rows_all % 256 == 0 else 128
+        for index in range(rows_all // part):
+            rows = pl.ds(index * part, part)
             q = q_ref[rows, :] * hm
             d = do_ref[rows, :] * hm
             qm[rows, :] = q
@@ -187,10 +193,7 @@
             delta = jnp.sum(
                 d.astype(jnp.float32) * o_ref[rows, :].astype(jnp.float32), axis=1, keepdims=True
             )
-            da[rows, :] = d - split_three(jnp.broadcast_to(delta, (128, 128)), place, outside)
-            return carry
-
-        lax.fori_loop(0, rows_all // 128, prepare, 0)
+            da[rows, :] = d - split_three(jnp.broadcast_to(delta, (part, 128)), place, outside)
 
         def step(rows, keys, mask, keep, dk, dv):
             st = dot_nt(ka[keys, :], qa[rows, :])
@@ -201,7 +204,7 @@
             ds = (p * dp).astype(jnp.bfloat16)
             dv[keep, :] += dot_nn(p.astype(jnp.bfloat16), dm[rows, :])
             dk[keep, :] += dot_nn(ds, qm[rows, :])
-            dqs[rows, :] += jnp.where(inside, dot_tn(ds, ka[keys, :]), 0.0)
+            dqs[:, rows] += dot_nn(kat[:, keys], ds)
 
         span = parts * QT
         for tile in range(tiles):
@@ -209,27 +212,16 @@
             for near in range(tile + 1):
                 keys = pl.ds(near * span, span)
                 step(rows, keys, mt_ref[tile] if near == tile else None, keys, dkt, dvt)
-        count = QT if (groups * GROUP) % QT == 0 else 128
-
-        def far_body(index, carry):
-            rows = pl.ds(pl.multiple_of(own + index * count, 128), count)
-            keys = pl.ds(0, TRUNK)
-            step(rows, keys, None, keys, dkt, dvt)
-            return carry
-
-        lax.fori_loop(0, groups * GROUP // count, far_body, 0)
-
-        def near_body(group, carry):
-            rows = pl.ds(pl.multiple_of(own + group * GROUP, 128), GROUP)
-            keys = pl.ds(pl.multiple_of(TRUNK + group * GROUP, 128), GROUP)
-            keep = pl.ds(pl.multiple_of(group * GROUP, 128), GROUP)
-            step(rows, keys, mg_ref[group], keep, dkg, dvg)
-            return carry
-
-        return lax.fori_loop(0, groups, near_body, carry)
-
-    lax.fori_loop(0, jnp.minimum(2, heads - 2 * pair), head_body, 0)
-    dq_ref[...] = (dqs[...] * HEAD_DIM**-0.5).astype(jnp.bfloat16)
+        step(pl.ds(own, groups * GROUP), pl.ds(0, TRUNK), None, pl.ds(0, TRUNK), dkt, dvt)
+        for group in range(groups):
+            step(
+                pl.ds(own + group * GROUP, GROUP), pl.ds(TRUNK + group * GROUP, GROUP), mg_ref[group],
+                pl.ds(group * GROUP, GROUP), dkg, dvg,
+            )
+
+    head_body(0)
+    pl.when(2 * pair + 1 < heads)(lambda: head_body(1))
+    dq_ref[...] = (dqs[...].T * HEAD_DIM**-0.5).astype(jnp.bfloat16)
     dk_ref[own:, :] = (dkg[...] * LN2).astype(jnp.bfloat16)
     dv_ref[own:, :] = dvg[...].astype(jnp.bfloat16)
     for tile in range(tiles):
@@ -294,69 +286,127 @@
             pltpu.VMEM((TRUNK, 128), jnp.float32),
             pltpu.VMEM((near, 128), jnp.float32),
             pltpu.VMEM((near, 128), jnp.float32),
-            pltpu.VMEM((rows, 128), jnp.float32),
+            pltpu.VMEM((128, rows), jnp.float32),
+            pltpu.VMEM((128, TRUNK + near), jnp.bfloat16),
         ],
         compiler_params=pltpu.CompilerParams(vmem_limit_bytes=56 * 1024 * 1024),
         cost_estimate=pl.CostEstimate(
-            flops=(stop - start) * rows * 12_200_000, bytes_accessed=rows * pairs * 4000, transcendentals=0
+            flops=(stop - start) * rows * 1_000_000, bytes_accessed=rows * pairs * 4000, transcendentals=0
         ),
         name="attention_backward",
     )(triple, triple, triple, others, others, mixed, mixed_grad, lse, mask_trunk, mask_group, *deps)
 
 
-ERF_TOP = (
-    -2.72614225801306e-10, 2.77068142495902e-08, -2.10102402082508e-06, -5.69250639462346e-05,
-    -7.34990630326855e-04, -2.95459980854025e-03, -1.60960333262415e-02,
-)
-ERF_LOW = (
-    -1.45660718464996e-05, -2.13374055278905e-04, -1.68282697438203e-03, -7.37332916720468e-03,
-    -1.42647390514189e-02,
-)
-
-
-def erf_float(value):
-    value = jnp.clip(value, -3.832506856900711, 3.832506856900711)
-    square = value * value
-    top = jnp.full_like(value, ERF_TOP[0])
-    for c in ERF_TOP[1:]:
-        top = top * square + c
-    low = jnp.full_like(value, ERF_LOW[0])
-    for c in ERF_LOW[1:]:
-        low = low * square + c
-    return value * top / low
+def normal_share(value):
+    size = jnp.abs(value)
+    turn = 1.0 / (1.0 + 0.23164189 * size)
+    bell = jnp.exp2(value * value * -0.7213475204444817)
+    poly = (((0.530702714 * turn - 0.726576013) * turn + 0.710706870) * turn - 0.142248368) * turn
+    tail = (poly + 0.127414796) * turn * bell
+    return jnp.where(value < 0, tail, 1.0 - tail), bell
 
 
 FF_BLOCK = 256
 ROW_CHUNK = 640
 
 
-def ffn_kernel(outs, chunk, scalars, *refs):
-    up_main, down_main, tails, second, seed, bias = refs[:6]
-    lowered, second_grad, bias_grad = refs[6:9]
-    mine_grads, theirs_grads = refs[9 : 9 + outs], refs[9 + outs : 9 + 2 * outs]
-    up, down, act, wide, up_grad, down_grad, second_t, seed_t = refs[9 + 2 * outs :]
+def join_tails(slabs, rows, up, down):
+    rest = FF_BLOCK // len(slabs)
+    for shift, target in ((0, up), (rest, down)):
+        joined = jnp.concatenate([slab[:, shift : shift + rest] for slab in slabs], axis=1)
+        target[rows, :] = joined.astype(jnp.bfloat16)
+
+
+def plain_load(step, is_rest, scalars, refs, up, down):
+    main, tails = refs
+
+    @pl.when(jnp.logical_not(is_rest))
+    def _():
+        up[...] = main[0, 0, :, :FF_BLOCK]
+        down[...] = main[0, 0, :, FF_BLOCK:]
+
+    @pl.when(is_rest)
+    def _():
+        slabs = [tails[0, c].astype(jnp.float32) for c in range(tails.shape[1])]
+        join_tails(slabs, slice(None), up, down)
+
+
+def plain_specs(main):
+    last = main.shape[1] - 1
+    return [
+        pl.BlockSpec((1, 1, main.shape[2], 2 * FF_BLOCK), lambda j, s: (0, jnp.minimum(j, last), 0, 0)),
+        pl.BlockSpec(main.shape[:3] + (128,), lambda j, s: (0, 0, 0, 4)),
+    ], [main, main]
+
+
+def quick_load(step, is_rest, scalars, refs, up, down):
+    role = scalars[0]
+    bodies, tails = (refs[:5], refs[5:10]), (refs[10:15], refs[15:20])
+    height = bodies[0][0].shape[1]
+    spot = lambda d: pl.ds(pl.multiple_of(scalars[1 + d], 16), height)
+    low_quarter = (step % 8) // 2 < 2
+
+    def place(pieces):
+        def put(d, piece):
+            up[spot(d), :] = piece[0, :, :FF_BLOCK]
+            down[spot(d), :] = piece[0, :, FF_BLOCK:]
+
+        for d in range(3):
+            put(d, pieces[d])
+        pl.when(low_quarter)(lambda: put(3, pieces[3]))
+        pl.when(jnp.logical_not(low_quarter))(lambda: put(3, pieces[4]))
+
+    use_mine = jnp.logical_and(step // 8 == role, jnp.logical_not(is_rest))
+    use_theirs = jnp.logical_and(step // 8 == 1 - role, jnp.logical_not(is_rest))
+    pl.when(use_mine)(lambda: place(bodies[0]))
+    pl.when(use_theirs)(lambda: place(bodies[1]))
+
+    def rest(order):
+        for d in range(4):
+            slabs = []
+            for which in order:
+                pieces = tails[which]
+                for q in range(4):
+                    piece = pieces[d][q] if d < 3 else (pieces[3][q] if q < 2 else pieces[4][q - 2])
+                    slabs.append(piece.astype(jnp.float32))
+            join_tails(slabs, spot(d), up, down)
+
+    pl.when(jnp.logical_and(is_rest, role == 0))(lambda: rest((0, 1)))
+    pl.when(jnp.logical_and(is_rest, role != 0))(lambda: rest((1, 0)))
+
+
+def quick_specs(mine, theirs):
+    def body(shape, which, low, high):
+        def index(j, s):
+            turn = jnp.clip(j - 8 * (s[0] if which == 0 else 1 - s[0]), 0, 7)
+            return (jnp.clip(turn // 2, low, high) - low, 0, turn % 2)
+
+        return pl.BlockSpec((1, shape[1], 2 * FF_BLOCK), index)
+
+    spans = ((0, 3), (0, 3), (0, 3), (0, 1), (2, 3))
+    bodies = [
+        body(piece.shape, which, *span)
+        for which, pieces in enumerate((mine, theirs))
+        for piece, span in zip(pieces, spans)
+    ]
+    tails = [
+        pl.BlockSpec(piece.shape[:2] + (128,), lambda j, s: (0, 0, 8))
+        for pieces in (mine, theirs)
+        for piece in pieces
+    ]
+    arrays = list(mine) + list(theirs)
+    return bodies + tails, arrays * 2
+
+
+def ffn_kernel(load, held, outs, chunk, scalars, *refs):
+    weights, refs = refs[:held], refs[held:]
+    second, seed, bias = refs[:3]
+    lowered, second_grad, bias_grad = refs[3:6]
+    mine_grads, theirs_grads = refs[6 : 6 + outs], refs[6 + outs : 6 + 2 * outs]
+    up, down, act, wide, up_grad, down_grad, second_t, seed_t = refs[6 + 2 * outs :]
     step = pl.program_id(0)
     role = scalars[0]
-    is_rest = step == pl.num_programs(0) - 1
-
-    @pl.when(jnp.logical_not(is_rest))
-    def _():
-        height = up_main.shape[2]
-        for index in range(up_main.shape[0]):
-            rows = pl.ds(index * height, height)
-            up[rows, :] = up_main[index, 0]
-            down[rows, :] = down_main[index, 0]
-
-    @pl.when(is_rest)
-    def _():
-        height, columns = tails.shape[2], tails.shape[1]
-        rest = FF_BLOCK // columns
-        for index in range(tails.shape[0]):
-            rows = pl.ds(index * height, height)
-            slabs = [tails[index, c].astype(jnp.float32) for c in range(columns)]
-            for shift, target in ((0, up), (rest, down)):
-                joined = jnp.concatenate([slab[:, shift : shift + rest] for slab in slabs], axis=1)
-                target[rows, :] = joined.astype(jnp.bfloat16)
+    load(step, step == pl.num_programs(0) - 1, scalars, weights, up, down)
 
     @pl.when(step == 0)
     def _():
@@ -372,9 +422,9 @@
         rows = pl.ds(start, chunk)
         wide_in = dot_nn(second[rows, :], up[...]) + bias[...]
         hidden = dot_nn(seed[rows, :], down[...])
-        share = 0.5 + 0.5 * erf_float(wide_in * 0.7071067811865476)
+        share, bell = normal_share(wide_in)
         act_now = (wide_in * share).astype(jnp.bfloat16)
-        slope = share + wide_in * (jnp.exp(-0.5 * wide_in * wide_in) * 0.3989422804014327)
+        slope = share + wide_in * (bell * 0.3989422804014327)
         wide_now = (hidden * slope).astype(jnp.bfloat16)
         total += jnp.sum(wide_now.astype(jnp.float32), axis=0, keepdims=True)
         act[rows, :] = act_now
@@ -401,32 +451,23 @@
         deliver(down_grad, up_grad)
 
 
-def feed_forward(scalars, main, second, seed, bias, outs):
+def feed_forward(scalars, pair, second, seed, bias, outs):
     rows, width = second.shape
     hidden = bias.shape[0]
-    last = hidden // FF_BLOCK - 2
-    per = (last + 1) // main.shape[1]
-
-    def main_spec(shift):
-        def index(j, s):
-            j = jnp.minimum(j, last)
-            return (0, j // per, 0, j % per + shift)
-
-        return pl.BlockSpec((main.shape[0], 1, main.shape[2], FF_BLOCK), index)
-
-    tail_spec = pl.BlockSpec(main.shape[:3] + (128,), lambda j, s: (0, 0, 0, 4 * per))
+    quick = len(pair) == 2
+    specs, arrays = quick_specs(*pair) if quick else plain_specs(*pair)
+    load = quick_load if quick else plain_load
     whole = lambda shape: pl.BlockSpec(shape, lambda j, s: (0, 0))
     grad_spec = pl.BlockSpec((width // outs, FF_BLOCK), lambda j, s: (0, j))
     grad_shape = jax.ShapeDtypeStruct((width // outs, hidden), jnp.bfloat16)
     line = pl.BlockSpec((1, FF_BLOCK), lambda j, s: (0, j))
     chunk = ROW_CHUNK if rows % ROW_CHUNK == 0 else rows // 2
     return pl.pallas_call(
-        partial(ffn_kernel, outs, chunk),
+        partial(ffn_kernel, load, len(specs), outs, chunk),
         grid_spec=pltpu.PrefetchScalarGridSpec(
             num_scalar_prefetch=1,
             grid=(hidden // FF_BLOCK,),
-            in_specs=[
-                main_spec(0), main_spec(per), tail_spec,
+            in_specs=specs + [
                 whole((rows, width)), whole((rows, width)), line,
             ],
             out_specs=[whole((rows, width)), whole((rows, width)), line] + [grad_spec] * (2 * outs),
@@ -453,7 +494,7 @@
             transcendentals=rows * hidden,
         ),
         name="feed_forward",
-    )(scalars, main, main, main, second, seed, bias.reshape(1, hidden))
+    )(scalars, *arrays, second, seed, bias.reshape(1, hidden))
 
 
 MESH = pl.DeviceIdType.MESH
@@ -818,7 +859,7 @@
         out_specs=pl.BlockSpec((2, 1, columns // 2, height, lanes), lambda r: (0, r, 0, 0, 0)),
         out_shape=jax.ShapeDtypeStruct((2, rows, columns // 2, height, lanes), jnp.bfloat16),
         compiler_params=pltpu.CompilerParams(vmem_limit_bytes=48 * 1024 * 1024),
-        cost_estimate=pl.CostEstimate(flops=12_000_000_000, bytes_accessed=0, transcendentals=0),
+        cost_estimate=pl.CostEstimate(flops=1_000_000_000, bytes_accessed=0, transcendentals=0),
         name="divide_gradients",
     )(triple, out)
 
@@ -869,7 +910,7 @@
             jax.ShapeDtypeStruct((1, 3 * padded), jnp.float32),
         ],
         compiler_params=pltpu.CompilerParams(vmem_limit_bytes=48 * 1024 * 1024),
-        cost_estimate=pl.CostEstimate(flops=8_000_000_000, bytes_accessed=0, transcendentals=0),
+        cost_estimate=pl.CostEstimate(flops=1_000_000_000, bytes_accessed=0, transcendentals=0),
         name="finish_gradients",
     )(dq, dk, dv, other_k, other_v, *deps)
 
@@ -897,14 +938,15 @@
     second[...] = (unit * gain[...] + shift[...]).astype(jnp.bfloat16)
 
 
-def by_rows(kernel, name, count, chunked, fixed, outs, sums=(), scratch=(), flops=0):
+def by_rows(kernel, name, count, chunked, fixed, outs, sums=(), scratch=(), flops=0, deps=()):
     chunk = count // 5
     block = lambda width: pl.BlockSpec((chunk, width), lambda i: (i, 0))
     whole = lambda shape: pl.BlockSpec(shape, lambda i: (0,) * len(shape))
     return pl.pallas_call(
         kernel,
         grid=(5,),
-        in_specs=[block(v.shape[1]) for v in chunked] + [whole(v.shape) for v in fixed],
+        in_specs=[block(v.shape[1]) for v in chunked] + [whole(v.shape) for v in fixed]
+        + [HOLD] * len(deps),
         out_specs=[block(width) for width, _ in outs] + [whole(shape) for shape, _ in sums],
         out_shape=[jax.ShapeDtypeStruct((count, width), dtype) for width, dtype in outs]
         + [jax.ShapeDtypeStruct(shape, dtype) for shape, dtype in sums],
@@ -912,7 +954,7 @@
         compiler_params=pltpu.CompilerParams(vmem_limit_bytes=56 * 1024 * 1024),
         cost_estimate=pl.CostEstimate(flops=flops, bytes_accessed=0, transcendentals=0),
         name=name,
-    )(*chunked, *fixed)
+    )(*chunked, *fixed, *deps)
 
 
 def project_out(mixed, rows, weight, bias, gain, shift):
@@ -928,8 +970,8 @@
     )
 
 
-def middle_kernel(second_grad, lowered, middle, seed, mixed, weight, gain, down_bias,
-                  result, middle_grad, mixed_grad, sums, out_grad, total):
+def middle_kernel(held, second_grad, lowered, middle, seed, mixed, weight, gain, down_bias, *refs):
+    result, middle_grad, mixed_grad, sums, out_grad, total = refs[held:]
     step = pl.program_id(0)
     width = middle.shape[1]
     value, up = middle[...], seed[...].astype(jnp.float32)
@@ -960,20 +1002,21 @@
         out_grad[:, width:] = jnp.zeros((width, out_grad.shape[1] - width), jnp.bfloat16)
 
 
-def middle_back(second_grad, lowered, middle, seed, mixed, weight, gain, down_bias):
+def middle_back(second_grad, lowered, middle, seed, mixed, weight, gain, down_bias, deps):
     rows, width = middle.shape
     padded = weight.shape[0]
     line = lambda v: v.reshape(1, width)
     return by_rows(
-        middle_kernel, "middle_back", rows, (second_grad, lowered, middle, seed, mixed),
+        partial(middle_kernel, len(deps)), "middle_back", rows, (second_grad, lowered, middle, seed, mixed),
         (weight, line(gain), line(down_bias)),
         ((width, jnp.bfloat16), (width, jnp.float32), (padded, jnp.bfloat16)),
         (((4, width), jnp.float32), ((width, padded), jnp.bfloat16)),
-        (pltpu.VMEM((padded, width), jnp.float32),), flops=25_000_000_000,
+        (pltpu.VMEM((padded, width), jnp.float32),), flops=25_000_000_000, deps=deps,
     )
 
 
-def first_kernel(triple_grad, rows, middle_grad, weight, gain, input_grad, sums):
+def first_kernel(held, triple_grad, rows, middle_grad, weight, gain, *refs):
+    input_grad, sums = refs[held:]
     step = pl.program_id(0)
     grad = dot_nt(triple_grad[...], weight[...])
     back, gain_sum, shift_sum = norm_back(grad, rows[...].astype(jnp.float32), gain[...])
@@ -989,11 +1032,11 @@
         sums[...] += lines
 
 
-def first_back(triple_grad, rows, middle_grad, weight, gain):
+def first_back(triple_grad, rows, middle_grad, weight, gain, deps):
     count, width = rows.shape
     return by_rows(
-        first_kernel, "first_back", count, (triple_grad, rows, middle_grad), (weight, gain.reshape(1, width)),
-        ((width, jnp.bfloat16),), (((2, width), jnp.float32),), flops=25_000_000_000,
+        partial(first_kernel, len(deps)), "first_back", count, (triple_grad, rows, middle_grad), (weight, gain.reshape(1, width)),
+        ((width, jnp.bfloat16),), (((2, width), jnp.float32),), flops=4_000_000_000, deps=deps,
     )
 
 
@@ -1004,7 +1047,7 @@
     out[0, :, main : 2 * main] = other[...]
     for shard in range(8):
 
-        @pl.when(2 * quarter + core[0] == shard)
+        @pl.when(quarter + 4 * core[0] == shard)
         def _():
             cut = slice(shard * rest, (shard + 1) * rest)
             out[0, :, 2 * main : 2 * main + rest] = total_tail[:, cut]
@@ -1013,7 +1056,7 @@
 
 def pair_blocks(core, total, other, main, rest):
     rows = total.shape[0]
-    spec = pl.BlockSpec((rows, main), lambda q, s: (0, 2 * q + s[0]))
+    spec = pl.BlockSpec((rows, main), lambda q, s: (0, q + 4 * s[0]))
     tail = pl.BlockSpec((rows, 8 * rest), lambda q, s: (0, main // rest))
     return pl.pallas_call(
         partial(blocks_kernel, rest),
@@ -1024,7 +1067,7 @@
             out_specs=pl.BlockSpec((1, rows, 2 * (main + rest)), lambda q, s: (q, 0, 0)),
         ),
         out_shape=jax.ShapeDtypeStruct((4, rows, 2 * (main + rest)), total.dtype),
-        cost_estimate=pl.CostEstimate(flops=5_000_000_000, bytes_accessed=0, transcendentals=0),
+        cost_estimate=pl.CostEstimate(flops=1_000_000_000, bytes_accessed=0, transcendentals=0),
         name="pair_blocks",
     )(core, total, other, total, other)
 
@@ -1041,6 +1084,30 @@
         input_output_aliases={0: 0},
         name="after",
     )(value, *deps)
+
+
+def order_kernel(table, *refs):
+    pieces, out = refs[:-1], refs[-1]
+    for index, piece in enumerate(pieces):
+        out[table[index]] = piece[...]
+
+
+def in_order(table, pieces):
+    rows, width = pieces[0].shape
+    whole = pl.BlockSpec((rows, width), lambda i, s: (0, 0))
+    return pl.pallas_call(
+        order_kernel,
+        grid_spec=pltpu.PrefetchScalarGridSpec(
+            num_scalar_prefetch=1,
+            grid=(1,),
+            in_specs=[whole] * len(pieces),
+            out_specs=pl.BlockSpec((len(pieces), rows, width), lambda i, s: (0, 0, 0)),
+        ),
+        out_shape=jax.ShapeDtypeStruct((len(pieces), rows, width), pieces[0].dtype),
+        compiler_params=pltpu.CompilerParams(vmem_limit_bytes=48 * 1024 * 1024),
+        cost_estimate=pl.CostEstimate(flops=0, bytes_accessed=4 * len(pieces) * rows * width, transcendentals=0),
+        name="in_order",
+    )(table, *pieces)
 
 
 def layer_norm(value, gain, bias):
@@ -1152,8 +1219,9 @@
         return lax.all_to_all(value, "col", 0, 0, axis_index_groups=groups, tiled=True)
 
     def tree_sources(self, value):
-        mine = value.reshape(self.micro * self.length, value.shape[2])
-        return [mine] + [lax.ppermute(mine, "col", self.part_perm(e)) for e in range(1, self.parts)]
+        flat = (self.micro * self.length, value.shape[2])
+        moved = [lax.ppermute(value, "col", self.part_perm(e)) for e in range(1, self.parts)]
+        return [v.reshape(flat) for v in [value] + moved]
 
     def to_tree(self, sources):
         grain, each = self.grain, self.length // self.grain
@@ -1167,7 +1235,9 @@
         return spread(mine[chunk], sources, grain, self.count)
 
     def from_tree_sources(self, value):
-        return [value] + [lax.ppermute(value, "col", self.part_perm(e)) for e in range(1, self.parts)]
+        split = value.reshape(-1, self.grain, value.shape[1])
+        moved = [lax.ppermute(split, "col", self.part_perm(e)) for e in range(1, self.parts)]
+        return [value] + [v.reshape(value.shape) for v in moved]
 
     def from_tree_parts(self, sources):
         grain, each, parts = self.grain, self.length // self.grain, self.parts
@@ -1282,7 +1352,10 @@
 def pack_pair(w_up, w_down):
     main = w_up.shape[1] // 256 * 256
     down = w_down.T
-    return jnp.concatenate([w_up[:, :main], down[:, :main], w_up[:, main:], down[:, main:]], axis=1)
+    parts = []
+    for start in range(0, main, FF_BLOCK):
+        parts += [w_up[:, start : start + FF_BLOCK], down[:, start : start + FF_BLOCK]]
+    return jnp.concatenate(parts + [w_up[:, main:], down[:, main:]], axis=1)
 
 
 class QuickWeights:
@@ -1302,8 +1375,15 @@
         full, rows, pack = start_exchange(
             jnp.concatenate([w_qkv, w_out], axis=1), self.pack, value, self.place.count
         )
-        pair = lax.all_gather(pack, BOTH, axis=0, tiled=False)
-        self.pair = pair.reshape(lax.axis_size("row"), self.cols, self.rows, 2 * self.up_cols)
+        place = self.place
+        pieces = [pack] + [
+            lax.ppermute(pack, "col", place.quarter_perm(d)) for d in range(1, place.micro)
+        ]
+        self.own = in_order(place.quarter ^ jnp.arange(place.micro, dtype=jnp.int32), pieces)
+        self.beside, self.below = across(self.own, 1), across(self.own, 2)
+        self.far = (self.beside[:2], self.below[2:])
+        mine = [self.own, self.beside, self.below, across(self.far[0], 2), across(self.far[1], 1)]
+        self.pair = (mine, [core_swap(place, piece) for piece in mine])
         self.triple, self.out = assemble(full, self.width, self.padded, self.qkv_cols)
         return rows
 
@@ -1315,14 +1395,17 @@
         return final[:, : self.qkv_cols], final[:, self.qkv_cols :], summed, tokens
 
     def bias_order(self, bias):
-        blocks = bias.reshape(self.cols, self.up_cols)
+        blocks = bias.reshape(self.place.micro, self.place.parts, self.up_cols).transpose(1, 0, 2)
+        blocks = blocks.reshape(self.cols, self.up_cols)
         return jnp.concatenate([blocks[:, : self.main].reshape(-1), blocks[:, self.main :].reshape(-1)])
 
     def bias_back(self, grad):
         edge = self.cols * self.main
-        return jnp.concatenate(
+        blocks = jnp.concatenate(
             [grad[:edge].reshape(self.cols, self.main), grad[edge:].reshape(self.cols, self.rest)], axis=1
-        ).reshape(-1)
+        )
+        blocks = blocks.reshape(self.place.parts, self.place.micro, self.up_cols)
+        return blocks.transpose(1, 0, 2).reshape(-1)
 
     def pair_final(self, parts):
         final = jnp.sum(parts.astype(jnp.float32), axis=0)
@@ -1349,7 +1432,7 @@
         self.rest = self.up_cols - self.main
         full = lax.all_gather(pack_pair(w_up, w_down), BOTH, axis=0, tiled=False)
         full = full.reshape(lax.axis_size("row"), self.cols, self.rows, 2 * self.up_cols)
-        self.pair = full.transpose(1, 0, 2, 3).reshape(1, self.cols, width, 2 * self.up_cols)
+        self.pair = (full.transpose(1, 0, 2, 3).reshape(1, self.cols, width, 2 * self.up_cols),)
         self.scalars = jnp.zeros((2,), jnp.int32)
 
     def bias_order(self, bias):
@@ -1408,7 +1491,7 @@
     parent_ids = lax.dynamic_index_in_dim(paths[1], place.quarter, 0, keepdims=False)
     mask_trunk, mask_group = place.masks(own_ids, parent_ids)
 
-    seed_moved = place.swap_quarters(cotangent)
+    seed_moved = place.swap_quarters(after(cotangent, weights.own) if quick else cotangent)
 
     q_scale = HEAD_DIM**-0.5 * LOG2E
     triple_bias = jnp.concatenate(
@@ -1421,7 +1504,15 @@
     others = jnp.concatenate(
         [lax.ppermute(shared, "col", place.part_perm(e)) for e in range(1, parts)], axis=0
     )
-    mixed, lse = attention_forward(parts, heads, triple, others, mask_trunk, mask_group, 0, pairs)
+    cuts = [round(pairs * part / 9) for part in (0, 6, 8, 9)]
+    before, gates = (), ((), (), ())
+    if quick:
+        gates = ((weights.own,), weights.far, tuple(weights.pair[0][3:]))
+    for start, stop, deps in zip(cuts[:-1], cuts[1:], gates):
+        before = attention_forward(
+            parts, heads, triple, others, mask_trunk, mask_group, start, stop, before, deps
+        )
+    mixed, lse = before
     seed_rows = place.to_tree(place.tree_sources(after(seed_moved, mixed)))
     middle, second = project_out(mixed, rows_low, weights.out, out_bias, ln2_gain, ln2_bias)
     outs = 4 if quick else 1
@@ -1430,43 +1521,41 @@
     )
     pair_mine, pair_theirs = pair_grads[:outs], pair_grads[outs:]
     up_bias_grad = weights.bias_back(up_bias_grad.reshape(-1))
+    far = ()
+    if quick:
+        pair_swapped = {d: core_swap(place, pair_theirs[d]) for d in (3, 1, 2, 0)}
+        far = far_sums(pair_mine, pair_swapped)
+        received = far_sends(far)
     result, middle_grad, mixed_grad, sums, out_padded = middle_back(
-        second_grad, lowered, middle, seed_rows, mixed, weights.out, ln2_gain, down_bias
+        second_grad, lowered, middle, seed_rows, mixed, weights.out, ln2_gain, down_bias, far
     )
     out_bias_grad, gain_two, shift_two, down_bias_grad = sums[0], sums[1], sums[2], sums[3]
 
     turned = jnp.swapaxes(mask_trunk, 1, 2), jnp.swapaxes(mask_group, 1, 2)
     result_sources = place.from_tree_sources(result)
+    result_parts = place.from_tree_parts(result_sources)
+    result_out = place.swap_quarters(result_parts)
+    cut = 5 * pairs // 9
+    deps = (result_parts,)
     if quick:
-        pair_swapped = {d: core_swap(place, pair_theirs[d]) for d in (3, 1, 2, 0)}
-        sums = far_sums(pair_mine, pair_swapped)
-    grads = ()
-    for index, (start, stop) in enumerate(cuts_of(pairs, 4)):
-        deps = ()
-        if quick and index == 0:
-            deps = sums
-            received = far_sends(sums)
-        if index == 1:
-            result_parts = place.from_tree_parts(result_sources)
-            deps = (result_parts,)
-            result_out = place.swap_quarters(result_parts)
-            if quick:
-                sums = near_sums(pair_mine, pair_swapped, received)
-                deps = deps + sums
-                last = near_sends(sums)
-        if quick and index == 3:
-            total = row_total(pair_mine, pair_swapped, received, last)
-            deps = (total,)
-        grads = attention_backward(
-            parts, heads, triple, others, mixed, mixed_grad, lse, *turned, start, stop, grads, deps
-        )
+        near = near_sums(pair_mine, pair_swapped, received)
+        last = near_sends(near)
+        deps += near
+    inputs = parts, heads, triple, others, mixed, mixed_grad, lse, *turned
+    grads = attention_backward(*inputs, 0, cut, (), deps)
     deps = ()
+    if quick:
+        last = after(last[0], grads[0]), last[1]
+        total = row_total(pair_mine, pair_swapped, received, last)
+        deps = (total,)
+    grads = attention_backward(*inputs, cut, pairs, grads, deps)
+    finish_deps, first_deps = (), ()
     if quick:
         blocks = pair_blocks(
             place.part.reshape(1).astype(jnp.int32), total, core_swap(place, total), weights.main, weights.rest
         )
         pair_parts = place.swap_quarters(blocks)
-        deps = (blocks,)
+        finish_deps = (blocks,)
     else:
         up_grad, down_grad = weights.scatter_pair(pair_mine[0], pair_theirs[0])
     dq, dk, dv, dko, dvo = grads
@@ -1480,10 +1569,12 @@
         )
         for part in (dko, dvo)
     )
-    triple_grad, triple_sums = finish_gradients(own_trunk, dq, dk, dv, other_k, other_v, deps)
+    triple_grad, triple_sums = finish_gradients(own_trunk, dq, dk, dv, other_k, other_v, finish_deps)
     q_bias_grad = triple_sums[0, :width]
     v_bias_grad = triple_sums[0, 2 * padded : 2 * padded + width]
-    input_grad, sums = first_back(triple_grad, rows_low, middle_grad, weights.triple, ln1_gain)
+    input_grad, sums = first_back(
+        triple_grad, rows_low, middle_grad, weights.triple, ln1_gain, first_deps
+    )
     gain_one, shift_one = sums[0], sums[1]
     triple_weight_grad = dot_tn(first, triple_grad).astype(bf16)
     small = [

time: 859 us -> 784 us (0.913)
  Pallas kernels: 629 us -> 567 us
  waiting for transfers between devices: 41.7 us -> 67 us
  local copies, waits for them, and re-layouts: 68.8 us -> 48.4 us
  between operations: 15.4 us -> 1.88 us
  other arithmetic: 34.9 us -> 25.6 us
    pallas_call x4 -> x2, Pallas kernels: 133 us -> 81.6 us  [attention_backward(): pl.pallas_call(partial(bwd_kernel, parts, heads, start, len(deps)), grid=...]
    ppermute x6 -> x10, waiting for transfers between devices: 0.02 us -> 48.3 us  [across(): lax.ppermute(value, 'row', [(r, r ^ shift) for r in range(lax.axis_size('...]
    all_to_all x3, waiting for transfers between devices: 41.7 us -> 0.01 us  [swap_quarters(): lax.all_to_all(value, 'col', 0, 0, axis_index_groups=groups, tiled=True)]
    ppermute x2 -> x5, waiting for transfers between devices: 0.01 us -> 14.5 us  [the longest x3 12.6 us: start(): lax.ppermute(pack, 'col', place.quarter_perm(d))]
    pallas_call x1 -> x3, Pallas kernels: 67.9 us -> 56.3 us  [attention_forward(): pl.pallas_call(partial(fwd_kernel, parts, heads, start, len(deps)), grid=...]
    ppermute x2 -> x0, local copies, waits for them, and re-layouts: 11 us -> none  [the longest x1 5.53 us: tree_sources(): lax.ppermute(mine, 'col', self.part_perm(e))]
    unnamed x113 -> x124, local copies, waits for them, and re-layouts: 23.9 us -> 26.9 us
    pallas_call x1 -> x2, Pallas kernels: 128 us -> 129 us  [the longest x1 125 us: feed_forward(): pl.pallas_call(partial(ffn_kernel, load, len(specs), outs, chunk), grid_s...]
  transfers between devices with their start and end apart: 20 -> 31, of which waited for: 1 -> 8; matrix products, arithmetic and copies ran while one was open for 12% -> 9% of each run, Pallas kernels for 35% -> 31%
where the time goes in v3:
time: 784 us; the launch traced here: 773 us
  Pallas kernels  567 us (72%)
  waiting for transfers between devices  67 us (9%)
  local copies, waits for them, and re-layouts  48.4 us (6%)
  starting transfers between devices  31.7 us (4%)
  matrix products  31.6 us (4%)
  other arithmetic  25.6 us (3%)
    pallas_call x1, Pallas kernels, feed_forward(): pl.pallas_call(partial(ffn_kernel, load, len(specs), outs, chunk), grid_s...  125 us
    pallas_call x1, Pallas kernels, end_exchange(): pl.pallas_call(partial(end_kernel, grain), in_specs=[HOLD, pl.BlockSpec(m...  106 us
    pallas_call x1, Pallas kernels, start_exchange(): pl.pallas_call(partial(start_kernel, grain), in_specs=[HOLD] * 3, out_spe...  99.2 us
    pallas_call x2, Pallas kernels, attention_backward(): pl.pallas_call(partial(bwd_kernel, parts, heads, start, len(deps)), grid=...  81.6 us
    pallas_call x3, Pallas kernels, attention_forward(): pl.pallas_call(partial(fwd_kernel, parts, heads, start, len(deps)), grid=...  56.3 us
    pallas_call x3, Pallas kernels, by_rows(): pl.pallas_call(kernel, grid=(5,), in_specs=[block(v.shape[1]) for v in ch...  52.3 us
    ppermute x10, waiting for transfers between devices, across(): lax.ppermute(value, 'row', [(r, r ^ shift) for r in range(lax.axis_size('...  48.3 us
    unnamed x124, local copies, waits for them, and re-layouts  26.9 us
  transfers between devices with their start and end apart: 31, of which 8 were waited for; matrix products, arithmetic and copies ran while one was open for 9% of the time, Pallas kernels for 31%

profile of v3, /device:TPU:8, one launch (start us, length us, event | category | flops | bytes accessed | tf_op | source)
XLA Modules:
  0.0 772.8 jit_solution(1792940786326517574)
XLA Ops:
  0.7 3.7 copy.132.refs_0_
  6.5 99.2 %start_exchange.1 = (bf16[2,4,4,272,544]{4,3,2,1,0:T(8,128)(2,1)}, bf16[1280,1088]{1,0:T(8,128)(2,1)}, bf16[272,1088]{1,0:T(8,128)(2,1)}) custom-call(bf16[272,544]{1,0:T(8,128)(2,1)} %pad_maximum_fusion.4.pack, bf16[272,1088]{1,0:T(8,128)(2,1)} %concatenate.42.later_pack, bf16[4,320,1088]{2,1,0:T(8,128)(2,1)} %value.1), custom_call_target="tpu_custom_call" | custom-call | flops 99999997952 | tf_op jit(solution)/shard_map/start_exchange/pallas_call | solution.py:608
  105.8 2.7 collective-permute-start.1
  109.2 2.3 convert_reduce_fusion
  112.6 9.0 %assemble_weights.1 = (bf16[1088,3456]{1,0:T(8,128)(2,1)}, bf16[1152,1152]{1,0:T(8,128)(2,1)S(1)}) custom-call(bf16[2,4,4,272,544]{4,3,2,1,0:T(8,128)(2,1)} %get-tuple-element.63.full), custom_call_target="tpu_custom_call" | custom-call | flops 12000000000 | tf_op jit(solution)/shard_map/assemble_weights/pallas_call | solution.py:821
  121.7 16.2 %fusion.1.q_ref.k_ref.v_ref = bf16[1280,3456]{1,0:T(8,128)(2,1)S(1)} fusion(bf16[1088,3456]{1,0:T(8,128)(2,1)} %get-tuple-element.64.weight, f32[3456]{0:T(1024)S(1)} %select_maximum_fusion, f32[3456]{0:T(1024)S(1)} %copy-done.55, bf16[1280,1088]{1,0:T(8,128)(2,1)S(1)} %copy-done.20, f32[1088]{0:T(1024)S(1)} %copy-done.52, f32[1088]{0:T(1024)S(1)} %copy-done.43, ...), kind=kOutput, calls=%fused_computation.5 | convolution fusion | flops 9647554560 | bytes 19199488 | tf_op jit(solution)/shard_map/dot_general | solution.py:21
  137.9 1.7 slice.247
  139.6 2.3 copy-done.16
  142.5 1.7 fusion.21
  144.2 1.6 copy.100.mg_ref
  146.9 1.6 fusion.20
  148.5 2.5 copy.99.mt_ref
  151.0 12.6 %collective-permute-done.2.refs_3_ = bf16[272,1088]{1,0:T(8,128)(2,1)} collective-permute-done((bf16[272,1088]{1,0:T(8,128)(2,1)}, bf16[272,1088]{1,0:T(8,128)(2,1)}, u32[]{:S(2)}, u32[]{:S(2)}) %collective-permute-start.2) | collective-permute-done | bytes 591904 | tf_op jit(solution)/shard_map/ppermute | solution.py:1380
  164.7 3.6 in_order.1.refs_0_.refs_1_.refs_10_
  170.8 5.0 all-to-all-start
  177.1 37.5 %attention_forward.3 = (bf16[1280,1152]{1,0:T(8,128)(2,1)}, f32[1280,1152]{1,0:T(8,128)}) custom-call(bf16[1280,3456]{1,0:T(8,128)(2,1)} %copy-done.16, bf16[1280,3456]{1,0:T(8,128)(2,1)} %copy-done.16, bf16[1280,3456]{1,0:T(8,128)(2,1)} %copy-done.16, bf16[512,2304]{1,0:T(8,128)(2,1)S(1)} %collective-permute-done.12.ko_ref.vo_ref, ...), custom_call_target="tpu_custom_call" | custom-call | flops 39936000000 | bytes 23040000 | tf_op jit(solution)/shard_map/attention_forward/pallas_call | solution.py:112
  214.6 9.2 %collective-permute-done.3.refs_1_.refs_11_ = bf16[4,272,1088]{2,1,0:T(8,128)(2,1)} collective-permute-done((bf16[4,272,1088]{2,1,0:T(8,128)(2,1)}, bf16[4,272,1088]{2,1,0:T(8,128)(2,1)}, u32[]{:S(2)}, u32[]{:S(2)}) %collective-permute-start.3) | collective-permute-done | bytes 2367520 | tf_op jit(solution)/shard_map/ppermute | solution.py:1303
  229.0 13.7 %attention_forward.4 = (bf16[1280,1152]{1,0:T(8,128)(2,1)}, f32[1280,1152]{1,0:T(8,128)}) custom-call(bf16[1280,3456]{1,0:T(8,128)(2,1)} %copy-done.16, bf16[1280,3456]{1,0:T(8,128)(2,1)} %copy-done.16, bf16[1280,3456]{1,0:T(8,128)(2,1)} %copy-done.16, bf16[512,2304]{1,0:T(8,128)(2,1)} %copy-done, ...), custom_call_target="tpu_custom_call", output_to_operand_aliasing={{0}: (7, {}), {1}: (8, {})} | custom-call | flops 13312000000 | bytes 23040000 | tf_op jit(solution)/shard_map/attention_forward/pallas_call | solution.py:112
  242.8 9.9 %collective-permute-done.5.refs_2_.refs_3_.refs_13_ = bf16[2,272,1088]{2,1,0:T(8,128)(2,1)S(1)} collective-permute-done((bf16[2,272,1088]{2,1,0:T(8,128)(2,1)S(1)}, bf16[2,272,1088]{2,1,0:T(8,128)(2,1)S(1)}, u32[]{:S(2)}, u32[]{:S(2)}) %collective-permute-start.5) | collective-permute-done | bytes 1183776 | tf_op jit(solution)/shard_map/ppermute | solution.py:1303
  252.7 2.7 collective-permute-done.6.refs_3_.refs_4_.refs_14_
  255.4 5.1 attention_forward.5
  265.5 1.8 collective-permute-done.13
  268.9 10.1 %project_out.1 = (f32[1280,1088]{1,0:T(8,128)}, bf16[1280,1088]{1,0:T(8,128)(2,1)}) custom-call(bf16[1280,1152]{1,0:T(8,128)(2,1)} %get-tuple-element.69.mixed.refs_1_.o_ref, bf16[1280,1088]{1,0:T(8,128)(2,1)} %get-tuple-element.62.rows, bf16[1152,1152]{1,0:T(8,128)(2,1)} %copy-done.15, f32[1,1088]{1,0:T(1,128)} %reshape.579.bias, f32[1,1088]{1,0:T(1,128)} %reshape.580.gain, ...), custom_call_target="tpu_custom_call" | custom-call | flops 12000000000 | tf_op jit(solution)/shard_map/project_out/pallas_call | solution.py:945
  279.1 3.8 spread_rows.1.refs_21_.seed
  282.8 1.6 copy-done.4
  284.5 125.4 %feed_forward.1 = (f32[1280,1088]{1,0:T(8,128)}, f32[1280,1088]{1,0:T(8,128)}, f32[1,4352]{1,0:T(1,128)}, bf16[272,4352]{1,0:T(8,128)(2,1)}, bf16[272,4352]{1,0:...) custom-call(s32[6]{0:T(128)} %stack.46.scalars, ...), custom_call_target="tpu_custom_call" | custom-call | flops 145458462720 | bytes 65732608 | tf_op jit(solution)/shard_map/feed_forward/pallas_call | solution.py:465
  411.5 3.3 collective-permute-done.14
  414.8 2.6 add_convert_fusion.6.refs_1_
  424.3 22.0 %middle_back.1 = (bf16[1280,1088]{1,0:T(8,128)(2,1)}, f32[1280,1088]{1,0:T(8,128)}, bf16[1280,1152]{1,0:T(8,128)(2,1)}, f32[4,1088]{1,0:T(4,128)}, bf16[1088,1152]{1,0:T(8,128)(2,1)}) custom-call(f32[1280,1088]{1,0:T(8,128)} %get-tuple-element.72.second_grad, f32[1280,1088]{1,0:T(8,128)} %get-tuple-element.73.lowered, ...), custom_call_target="tpu_custom_call" | custom-call | flops 24999999488 | tf_op jit(solution)/shard_map/middle_back/pallas_call | solution.py:945
  450.8 26.5 %collective-permute-done.18 = bf16[144,4352]{1,0:T(8,128)(2,1)S(1)} collective-permute-done((bf16[144,4352]{1,0:T(8,128)(2,1)}, bf16[144,4352]{1,0:T(8,128)(2,1)S(1)}, u32[]{:S(2)}, u32[]{:S(2)}) %collective-permute-start.18) | collective-permute-done | bytes 1253408 | tf_op jit(solution)/shard_map/ppermute | solution.py:1303
  477.8 1.6 add_convert_fusion.1.refs_1_
  482.6 4.4 collect_rows.1
  487.0 4.9 all-to-all-start.1
  491.9 47.0 %attention_backward.2 = (bf16[1280,1152]{1,0:T(8,128)(2,1)}, bf16[1280,1152]{1,0:T(8,128)(2,1)}, bf16[1280,1152]{1,0:T(8,128)(2,1)}, bf16[512,1152]{1,0:T(8,128)(2,1)}, bf16[512,1152]{1,0:T(8,128)(2,1)}) custom-call(bf16[1280,3456]{1,0:T(8,128)(2,1)} %copy-done.16, bf16[1280,3456]{1,0:T(8,128)(2,1)} %copy-done.16, bf16[1280,3456]{1,0:T(8,128)(2,1)} %copy-done.16, ...), custom_call_target="tpu_custom_call" | custom-call | flops 6400000000 | bytes 46080000 | tf_op jit(solution)/shard_map/attention_backward/pallas_call | solution.py:251
  538.9 4.4 add_convert_fusion.refs_5_.total.total_tail
  544.8 34.6 %attention_backward.3 = (bf16[1280,1152]{1,0:T(8,128)(2,1)}, bf16[1280,1152]{1,0:T(8,128)(2,1)}, bf16[1280,1152]{1,0:T(8,128)(2,1)}, bf16[512,1152]{1,0:T(8,128)(2,1)}, bf16[512,1152]{1,0:T(8,128)(2,1)}) custom-call(bf16[1280,3456]{1,0:T(8,128)(2,1)} %copy-done.16, ...), custom_call_target="tpu_custom_call", output_to_operand_aliasing={{0}: (10, {}), {1}: (11, {}), {2}: (12, {}), {3}: (13, {}),... | custom-call | flops 5120000000 | bytes 46080000 | tf_op jit(solution)/shard_map/attention_backward/pallas_call | solution.py:251
  580.8 4.4 pair_blocks.1.refs_0_
  585.2 4.8 all-to-all-start.2
  590.2 11.3 %finish_gradients.1 = (bf16[1280,3456]{1,0:T(8,128)(2,1)}, f32[1,3456]{1,0:T(1,128)S(1)}) custom-call(bf16[1280,1152]{1,0:T(8,128)(2,1)} %get-tuple-element.91.dq, bf16[1280,1152]{1,0:T(8,128)(2,1)} %get-tuple-element.92.dk, bf16[1280,1152]{1,0:T(8,128)(2,1)} %get-tuple-element.93.dv, bf16[512,1152]{1,0:T(8,128)(2,1)} %collective-permute-done.25.other_k, ...), custom_call_target="tpu_custom_call" | custom-call | flops 1000000000 | tf_op jit(solution)/shard_map/finish_gradients/pallas_call | solution.py:898
  601.5 20.2 %first_back.1 = (bf16[1280,1088]{1,0:T(8,128)(2,1)}, f32[2,1088]{1,0:T(2,128)}) custom-call(bf16[1280,3456]{1,0:T(8,128)(2,1)} %get-tuple-element.96.triple_grad, bf16[1280,1088]{1,0:T(8,128)(2,1)} %get-tuple-element.62.rows, f32[1280,1088]{1,0:T(8,128)} %get-tuple-element.98.middle_grad, bf16[1088,3456]{1,0:T(8,128)(2,1)} %get-tuple-element.64.weight, ...), custom_call_target="tpu_custom_call" | custom-call | flops 4000000000 | tf_op jit(solution)/shard_map/first_back/pallas_call | solution.py:945
  622.7 15.4 %convolution_convert_fusion.triple = bf16[1088,3456]{1,0:T(8,128)(2,1)} fusion(bf16[1280,3456]{1,0:T(8,128)(2,1)} %get-tuple-element.96.triple_grad, bf16[1280,1088]{1,0:T(8,128)(2,1)S(1)} %copy-done.21, f32[1088]{0:T(1024)S(1)} %copy-done.53, f32[1088]{0:T(1024)S(1)} %copy-done.44, f32[1280]{0:T(1024)S(1)} %copy-done.46, f32[1280]{0:T(1024)S(1)} %copy-done.33), kind=kOutput, calls=%fused_computation.6 | convolution fusion | flops 9638043648 | bytes 19171840 | tf_op jit(solution)/shard_map/dot_general | solution.py:29
  638.1 9.1 %divide_gradients.1.grads = bf16[2,4,4,272,544]{4,3,2,1,0:T(8,128)(2,1)} custom-call(bf16[1088,3456]{1,0:T(8,128)(2,1)} %convolution_convert_fusion.triple, bf16[1088,1152]{1,0:T(8,128)(2,1)S(1)} %copy-done.8), custom_call_target="tpu_custom_call" | custom-call | flops 1000000000 | tf_op jit(solution)/shard_map/divide_gradients/pallas_call | solution.py:852
  647.2 2.2 convert_reduce_fusion.1
  652.8 2.1 copy-done.14
  655.0 106.2 %end_exchange.1 = (f32[272,544]{1,0:T(8,128)S(1)}, f32[104,128]{1,0:T(8,128)S(1)}, bf16[4,320,1088]{2,1,0:T(8,128)(2,1)S(1)}) custom-call(bf16[2,4,4,272,544]{4,3,2,1,0:T(8,128)(2,1)} %divide_gradients.1.grads, f32[104,128]{1,0:T(8,128)S(1)} %pad_bitcast_fusion.small, bf16[1280,1088]{1,0:T(8,128)(2,1)S(1)} %copy-done.14, f32[272,544]{1,0:T(8,128)S(1)} %copy.108.refs_0_, ...), custom_call_target="tpu_custom_call" | custom-call | flops 99999997952 | tf_op jit(solution)/shard_map/end_exchange/pallas_call | solution.py:758
  761.2 1.6 copy-done.6
  767.1 3.8 copy.133
  771.0 1.6 copy.134
  (246 shorter events, 50.4 us)
Async XLA Ops:
  105.7 45.3 %collective-permute-start = (bf16[272,1088]{1,0:T(8,128)(2,1)}, bf16[272,1088]{1,0:T(8,128)(2,1)}, u32[]{:S(2)}, u32[]{:S(2)}) collective-permute-start(bf16[272,1088]{1,0:T(8,128)(2,1)} %get-tuple-element.61.refs_0_), channel_id=1, source_target_pairs={{0,2},{1,3},{2,0},{3,1},{4,6},{5,7},{6,4},{7,5},{8,10},{9,11},{10,... | collective-permute-start | bytes 1775624 | tf_op jit(solution)/shard_map/ppermute | solution.py:1380
  105.8 45.2 %collective-permute-start.1 = (bf16[272,1088]{1,0:T(8,128)(2,1)}, bf16[272,1088]{1,0:T(8,128)(2,1)}, u32[]{:S(2)}, u32[]{:S(2)}) collective-permute-start(bf16[272,1088]{1,0:T(8,128)(2,1)} %get-tuple-element.61.refs_0_), channel_id=1, source_target_pairs={{0,4},{1,5},{2,6},{3,7},{4,0},{5,1},{6,2},{7,3},{8,12},{9,13},{10,... | collective-permute-start | bytes 1775624 | tf_op jit(solution)/shard_map/ppermute | solution.py:1380
  108.4 55.2 %collective-permute-start.2 = (bf16[272,1088]{1,0:T(8,128)(2,1)}, bf16[272,1088]{1,0:T(8,128)(2,1)}, u32[]{:S(2)}, u32[]{:S(2)}) collective-permute-start(bf16[272,1088]{1,0:T(8,128)(2,1)} %get-tuple-element.61.refs_0_), channel_id=1, source_target_pairs={{0,6},{1,7},{2,4},{3,5},{4,2},{5,3},{6,0},{7,1},{8,14},{9,15},{10,... | collective-permute-start | bytes 1775624 | tf_op jit(solution)/shard_map/ppermute | solution.py:1380
  121.6 16.3 %copy-start.15 = (bf16[1152,1152]{1,0:T(8,128)(2,1)}, bf16[1152,1152]{1,0:T(8,128)(2,1)S(1)}, u32[]{:S(2)}) copy-start(bf16[1152,1152]{1,0:T(8,128)(2,1)S(1)} %get-tuple-element.70.weight) | copy-start | bytes 7962628
  141.9 33.9 %collective-permute-start.12 = (bf16[512,2304]{1,0:T(8,128)(2,1)}, bf16[512,2304]{1,0:T(8,128)(2,1)S(1)}, u32[]{:S(2)}, u32[]{:S(2)}) collective-permute-start(bf16[512,2304]{1,0:T(8,128)(2,1)} %slice.247), channel_id=1, source_target_pairs={{0,1},{1,0},{2,3},{3,2},{4,5},{5,4},{6,7},{7,6},{8,9},{9,8},{10,11... | collective-permute-start | bytes 7077896 | tf_op jit(solution)/shard_map/ppermute | solution.py:1505
  168.3 55.5 %collective-permute-start.3 = (bf16[4,272,1088]{2,1,0:T(8,128)(2,1)}, bf16[4,272,1088]{2,1,0:T(8,128)(2,1)}, u32[]{:S(2)}, u32[]{:S(2)}) collective-permute-start(bf16[4,272,1088]{2,1,0:T(8,128)(2,1)} %in_order.1.refs_0_.refs_1_.refs_10_), channel_id=1, source_target_pairs={{0,8},{8,0},{16,24},{24,16},{1,9},{9,1},{17,25},{25,17},{2,10},{10... | collective-permute-start | bytes 7102472 | tf_op jit(solution)/shard_map/ppermute | solution.py:1303
  169.8 57.0 %collective-permute-start.4 = (bf16[4,272,1088]{2,1,0:T(8,128)(2,1)}, bf16[4,272,1088]{2,1,0:T(8,128)(2,1)}, u32[]{:S(2)}, u32[]{:S(2)}) collective-permute-start(bf16[4,272,1088]{2,1,0:T(8,128)(2,1)} %in_order.1.refs_0_.refs_1_.refs_10_), channel_id=1, source_target_pairs={{0,16},{8,24},{16,0},{24,8},{1,17},{9,25},{17,1},{25,9},{2,18},{10... | collective-permute-start | bytes 7102472 | tf_op jit(solution)/shard_map/ppermute | solution.py:1303
  170.8 90.7 %all-to-all-start = ((bf16[4,320,1088]{2,1,0:T(8,128)(2,1)}), bf16[4,320,1088]{2,1,0:T(8,128)(2,1)}, u32[]{:S(2)}, u32[]{:S(2)}) async-start(bf16[4,320,1088]{2,1,0:T(8,128)(2,1)} %after.3), calls=%async_computation | async-start | bytes 5898240 | tf_op jit(solution)/shard_map/all_to_all | solution.py:1219
  177.1 37.5 %copy-start = (bf16[512,2304]{1,0:T(8,128)(2,1)}, bf16[512,2304]{1,0:T(8,128)(2,1)S(1)}, u32[]{:S(2)}) copy-start(bf16[512,2304]{1,0:T(8,128)(2,1)S(1)} %collective-permute-done.12.ko_ref.vo_ref) | copy-start | bytes 7077892
  225.2 27.5 %collective-permute-start.5 = (bf16[2,272,1088]{2,1,0:T(8,128)(2,1)S(1)}, bf16[2,272,1088]{2,1,0:T(8,128)(2,1)S(1)}, u32[]{:S(2)}, u32[]{:S(2)}) collective-permute-start(bf16[2,272,1088]{2,1,0:T(8,128)(2,1)S(1)} %slice.245.refs_2_), channel_id=1, source_target_pairs={{0,16},{8,24},{16,0},{24,8},{1,17},{9,25},{17,1},{25,9},{2,18},{10... | collective-permute-start | bytes 3551240 | tf_op jit(solution)/shard_map/ppermute | solution.py:1303
  228.2 27.2 %collective-permute-start.6 = (bf16[2,272,1088]{2,1,0:T(8,128)(2,1)S(1)}, bf16[2,272,1088]{2,1,0:T(8,128)(2,1)S(1)}, u32[]{:S(2)}, u32[]{:S(2)}) collective-permute-start(bf16[2,272,1088]{2,1,0:T(8,128)(2,1)S(1)} %slice.246.refs_3_), channel_id=1, source_target_pairs={{0,8},{8,0},{16,24},{24,16},{1,9},{9,1},{17,25},{25,17},{2,10},{10... | collective-permute-start | bytes 3551240 | tf_op jit(solution)/shard_map/ppermute | solution.py:1303
  261.6 5.8 collective-permute-start.13
  261.7 22.8 %collective-permute-start.7 = (bf16[4,272,1088]{2,1,0:T(8,128)(2,1)}, bf16[4,272,1088]{2,1,0:T(8,128)(2,1)}, u32[]{:S(2)}, u32[]{:S(2)}) collective-permute-start(bf16[4,272,1088]{2,1,0:T(8,128)(2,1)} %in_order.1.refs_0_.refs_1_.refs_10_), channel_id=1, source_target_pairs={{0,1},{1,0},{2,3},{3,2},{4,5},{5,4},{6,7},{7,6},{8,9},{9,8},{10,11... | collective-permute-start | bytes 7102472 | tf_op jit(solution)/shard_map/ppermute | solution.py:1319
  262.2 22.3 %collective-permute-start.8 = (bf16[4,272,1088]{2,1,0:T(8,128)(2,1)}, bf16[4,272,1088]{2,1,0:T(8,128)(2,1)}, u32[]{:S(2)}, u32[]{:S(2)}) collective-permute-start(bf16[4,272,1088]{2,1,0:T(8,128)(2,1)} %collective-permute-done.3.refs_1_.refs_11_), channel_id=1, source_target_pairs={{0,1},{1,0},{2,3},{3,2},{4,5},{5,4},{6,7},{7,6},{8,9},{9,8},{10,11... | collective-permute-start | bytes 7102472 | tf_op jit(solution)/shard_map/ppermute | solution.py:1319
  262.3 22.2 %collective-permute-start.9 = (bf16[4,272,1088]{2,1,0:T(8,128)(2,1)}, bf16[4,272,1088]{2,1,0:T(8,128)(2,1)}, u32[]{:S(2)}, u32[]{:S(2)}) collective-permute-start(bf16[4,272,1088]{2,1,0:T(8,128)(2,1)} %collective-permute-done.4.refs_2_.refs_12_), channel_id=1, source_target_pairs={{0,1},{1,0},{2,3},{3,2},{4,5},{5,4},{6,7},{7,6},{8,9},{9,8},{10,11... | collective-permute-start | bytes 7102472 | tf_op jit(solution)/shard_map/ppermute | solution.py:1319
  265.4 19.1 %collective-permute-start.10 = (bf16[2,272,1088]{2,1,0:T(8,128)(2,1)S(1)}, bf16[2,272,1088]{2,1,0:T(8,128)(2,1)}, u32[]{:S(2)}, u32[]{:S(2)}) collective-permute-start(bf16[2,272,1088]{2,1,0:T(8,128)(2,1)S(1)} %collective-permute-done.5.refs_2_.refs_3_.refs_13_), channel_id=1, source_target_pairs={{0,1},{1,0},{2,3},{3,2},{4,5},{5,4},{6,7},{7,6},{8,9},{9,8},{10,11... | collective-permute-start | bytes 3551240 | tf_op jit(solution)/shard_map/ppermute | solution.py:1319
  267.4 17.1 %collective-permute-start.11 = (bf16[2,272,1088]{2,1,0:T(8,128)(2,1)S(1)}, bf16[2,272,1088]{2,1,0:T(8,128)(2,1)}, u32[]{:S(2)}, u32[]{:S(2)}) collective-permute-start(bf16[2,272,1088]{2,1,0:T(8,128)(2,1)S(1)} %copy-done.11), channel_id=1, source_target_pairs={{0,1},{1,0},{2,3},{3,2},{4,5},{5,4},{6,7},{7,6},{8,9},{9,8},{10,11... | collective-permute-start | bytes 3551240 | tf_op jit(solution)/shard_map/ppermute | solution.py:1319
  284.5 125.9 %copy-start.42 = (f32[1088]{0:T(1024)S(1)}, f32[1088]{0:T(1024)}, u32[]{:S(2)}) copy-start(f32[1088]{0:T(1024)} %param.39) | copy-start | bytes 13060
  410.0 4.8 collective-permute-start.14
  411.0 8.3 %collective-permute-start.16 = (bf16[272,4352]{1,0:T(8,128)(2,1)}, bf16[272,4352]{1,0:T(8,128)(2,1)S(1)}, u32[]{:S(2)}, u32[]{:S(2)}) collective-permute-start(bf16[272,4352]{1,0:T(8,128)(2,1)} %get-tuple-element.80), channel_id=1, source_target_pairs={{0,1},{1,0},{2,3},{3,2},{4,5},{5,4},{6,7},{7,6},{8,9},{9,8},{10,11... | collective-permute-start | bytes 7102472 | tf_op jit(solution)/shard_map/ppermute | solution.py:1319
  411.1 10.4 %collective-permute-start.15 = (bf16[272,4352]{1,0:T(8,128)(2,1)}, bf16[272,4352]{1,0:T(8,128)(2,1)S(1)}, u32[]{:S(2)}, u32[]{:S(2)}) collective-permute-start(bf16[272,4352]{1,0:T(8,128)(2,1)} %get-tuple-element.78), channel_id=1, source_target_pairs={{0,1},{1,0},{2,3},{3,2},{4,5},{5,4},{6,7},{7,6},{8,9},{9,8},{10,11... | collective-permute-start | bytes 7102472 | tf_op jit(solution)/shard_map/ppermute | solution.py:1319
  417.4 31.4 %collective-permute-start.19 = (bf16[128,4352]{1,0:T(8,128)(2,1)}, bf16[128,4352]{1,0:T(8,128)(2,1)S(1)}, u32[]{:S(2)}, u32[]{:S(2)}) collective-permute-start(bf16[128,4352]{1,0:T(8,128)(2,1)} %add_convert_fusion.6.refs_1_), channel_id=1, source_target_pairs={{0,8},{8,0},{16,24},{24,16},{1,9},{9,1},{17,25},{25,17},{2,10},{10... | collective-permute-start | bytes 3342344 | tf_op jit(solution)/shard_map/ppermute | solution.py:1303
  446.3 31.6 %copy-start.25 = (bf16[272,4352]{1,0:T(8,128)(2,1)S(1)}, bf16[272,4352]{1,0:T(8,128)(2,1)}, u32[]{:S(2)}) copy-start(bf16[272,4352]{1,0:T(8,128)(2,1)} %copy-done.24) | copy-start | bytes 7102468
  446.3 33.1 %collective-permute-start.17 = (bf16[20,64,1088]{2,1,0:T(8,128)(2,1)}, bf16[20,64,1088]{2,1,0:T(8,128)(2,1)}, u32[]{:S(2)}, u32[]{:S(2)}) collective-permute-start(bf16[20,64,1088]{2,1,0:T(8,128)(2,1)} %bitcast.38), channel_id=1, source_target_pairs={{0,1},{1,0},{2,3},{3,2},{4,5},{5,4},{6,7},{7,6},{8,9},{9,8},{10,11... | collective-permute-start | bytes 8355848 | tf_op jit(solution)/shard_map/ppermute | solution.py:1239
  446.7 30.6 %collective-permute-start.18 = (bf16[144,4352]{1,0:T(8,128)(2,1)}, bf16[144,4352]{1,0:T(8,128)(2,1)S(1)}, u32[]{:S(2)}, u32[]{:S(2)}) collective-permute-start(bf16[144,4352]{1,0:T(8,128)(2,1)} %add_convert_fusion.3.refs_0_), channel_id=1, source_target_pairs={{0,16},{8,24},{16,0},{24,8},{1,17},{9,25},{17,1},{25,9},{2,18},{10... | collective-permute-start | bytes 3760136 | tf_op jit(solution)/shard_map/ppermute | solution.py:1303
  447.2 91.7 %collective-permute-start.20 = (bf16[272,4352]{1,0:T(8,128)(2,1)}, bf16[272,4352]{1,0:T(8,128)(2,1)}, u32[]{:S(2)}, u32[]{:S(2)}) collective-permute-start(bf16[272,4352]{1,0:T(8,128)(2,1)} %get-tuple-element.90), channel_id=1, source_target_pairs={{0,1},{1,0},{2,3},{3,2},{4,5},{5,4},{6,7},{7,6},{8,9},{9,8},{10,11... | collective-permute-start | bytes 7102472 | tf_op jit(solution)/shard_map/ppermute | solution.py:1319
  447.2 91.7 %collective-permute-start.23 = (bf16[144,4352]{1,0:T(8,128)(2,1)}, bf16[144,4352]{1,0:T(8,128)(2,1)}, u32[]{:S(2)}, u32[]{:S(2)}) collective-permute-start(bf16[144,4352]{1,0:T(8,128)(2,1)} %add_convert_fusion.2.refs_3_), channel_id=1, source_target_pairs={{0,16},{8,24},{16,0},{24,8},{1,17},{9,25},{17,1},{25,9},{2,18},{10... | collective-permute-start | bytes 3760136 | tf_op jit(solution)/shard_map/ppermute | solution.py:1303
  448.7 90.2 %collective-permute-start.22 = (bf16[128,4352]{1,0:T(8,128)(2,1)}, bf16[128,4352]{1,0:T(8,128)(2,1)}, u32[]{:S(2)}, u32[]{:S(2)}) collective-permute-start(bf16[128,4352]{1,0:T(8,128)(2,1)} %add_convert_fusion.5.refs_2_), channel_id=1, source_target_pairs={{0,8},{8,0},{16,24},{24,16},{1,9},{9,1},{17,25},{25,17},{2,10},{10... | collective-permute-start | bytes 3342344 | tf_op jit(solution)/shard_map/ppermute | solution.py:1303
  450.8 30.1 %copy-start.50 = (s32[20]{0:T(128)S(1)}, s32[20]{0:T(128)}, u32[]{:S(2)}) copy-start(s32[20]{0:T(128)} %constant.189.clone) | copy-start | bytes 244
  450.8 30.1 %copy-start.51 = (s32[20]{0:T(128)S(1)}, s32[20]{0:T(128)}, u32[]{:S(2)}) copy-start(s32[20]{0:T(128)} %constant.190.clone) | copy-start | bytes 244
  450.8 30.1 %copy-start.18 = (s32[40]{0:T(128)S(1)}, s32[40]{0:T(128)}, u32[]{:S(2)}) copy-start(s32[40]{0:T(128)} %constant.191.clone) | copy-start | bytes 484
  450.8 30.9 %copy-start.17 = (s32[40]{0:T(128)S(1)}, s32[40]{0:T(128)}, u32[]{:S(2)}) copy-start(s32[40]{0:T(128)} %constant.192.clone) | copy-start | bytes 484
  450.8 31.8 %copy-start.5 = (bf16[1280,1088]{1,0:T(8,128)(2,1)S(1)}, bf16[1280,1088]{1,0:T(8,128)(2,1)}, u32[]{:S(2)}) copy-start(bf16[1280,1088]{1,0:T(8,128)(2,1)} %get-tuple-element.81.refs_0_) | copy-start | bytes 8355844
  477.3 61.6 %collective-permute-start.24 = (bf16[128,4352]{1,0:T(8,128)(2,1)}, bf16[128,4352]{1,0:T(8,128)(2,1)}, u32[]{:S(2)}, u32[]{:S(2)}) collective-permute-start(bf16[128,4352]{1,0:T(8,128)(2,1)} %add_convert_fusion.4.refs_2_), channel_id=1, source_target_pairs={{0,16},{8,24},{16,0},{24,8},{1,17},{9,25},{17,1},{25,9},{2,18},{10... | collective-permute-start | bytes 3342344 | tf_op jit(solution)/shard_map/ppermute | solution.py:1303
  479.4 59.5 %collective-permute-start.21 = (bf16[144,4352]{1,0:T(8,128)(2,1)}, bf16[144,4352]{1,0:T(8,128)(2,1)}, u32[]{:S(2)}, u32[]{:S(2)}) collective-permute-start(bf16[144,4352]{1,0:T(8,128)(2,1)} %add_convert_fusion.1.refs_1_), channel_id=1, source_target_pairs={{0,8},{8,0},{16,24},{24,16},{1,9},{9,1},{17,25},{25,17},{2,10},{10... | collective-permute-start | bytes 3760136 | tf_op jit(solution)/shard_map/ppermute | solution.py:1303
  487.0 98.2 %all-to-all-start.1 = ((bf16[4,320,1088]{2,1,0:T(8,128)(2,1)}), bf16[4,320,1088]{2,1,0:T(8,128)(2,1)}, u32[]{:S(2)}, u32[]{:S(2)}) async-start(bf16[4,320,1088]{2,1,0:T(8,128)(2,1)} %bitcast.19.refs_0_), calls=%async_computation.1 | async-start | bytes 5898240 | tf_op jit(solution)/shard_map/all_to_all | solution.py:1219
  543.3 37.5 %collective-permute-start.27 = (bf16[272,4352]{1,0:T(8,128)(2,1)S(1)}, bf16[272,4352]{1,0:T(8,128)(2,1)}, u32[]{:S(2)}, u32[]{:S(2)}) collective-permute-start(bf16[272,4352]{1,0:T(8,128)(2,1)S(1)} %add_convert_fusion.refs_5_.total.total_tail), channel_id=1, source_target_pairs={{0,1},{1,0},{2,3},{3,2},{4,5},{5,4},{6,7},{7,6},{8,9},{9,8},{10,11... | collective-permute-start | bytes 7102472 | tf_op jit(solution)/shard_map/ppermute | solution.py:1319
  544.8 35.2 %copy-start.44 = (f32[1088]{0:T(1024)S(1)}, f32[1088]{0:T(1024)}, u32[]{:S(2)}) copy-start(f32[1088]{0:T(1024)} %param.27) | copy-start | bytes 13060
  544.8 35.8 %copy-start.36 = (f32[1,4352]{1,0:T(1,128)S(1)}, f32[1,4352]{1,0:T(1,128)}, u32[]{:S(2)}) copy-start(f32[1,4352]{1,0:T(1,128)} %get-tuple-element.102) | copy-start | bytes 52228
  579.4 10.7 %collective-permute-start.25 = (bf16[512,1152]{1,0:T(8,128)(2,1)}, bf16[512,1152]{1,0:T(8,128)(2,1)}, u32[]{:S(2)}, u32[]{:S(2)}) collective-permute-start(bf16[512,1152]{1,0:T(8,128)(2,1)} %get-tuple-element.94), channel_id=1, source_target_pairs={{0,1},{1,0},{2,3},{3,2},{4,5},{5,4},{6,7},{7,6},{8,9},{9,8},{10,11... | collective-permute-start | bytes 3538952 | tf_op jit(solution)/shard_map/ppermute | solution.py:1565
  579.5 10.7 %collective-permute-start.26 = (bf16[512,1152]{1,0:T(8,128)(2,1)}, bf16[512,1152]{1,0:T(8,128)(2,1)}, u32[]{:S(2)}, u32[]{:S(2)}) collective-permute-start(bf16[512,1152]{1,0:T(8,128)(2,1)} %get-tuple-element.95), channel_id=1, source_target_pairs={{0,1},{1,0},{2,3},{3,2},{4,5},{5,4},{6,7},{7,6},{8,9},{9,8},{10,11... | collective-permute-start | bytes 3538952 | tf_op jit(solution)/shard_map/ppermute | solution.py:1565
  585.2 62.0 %all-to-all-start.2 = ((bf16[4,272,1088]{2,1,0:T(8,128)(2,1)}), bf16[4,272,1088]{2,1,0:T(8,128)(2,1)}, u32[]{:S(2)}, u32[]{:S(2)}) async-start(bf16[4,272,1088]{2,1,0:T(8,128)(2,1)} %pair_blocks.1.refs_0_), calls=%async_computation.2 | async-start | bytes 5013504 | tf_op jit(solution)/shard_map/all_to_all | solution.py:1219
  601.5 21.1 %copy-start.21 = (bf16[1280,1088]{1,0:T(8,128)(2,1)S(1)}, bf16[1280,1088]{1,0:T(8,128)(2,1)}, u32[]{:S(2)}) copy-start(bf16[1280,1088]{1,0:T(8,128)(2,1)} %get-tuple-element.62.rows) | copy-start | bytes 8355844
  601.5 21.1 %copy-start.33 = (f32[1280]{0:T(1024)S(1)}, f32[1280]{0:T(1024)}, u32[]{:S(2)}) copy-start(f32[1280]{0:T(1024)} %copy-done.32) | copy-start | bytes 15364
  601.5 21.1 %copy-start.46 = (f32[1280]{0:T(1024)S(1)}, f32[1280]{0:T(1024)}, u32[]{:S(2)}) copy-start(f32[1280]{0:T(1024)} %copy-done.45) | copy-start | bytes 15364
  601.5 21.1 %copy-start.53 = (f32[1088]{0:T(1024)S(1)}, f32[1088]{0:T(1024)}, u32[]{:S(2)}) copy-start(f32[1088]{0:T(1024)} %param.28) | copy-start | bytes 13060
  622.7 15.4 %copy-start.8 = (bf16[1088,1152]{1,0:T(8,128)(2,1)S(1)}, bf16[1088,1152]{1,0:T(8,128)(2,1)}, u32[]{:S(2)}) copy-start(bf16[1088,1152]{1,0:T(8,128)(2,1)} %get-tuple-element.97.out) | copy-start | bytes 7520260
  652.8 108.3 %copy-start.12 = (f32[272,544]{1,0:T(8,128)}, f32[272,544]{1,0:T(8,128)S(1)}, u32[]{:S(2)}) copy-start(f32[272,544]{1,0:T(8,128)S(1)} %copy.108.refs_0_) | copy-start | bytes 1775620
  (40 other events, 196.2 us)

commit v4 on v3

--- a/solution.py
+++ b/solution.py
@@ -1321,19 +1321,20 @@
 
 def far_sums(own, swapped):
     f32, bf16 = jnp.float32, jnp.bfloat16
-    add = lambda d, part: (own[d][part].astype(f32) + swapped[d][part].astype(f32)).astype(bf16)
-    top, bottom = slice(0, ROW_CUT), slice(ROW_CUT, None)
-    return add(3, top), add(3, bottom), add(1, bottom), add(2, top)
+    total = (own[3].astype(f32) + swapped[3].astype(f32)).astype(bf16)
+    return total[:ROW_CUT], total[ROW_CUT:]
 
 
 def far_sends(sums):
-    return across(sums[0], 2), across(sums[1], 1), across(sums[2], 1), across(sums[3], 2)
+    return across(sums[0], 2), across(sums[1], 1)
 
 
 def near_sums(own, swapped, received):
     f32 = jnp.float32
-    beside = own[1][:ROW_CUT].astype(f32) + swapped[1][:ROW_CUT].astype(f32) + received[0].astype(f32)
-    below = own[2][ROW_CUT:].astype(f32) + swapped[2][ROW_CUT:].astype(f32) + received[1].astype(f32)
+    beside = own[1].astype(f32) + swapped[1].astype(f32)
+    below = own[2].astype(f32) + swapped[2].astype(f32)
+    beside = jnp.concatenate([beside[:ROW_CUT] + received[0].astype(f32), beside[ROW_CUT:]], axis=0)
+    below = jnp.concatenate([below[:ROW_CUT], below[ROW_CUT:] + received[1].astype(f32)], axis=0)
     return beside.astype(jnp.bfloat16), below.astype(jnp.bfloat16)
 
 
@@ -1341,12 +1342,10 @@
     return across(sums[0], 1), across(sums[1], 2)
 
 
-def row_total(own, swapped, received, last):
+def row_total(own, swapped, last):
     f32 = jnp.float32
     base = own[0].astype(f32) + swapped[0].astype(f32)
-    beside = jnp.concatenate([last[0], received[2]], axis=0).astype(f32)
-    below = jnp.concatenate([received[3], last[1]], axis=0).astype(f32)
-    return (base + beside + below).astype(jnp.bfloat16)
+    return (base + last[0].astype(f32) + last[1].astype(f32)).astype(jnp.bfloat16)
 
 
 def pack_pair(w_up, w_down):
@@ -1546,7 +1545,7 @@
     deps = ()
     if quick:
         last = after(last[0], grads[0]), last[1]
-        total = row_total(pair_mine, pair_swapped, received, last)
+        total = row_total(pair_mine, pair_swapped, last)
         deps = (total,)
     grads = attention_backward(*inputs, cut, pairs, grads, deps)
     finish_deps, first_deps = (), ()

time: 784 us -> 759 us (0.968)
  waiting for transfers between devices: 67 us -> 39.7 us
    ppermute x10 -> x8, waiting for transfers between devices: 48.3 us -> 21.9 us  [across(): lax.ppermute(value, 'row', [(r, r ^ shift) for r in range(lax.axis_size('...]
    unnamed x124 -> x118, local copies, waits for them, and re-layouts: 26.9 us -> 27 us
  transfers between devices with their start and end apart: 31 -> 29, of which waited for: 8 -> 7; matrix products, arithmetic and copies ran while one was open for 9% -> 10% of each run, Pallas kernels for 31% -> 31%
where the time goes in v4:
time: 759 us; the launch traced here: 749 us
  Pallas kernels  566 us (75%)
  local copies, waits for them, and re-layouts  51 us (7%)
  waiting for transfers between devices  39.7 us (5%)
  matrix products  31.6 us (4%)
  starting transfers between devices  30.8 us (4%)
  other arithmetic  27.4 us (4%)
    pallas_call x1, Pallas kernels, feed_forward(): pl.pallas_call(partial(ffn_kernel, load, len(specs), outs, chunk), grid_s...  125 us
    pallas_call x1, Pallas kernels, end_exchange(): pl.pallas_call(partial(end_kernel, grain), in_specs=[HOLD, pl.BlockSpec(m...  106 us
    pallas_call x1, Pallas kernels, start_exchange(): pl.pallas_call(partial(start_kernel, grain), in_specs=[HOLD] * 3, out_spe...  99.2 us
    pallas_call x2, Pallas kernels, attention_backward(): pl.pallas_call(partial(bwd_kernel, parts, heads, start, len(deps)), grid=...  81.3 us
    pallas_call x3, Pallas kernels, attention_forward(): pl.pallas_call(partial(fwd_kernel, parts, heads, start, len(deps)), grid=...  56.4 us
    pallas_call x3, Pallas kernels, by_rows(): pl.pallas_call(kernel, grid=(5,), in_specs=[block(v.shape[1]) for v in ch...  52.4 us
    unnamed x118, local copies, waits for them, and re-layouts  27 us
    ppermute x8, waiting for transfers between devices, across(): lax.ppermute(value, 'row', [(r, r ^ shift) for r in range(lax.axis_size('...  21.9 us
  transfers between devices with their start and end apart: 29, of which 7 were waited for; matrix products, arithmetic and copies ran while one was open for 10% of the time, Pallas kernels for 31%

profile of v4, /device:TPU:8, one launch (start us, length us, event | category | flops | bytes accessed | tf_op | source)
XLA Modules:
  0.0 749.1 jit_solution(16267737840670005595)
XLA Ops:
  0.7 3.7 copy.132.refs_0_
  6.5 99.2 %start_exchange.1 = (bf16[2,4,4,272,544]{4,3,2,1,0:T(8,128)(2,1)}, bf16[1280,1088]{1,0:T(8,128)(2,1)}, bf16[272,1088]{1,0:T(8,128)(2,1)}) custom-call(bf16[272,544]{1,0:T(8,128)(2,1)} %pad_maximum_fusion.6.pack, bf16[272,1088]{1,0:T(8,128)(2,1)} %concatenate.44.later_pack, bf16[4,320,1088]{2,1,0:T(8,128)(2,1)} %value.1), custom_call_target="tpu_custom_call" | custom-call | flops 99999997952 | tf_op jit(solution)/shard_map/start_exchange/pallas_call | solution.py:608
  105.8 2.7 collective-permute-start.1
  109.2 2.3 convert_reduce_fusion
  112.6 9.0 %assemble_weights.1 = (bf16[1088,3456]{1,0:T(8,128)(2,1)}, bf16[1152,1152]{1,0:T(8,128)(2,1)S(1)}) custom-call(bf16[2,4,4,272,544]{4,3,2,1,0:T(8,128)(2,1)} %get-tuple-element.63.full), custom_call_target="tpu_custom_call" | custom-call | flops 12000000000 | tf_op jit(solution)/shard_map/assemble_weights/pallas_call | solution.py:821
  121.7 16.2 %fusion.1.q_ref.k_ref.v_ref = bf16[1280,3456]{1,0:T(8,128)(2,1)S(1)} fusion(bf16[1088,3456]{1,0:T(8,128)(2,1)} %get-tuple-element.64.weight, f32[3456]{0:T(1024)S(1)} %select_maximum_fusion, f32[3456]{0:T(1024)S(1)} %copy-done.52, bf16[1280,1088]{1,0:T(8,128)(2,1)S(1)} %copy-done.20, f32[1088]{0:T(1024)S(1)} %copy-done.49, f32[1088]{0:T(1024)S(1)} %copy-done.40, ...), kind=kOutput, calls=%fused_computation.5 | convolution fusion | flops 9647554560 | bytes 19199488 | tf_op jit(solution)/shard_map/dot_general | solution.py:21
  137.9 1.7 slice.225
  139.6 2.4 copy-done.16
  142.5 1.7 fusion.23
  144.2 1.6 copy.100.mg_ref
  148.4 2.5 copy.99.mt_ref
  151.0 12.6 %collective-permute-done.2.refs_3_ = bf16[272,1088]{1,0:T(8,128)(2,1)} collective-permute-done((bf16[272,1088]{1,0:T(8,128)(2,1)}, bf16[272,1088]{1,0:T(8,128)(2,1)}, u32[]{:S(2)}, u32[]{:S(2)}) %collective-permute-start.2) | collective-permute-done | bytes 591904 | tf_op jit(solution)/shard_map/ppermute | solution.py:1379
  164.7 3.6 in_order.1.refs_0_.refs_1_.refs_10_
  170.8 4.9 all-to-all-start
  177.0 37.5 %attention_forward.3 = (bf16[1280,1152]{1,0:T(8,128)(2,1)}, f32[1280,1152]{1,0:T(8,128)}) custom-call(bf16[1280,3456]{1,0:T(8,128)(2,1)} %copy-done.16, bf16[1280,3456]{1,0:T(8,128)(2,1)} %copy-done.16, bf16[1280,3456]{1,0:T(8,128)(2,1)} %copy-done.16, bf16[512,2304]{1,0:T(8,128)(2,1)S(1)} %collective-permute-done.12.ko_ref.vo_ref, ...), custom_call_target="tpu_custom_call" | custom-call | flops 39936000000 | bytes 23040000 | tf_op jit(solution)/shard_map/attention_forward/pallas_call | solution.py:112
  214.5 9.3 %collective-permute-done.3.refs_1_.refs_11_ = bf16[4,272,1088]{2,1,0:T(8,128)(2,1)} collective-permute-done((bf16[4,272,1088]{2,1,0:T(8,128)(2,1)}, bf16[4,272,1088]{2,1,0:T(8,128)(2,1)}, u32[]{:S(2)}, u32[]{:S(2)}) %collective-permute-start.3) | collective-permute-done | bytes 2367520 | tf_op jit(solution)/shard_map/ppermute | solution.py:1303
  229.0 13.8 %attention_forward.4 = (bf16[1280,1152]{1,0:T(8,128)(2,1)}, f32[1280,1152]{1,0:T(8,128)}) custom-call(bf16[1280,3456]{1,0:T(8,128)(2,1)} %copy-done.16, bf16[1280,3456]{1,0:T(8,128)(2,1)} %copy-done.16, bf16[1280,3456]{1,0:T(8,128)(2,1)} %copy-done.16, bf16[512,2304]{1,0:T(8,128)(2,1)} %copy-done, ...), custom_call_target="tpu_custom_call", output_to_operand_aliasing={{0}: (7, {}), {1}: (8, {})} | custom-call | flops 13312000000 | bytes 23040000 | tf_op jit(solution)/shard_map/attention_forward/pallas_call | solution.py:112
  242.8 9.9 %collective-permute-done.5.refs_2_.refs_3_.refs_13_ = bf16[2,272,1088]{2,1,0:T(8,128)(2,1)S(1)} collective-permute-done((bf16[2,272,1088]{2,1,0:T(8,128)(2,1)S(1)}, bf16[2,272,1088]{2,1,0:T(8,128)(2,1)S(1)}, u32[]{:S(2)}, u32[]{:S(2)}) %collective-permute-start.5) | collective-permute-done | bytes 1183776 | tf_op jit(solution)/shard_map/ppermute | solution.py:1303
  252.7 2.7 collective-permute-done.6.refs_3_.refs_4_.refs_14_
  255.4 5.1 attention_forward.5
  265.5 1.8 collective-permute-done.13
  268.9 10.1 %project_out.1 = (f32[1280,1088]{1,0:T(8,128)}, bf16[1280,1088]{1,0:T(8,128)(2,1)}) custom-call(bf16[1280,1152]{1,0:T(8,128)(2,1)} %get-tuple-element.69.mixed.refs_1_.o_ref, bf16[1280,1088]{1,0:T(8,128)(2,1)} %get-tuple-element.62.rows, bf16[1152,1152]{1,0:T(8,128)(2,1)} %copy-done.15, f32[1,1088]{1,0:T(1,128)} %reshape.579.bias, f32[1,1088]{1,0:T(1,128)} %reshape.580.gain, ...), custom_call_target="tpu_custom_call" | custom-call | flops 12000000000 | tf_op jit(solution)/shard_map/project_out/pallas_call | solution.py:945
  279.0 3.8 spread_rows.1.refs_21_.seed
  282.8 1.6 copy-done.4
  284.5 125.5 %feed_forward.1 = (f32[1280,1088]{1,0:T(8,128)}, f32[1280,1088]{1,0:T(8,128)}, f32[1,4352]{1,0:T(1,128)}, bf16[272,4352]{1,0:T(8,128)(2,1)}, bf16[272,4352]{1,0:...) custom-call(s32[6]{0:T(128)} %stack.46.scalars, ...), custom_call_target="tpu_custom_call" | custom-call | flops 145458462720 | bytes 65732608 | tf_op jit(solution)/shard_map/feed_forward/pallas_call | solution.py:465
  411.7 3.1 collective-permute-done.14
  414.8 2.3 add_convert_fusion.1
  422.1 22.1 %middle_back.1 = (bf16[1280,1088]{1,0:T(8,128)(2,1)}, f32[1280,1088]{1,0:T(8,128)}, bf16[1280,1152]{1,0:T(8,128)(2,1)}, f32[4,1088]{1,0:T(4,128)}, bf16[1088,1152]{1,0:T(8,128)(2,1)}) custom-call(f32[1280,1088]{1,0:T(8,128)} %get-tuple-element.72.second_grad, f32[1280,1088]{1,0:T(8,128)} %get-tuple-element.73.lowered, ...), custom_call_target="tpu_custom_call" | custom-call | flops 24999999488 | tf_op jit(solution)/shard_map/middle_back/pallas_call | solution.py:945
  444.2 2.1 convert_add_fusion.1
  446.6 1.6 copy-done.5
  451.5 1.6 pad_maximum_fusion.refs_1_
  458.4 4.4 collect_rows.1
  462.8 5.0 all-to-all-start.1
  467.9 46.9 %attention_backward.2 = (bf16[1280,1152]{1,0:T(8,128)(2,1)}, bf16[1280,1152]{1,0:T(8,128)(2,1)}, bf16[1280,1152]{1,0:T(8,128)(2,1)}, bf16[512,1152]{1,0:T(8,128)(2,1)}, bf16[512,1152]{1,0:T(8,128)(2,1)}) custom-call(bf16[1280,3456]{1,0:T(8,128)(2,1)} %copy-done.16, bf16[1280,3456]{1,0:T(8,128)(2,1)} %copy-done.16, bf16[1280,3456]{1,0:T(8,128)(2,1)} %copy-done.16, ...), custom_call_target="tpu_custom_call" | custom-call | flops 6400000000 | bytes 46080000 | tf_op jit(solution)/shard_map/attention_backward/pallas_call | solution.py:251
  514.8 4.9 add_convert_fusion.refs_5_.total.total_tail
  521.2 34.3 %attention_backward.3 = (bf16[1280,1152]{1,0:T(8,128)(2,1)}, bf16[1280,1152]{1,0:T(8,128)(2,1)}, bf16[1280,1152]{1,0:T(8,128)(2,1)}, bf16[512,1152]{1,0:T(8,128)(2,1)}, bf16[512,1152]{1,0:T(8,128)(2,1)}) custom-call(bf16[1280,3456]{1,0:T(8,128)(2,1)} %copy-done.16, ...), custom_call_target="tpu_custom_call", output_to_operand_aliasing={{0}: (10, {}), {1}: (11, {}), {2}: (12, {}), {3}: (13, {}),... | custom-call | flops 5120000000 | bytes 46080000 | tf_op jit(solution)/shard_map/attention_backward/pallas_call | solution.py:251
  556.9 4.4 pair_blocks.1.refs_0_
  561.3 4.9 all-to-all-start.2
  566.4 11.2 %finish_gradients.1 = (bf16[1280,3456]{1,0:T(8,128)(2,1)}, f32[1,3456]{1,0:T(1,128)S(1)}) custom-call(bf16[1280,1152]{1,0:T(8,128)(2,1)} %get-tuple-element.91.dq, bf16[1280,1152]{1,0:T(8,128)(2,1)} %get-tuple-element.92.dk, bf16[1280,1152]{1,0:T(8,128)(2,1)} %get-tuple-element.93.dv, bf16[512,1152]{1,0:T(8,128)(2,1)} %collective-permute-done.23.other_k, ...), custom_call_target="tpu_custom_call" | custom-call | flops 1000000000 | tf_op jit(solution)/shard_map/finish_gradients/pallas_call | solution.py:898
  577.7 20.2 %first_back.1 = (bf16[1280,1088]{1,0:T(8,128)(2,1)}, f32[2,1088]{1,0:T(2,128)}) custom-call(bf16[1280,3456]{1,0:T(8,128)(2,1)} %get-tuple-element.96.triple_grad, bf16[1280,1088]{1,0:T(8,128)(2,1)} %get-tuple-element.62.rows, f32[1280,1088]{1,0:T(8,128)} %get-tuple-element.98.middle_grad, bf16[1088,3456]{1,0:T(8,128)(2,1)} %get-tuple-element.64.weight, ...), custom_call_target="tpu_custom_call" | custom-call | flops 4000000000 | tf_op jit(solution)/shard_map/first_back/pallas_call | solution.py:945
  598.8 15.4 %convolution_convert_fusion.triple = bf16[1088,3456]{1,0:T(8,128)(2,1)} fusion(bf16[1280,3456]{1,0:T(8,128)(2,1)} %get-tuple-element.96.triple_grad, bf16[1280,1088]{1,0:T(8,128)(2,1)S(1)} %copy-done.21, f32[1088]{0:T(1024)S(1)} %copy-done.50, f32[1088]{0:T(1024)S(1)} %copy-done.41, f32[1280]{0:T(1024)S(1)} %copy-done.43, f32[1280]{0:T(1024)S(1)} %copy-done.30), kind=kOutput, calls=%fused_computation.6 | convolution fusion | flops 9638043648 | bytes 19171840 | tf_op jit(solution)/shard_map/dot_general | solution.py:29
  614.2 9.2 %divide_gradients.1.grads = bf16[2,4,4,272,544]{4,3,2,1,0:T(8,128)(2,1)} custom-call(bf16[1088,3456]{1,0:T(8,128)(2,1)} %convolution_convert_fusion.triple, bf16[1088,1152]{1,0:T(8,128)(2,1)S(1)} %copy-done.8), custom_call_target="tpu_custom_call" | custom-call | flops 1000000000 | tf_op jit(solution)/shard_map/divide_gradients/pallas_call | solution.py:852
  623.4 2.2 convert_reduce_fusion.1
  629.0 2.1 copy-done.14
  631.1 106.2 %end_exchange.1 = (f32[272,544]{1,0:T(8,128)S(1)}, f32[104,128]{1,0:T(8,128)S(1)}, bf16[4,320,1088]{2,1,0:T(8,128)(2,1)S(1)}) custom-call(bf16[2,4,4,272,544]{4,3,2,1,0:T(8,128)(2,1)} %divide_gradients.1.grads, f32[104,128]{1,0:T(8,128)S(1)} %pad_bitcast_fusion.small, bf16[1280,1088]{1,0:T(8,128)(2,1)S(1)} %copy-done.14, f32[272,544]{1,0:T(8,128)S(1)} %copy.108.refs_0_, ...), custom_call_target="tpu_custom_call" | custom-call | flops 99999997952 | tf_op jit(solution)/shard_map/end_exchange/pallas_call | solution.py:758
  737.3 1.6 copy-done.6
  743.3 3.8 copy.133
  747.1 1.6 copy.134
  (241 shorter events, 50.7 us)
Async XLA Ops:
  105.7 45.3 %collective-permute-start = (bf16[272,1088]{1,0:T(8,128)(2,1)}, bf16[272,1088]{1,0:T(8,128)(2,1)}, u32[]{:S(2)}, u32[]{:S(2)}) collective-permute-start(bf16[272,1088]{1,0:T(8,128)(2,1)} %get-tuple-element.61.refs_0_), channel_id=1, source_target_pairs={{0,2},{1,3},{2,0},{3,1},{4,6},{5,7},{6,4},{7,5},{8,10},{9,11},{10,... | collective-permute-start | bytes 1775624 | tf_op jit(solution)/shard_map/ppermute | solution.py:1379
  105.8 45.2 %collective-permute-start.1 = (bf16[272,1088]{1,0:T(8,128)(2,1)}, bf16[272,1088]{1,0:T(8,128)(2,1)}, u32[]{:S(2)}, u32[]{:S(2)}) collective-permute-start(bf16[272,1088]{1,0:T(8,128)(2,1)} %get-tuple-element.61.refs_0_), channel_id=1, source_target_pairs={{0,4},{1,5},{2,6},{3,7},{4,0},{5,1},{6,2},{7,3},{8,12},{9,13},{10,... | collective-permute-start | bytes 1775624 | tf_op jit(solution)/shard_map/ppermute | solution.py:1379
  108.4 55.2 %collective-permute-start.2 = (bf16[272,1088]{1,0:T(8,128)(2,1)}, bf16[272,1088]{1,0:T(8,128)(2,1)}, u32[]{:S(2)}, u32[]{:S(2)}) collective-permute-start(bf16[272,1088]{1,0:T(8,128)(2,1)} %get-tuple-element.61.refs_0_), channel_id=1, source_target_pairs={{0,6},{1,7},{2,4},{3,5},{4,2},{5,3},{6,0},{7,1},{8,14},{9,15},{10,... | collective-permute-start | bytes 1775624 | tf_op jit(solution)/shard_map/ppermute | solution.py:1379
  111.6 10.1 %copy-start.29 = (f32[1280]{0:T(1024)}, f32[1280]{0:T(1024)S(1)}, u32[]{:S(2)}) copy-start(f32[1280]{0:T(1024)S(1)} %broadcast_multiply_fusion.1) | copy-start | bytes 15364
  112.5 9.1 %copy-start.42 = (f32[1280]{0:T(1024)}, f32[1280]{0:T(1024)S(1)}, u32[]{:S(2)}) copy-start(f32[1280]{0:T(1024)S(1)} %add_rsqrt_fusion) | copy-start | bytes 15364
  112.6 9.1 %copy-start.40 = (f32[1088]{0:T(1024)S(1)}, f32[1088]{0:T(1024)}, u32[]{:S(2)}) copy-start(f32[1088]{0:T(1024)} %param.27) | copy-start | bytes 13060
  112.6 9.1 %copy-start.49 = (f32[1088]{0:T(1024)S(1)}, f32[1088]{0:T(1024)}, u32[]{:S(2)}) copy-start(f32[1088]{0:T(1024)} %param.28) | copy-start | bytes 13060
  112.6 9.1 %copy-start.52 = (f32[3456]{0:T(1024)S(1)}, f32[3456]{0:T(1024)}, u32[]{:S(2)}) copy-start(f32[3456]{0:T(1024)} %constant.175.clone.1) | copy-start | bytes 41476
  121.6 16.3 %copy-start.15 = (bf16[1152,1152]{1,0:T(8,128)(2,1)}, bf16[1152,1152]{1,0:T(8,128)(2,1)S(1)}, u32[]{:S(2)}) copy-start(bf16[1152,1152]{1,0:T(8,128)(2,1)S(1)} %get-tuple-element.70.weight) | copy-start | bytes 7962628
  141.9 33.8 %collective-permute-start.12 = (bf16[512,2304]{1,0:T(8,128)(2,1)}, bf16[512,2304]{1,0:T(8,128)(2,1)S(1)}, u32[]{:S(2)}, u32[]{:S(2)}) collective-permute-start(bf16[512,2304]{1,0:T(8,128)(2,1)} %slice.225), channel_id=1, source_target_pairs={{0,1},{1,0},{2,3},{3,2},{4,5},{5,4},{6,7},{7,6},{8,9},{9,8},{10,11... | collective-permute-start | bytes 7077896 | tf_op jit(solution)/shard_map/ppermute | solution.py:1504
  168.3 55.5 %collective-permute-start.3 = (bf16[4,272,1088]{2,1,0:T(8,128)(2,1)}, bf16[4,272,1088]{2,1,0:T(8,128)(2,1)}, u32[]{:S(2)}, u32[]{:S(2)}) collective-permute-start(bf16[4,272,1088]{2,1,0:T(8,128)(2,1)} %in_order.1.refs_0_.refs_1_.refs_10_), channel_id=1, source_target_pairs={{0,8},{8,0},{16,24},{24,16},{1,9},{9,1},{17,25},{25,17},{2,10},{10... | collective-permute-start | bytes 7102472 | tf_op jit(solution)/shard_map/ppermute | solution.py:1303
  169.8 57.0 %collective-permute-start.4 = (bf16[4,272,1088]{2,1,0:T(8,128)(2,1)}, bf16[4,272,1088]{2,1,0:T(8,128)(2,1)}, u32[]{:S(2)}, u32[]{:S(2)}) collective-permute-start(bf16[4,272,1088]{2,1,0:T(8,128)(2,1)} %in_order.1.refs_0_.refs_1_.refs_10_), channel_id=1, source_target_pairs={{0,16},{8,24},{16,0},{24,8},{1,17},{9,25},{17,1},{25,9},{2,18},{10... | collective-permute-start | bytes 7102472 | tf_op jit(solution)/shard_map/ppermute | solution.py:1303
  170.8 90.7 %all-to-all-start = ((bf16[4,320,1088]{2,1,0:T(8,128)(2,1)}), bf16[4,320,1088]{2,1,0:T(8,128)(2,1)}, u32[]{:S(2)}, u32[]{:S(2)}) async-start(bf16[4,320,1088]{2,1,0:T(8,128)(2,1)} %after.3), calls=%async_computation | async-start | bytes 5898240 | tf_op jit(solution)/shard_map/all_to_all | solution.py:1219
  177.0 37.5 %copy-start = (bf16[512,2304]{1,0:T(8,128)(2,1)}, bf16[512,2304]{1,0:T(8,128)(2,1)S(1)}, u32[]{:S(2)}) copy-start(bf16[512,2304]{1,0:T(8,128)(2,1)S(1)} %collective-permute-done.12.ko_ref.vo_ref) | copy-start | bytes 7077892
  214.5 14.5 %copy-start.3 = (f32[2,256,512]{2,1,0:T(8,128)S(1)}, f32[2,256,512]{2,1,0:T(8,128)}, u32[]{:S(2)}) copy-start(f32[2,256,512]{2,1,0:T(8,128)} %copy.99.mt_ref) | copy-start | bytes 3145732
  225.2 27.5 %collective-permute-start.5 = (bf16[2,272,1088]{2,1,0:T(8,128)(2,1)S(1)}, bf16[2,272,1088]{2,1,0:T(8,128)(2,1)S(1)}, u32[]{:S(2)}, u32[]{:S(2)}) collective-permute-start(bf16[2,272,1088]{2,1,0:T(8,128)(2,1)S(1)} %slice.223.refs_2_), channel_id=1, source_target_pairs={{0,16},{8,24},{16,0},{24,8},{1,17},{9,25},{17,1},{25,9},{2,18},{10... | collective-permute-start | bytes 3551240 | tf_op jit(solution)/shard_map/ppermute | solution.py:1303
  228.2 27.2 %collective-permute-start.6 = (bf16[2,272,1088]{2,1,0:T(8,128)(2,1)S(1)}, bf16[2,272,1088]{2,1,0:T(8,128)(2,1)S(1)}, u32[]{:S(2)}, u32[]{:S(2)}) collective-permute-start(bf16[2,272,1088]{2,1,0:T(8,128)(2,1)S(1)} %slice.224.refs_3_), channel_id=1, source_target_pairs={{0,8},{8,0},{16,24},{24,16},{1,9},{9,1},{17,25},{25,17},{2,10},{10... | collective-permute-start | bytes 3551240 | tf_op jit(solution)/shard_map/ppermute | solution.py:1303
  252.7 12.7 %copy-start.9 = (bf16[2,272,1088]{2,1,0:T(8,128)(2,1)}, bf16[2,272,1088]{2,1,0:T(8,128)(2,1)S(1)}, u32[]{:S(2)}) copy-start(bf16[2,272,1088]{2,1,0:T(8,128)(2,1)S(1)} %collective-permute-done.5.refs_2_.refs_3_.refs_13_) | copy-start | bytes 3551236
  261.6 5.8 collective-permute-start.13
  261.7 22.8 %collective-permute-start.7 = (bf16[4,272,1088]{2,1,0:T(8,128)(2,1)}, bf16[4,272,1088]{2,1,0:T(8,128)(2,1)}, u32[]{:S(2)}, u32[]{:S(2)}) collective-permute-start(bf16[4,272,1088]{2,1,0:T(8,128)(2,1)} %in_order.1.refs_0_.refs_1_.refs_10_), channel_id=1, source_target_pairs={{0,1},{1,0},{2,3},{3,2},{4,5},{5,4},{6,7},{7,6},{8,9},{9,8},{10,11... | collective-permute-start | bytes 7102472 | tf_op jit(solution)/shard_map/ppermute | solution.py:1319
  262.2 22.3 %collective-permute-start.8 = (bf16[4,272,1088]{2,1,0:T(8,128)(2,1)}, bf16[4,272,1088]{2,1,0:T(8,128)(2,1)}, u32[]{:S(2)}, u32[]{:S(2)}) collective-permute-start(bf16[4,272,1088]{2,1,0:T(8,128)(2,1)} %collective-permute-done.3.refs_1_.refs_11_), channel_id=1, source_target_pairs={{0,1},{1,0},{2,3},{3,2},{4,5},{5,4},{6,7},{7,6},{8,9},{9,8},{10,11... | collective-permute-start | bytes 7102472 | tf_op jit(solution)/shard_map/ppermute | solution.py:1319
  262.2 22.2 %collective-permute-start.9 = (bf16[4,272,1088]{2,1,0:T(8,128)(2,1)}, bf16[4,272,1088]{2,1,0:T(8,128)(2,1)}, u32[]{:S(2)}, u32[]{:S(2)}) collective-permute-start(bf16[4,272,1088]{2,1,0:T(8,128)(2,1)} %collective-permute-done.4.refs_2_.refs_12_), channel_id=1, source_target_pairs={{0,1},{1,0},{2,3},{3,2},{4,5},{5,4},{6,7},{7,6},{8,9},{9,8},{10,11... | collective-permute-start | bytes 7102472 | tf_op jit(solution)/shard_map/ppermute | solution.py:1319
  265.4 19.1 %collective-permute-start.10 = (bf16[2,272,1088]{2,1,0:T(8,128)(2,1)S(1)}, bf16[2,272,1088]{2,1,0:T(8,128)(2,1)}, u32[]{:S(2)}, u32[]{:S(2)}) collective-permute-start(bf16[2,272,1088]{2,1,0:T(8,128)(2,1)S(1)} %collective-permute-done.5.refs_2_.refs_3_.refs_13_), channel_id=1, source_target_pairs={{0,1},{1,0},{2,3},{3,2},{4,5},{5,4},{6,7},{7,6},{8,9},{9,8},{10,11... | collective-permute-start | bytes 3551240 | tf_op jit(solution)/shard_map/ppermute | solution.py:1319
  267.4 17.1 %collective-permute-start.11 = (bf16[2,272,1088]{2,1,0:T(8,128)(2,1)S(1)}, bf16[2,272,1088]{2,1,0:T(8,128)(2,1)}, u32[]{:S(2)}, u32[]{:S(2)}) collective-permute-start(bf16[2,272,1088]{2,1,0:T(8,128)(2,1)S(1)} %copy-done.11), channel_id=1, source_target_pairs={{0,1},{1,0},{2,3},{3,2},{4,5},{5,4},{6,7},{7,6},{8,9},{9,8},{10,11... | collective-permute-start | bytes 3551240 | tf_op jit(solution)/shard_map/ppermute | solution.py:1319
  284.5 126.1 %copy-start.39 = (f32[1088]{0:T(1024)S(1)}, f32[1088]{0:T(1024)}, u32[]{:S(2)}) copy-start(f32[1088]{0:T(1024)} %param.39) | copy-start | bytes 13060
  410.0 4.8 collective-permute-start.14
  410.4 11.2 %collective-permute-start.18 = (bf16[272,4352]{1,0:T(8,128)(2,1)}, bf16[272,4352]{1,0:T(8,128)(2,1)S(1)}, u32[]{:S(2)}, u32[]{:S(2)}) collective-permute-start(bf16[272,4352]{1,0:T(8,128)(2,1)} %get-tuple-element.83), channel_id=1, source_target_pairs={{0,1},{1,0},{2,3},{3,2},{4,5},{5,4},{6,7},{7,6},{8,9},{9,8},{10,11... | collective-permute-start | bytes 7102472 | tf_op jit(solution)/shard_map/ppermute | solution.py:1319
  411.1 33.1 %collective-permute-start.16 = (bf16[272,4352]{1,0:T(8,128)(2,1)}, bf16[272,4352]{1,0:T(8,128)(2,1)}, u32[]{:S(2)}, u32[]{:S(2)}) collective-permute-start(bf16[272,4352]{1,0:T(8,128)(2,1)} %get-tuple-element.81), channel_id=1, source_target_pairs={{0,1},{1,0},{2,3},{3,2},{4,5},{5,4},{6,7},{7,6},{8,9},{9,8},{10,11... | collective-permute-start | bytes 7102472 | tf_op jit(solution)/shard_map/ppermute | solution.py:1319
  411.5 103.3 %collective-permute-start.20 = (bf16[272,4352]{1,0:T(8,128)(2,1)}, bf16[272,4352]{1,0:T(8,128)(2,1)}, u32[]{:S(2)}, u32[]{:S(2)}) collective-permute-start(bf16[272,4352]{1,0:T(8,128)(2,1)} %get-tuple-element.90), channel_id=1, source_target_pairs={{0,1},{1,0},{2,3},{3,2},{4,5},{5,4},{6,7},{7,6},{8,9},{9,8},{10,11... | collective-permute-start | bytes 7102472 | tf_op jit(solution)/shard_map/ppermute | solution.py:1319
  419.3 29.2 %collective-permute-start.19 = (bf16[128,4352]{1,0:T(8,128)(2,1)}, bf16[128,4352]{1,0:T(8,128)(2,1)}, u32[]{:S(2)}, u32[]{:S(2)}) collective-permute-start(bf16[128,4352]{1,0:T(8,128)(2,1)} %slice.229.refs_1_), channel_id=1, source_target_pairs={{0,8},{8,0},{16,24},{24,16},{1,9},{9,1},{17,25},{25,17},{2,10},{10... | collective-permute-start | bytes 3342344 | tf_op jit(solution)/shard_map/ppermute | solution.py:1303
  419.9 30.1 %collective-permute-start.17 = (bf16[144,4352]{1,0:T(8,128)(2,1)}, bf16[144,4352]{1,0:T(8,128)(2,1)}, u32[]{:S(2)}, u32[]{:S(2)}) collective-permute-start(bf16[144,4352]{1,0:T(8,128)(2,1)} %slice.228.refs_0_), channel_id=1, source_target_pairs={{0,16},{8,24},{16,0},{24,8},{1,17},{9,25},{17,1},{25,9},{2,18},{10... | collective-permute-start | bytes 3760136 | tf_op jit(solution)/shard_map/ppermute | solution.py:1303
  422.1 22.2 %copy-start.22 = (bf16[272,4352]{1,0:T(8,128)(2,1)S(1)}, bf16[272,4352]{1,0:T(8,128)(2,1)}, u32[]{:S(2)}) copy-start(bf16[272,4352]{1,0:T(8,128)(2,1)} %get-tuple-element.80) | copy-start | bytes 7102468
  448.2 10.2 %collective-permute-start.15 = (bf16[20,64,1088]{2,1,0:T(8,128)(2,1)S(1)}, bf16[20,64,1088]{2,1,0:T(8,128)(2,1)}, u32[]{:S(2)}, u32[]{:S(2)}) collective-permute-start(bf16[20,64,1088]{2,1,0:T(8,128)(2,1)S(1)} %bitcast.38), channel_id=1, source_target_pairs={{0,1},{1,0},{2,3},{3,2},{4,5},{5,4},{6,7},{7,6},{8,9},{9,8},{10,11... | collective-permute-start | bytes 8355848 | tf_op jit(solution)/shard_map/ppermute | solution.py:1239
  453.1 61.7 %collective-permute-start.21 = (bf16[272,4352]{1,0:T(8,128)(2,1)}, bf16[272,4352]{1,0:T(8,128)(2,1)}, u32[]{:S(2)}, u32[]{:S(2)}) collective-permute-start(bf16[272,4352]{1,0:T(8,128)(2,1)} %pad_maximum_fusion.refs_1_), channel_id=1, source_target_pairs={{0,8},{8,0},{16,24},{24,16},{1,9},{9,1},{17,25},{25,17},{2,10},{10... | collective-permute-start | bytes 7102472 | tf_op jit(solution)/shard_map/ppermute | solution.py:1303
  455.9 58.9 %collective-permute-start.22 = (bf16[272,4352]{1,0:T(8,128)(2,1)}, bf16[272,4352]{1,0:T(8,128)(2,1)}, u32[]{:S(2)}, u32[]{:S(2)}) collective-permute-start(bf16[272,4352]{1,0:T(8,128)(2,1)} %pad_maximum_fusion.1.refs_2_), channel_id=1, source_target_pairs={{0,16},{8,24},{16,0},{24,8},{1,17},{9,25},{17,1},{25,9},{2,18},{10... | collective-permute-start | bytes 7102472 | tf_op jit(solution)/shard_map/ppermute | solution.py:1303
  462.8 98.5 %all-to-all-start.1 = ((bf16[4,320,1088]{2,1,0:T(8,128)(2,1)}), bf16[4,320,1088]{2,1,0:T(8,128)(2,1)}, u32[]{:S(2)}, u32[]{:S(2)}) async-start(bf16[4,320,1088]{2,1,0:T(8,128)(2,1)} %bitcast.19.refs_0_), calls=%async_computation.1 | async-start | bytes 5898240 | tf_op jit(solution)/shard_map/all_to_all | solution.py:1219
  519.8 37.2 %collective-permute-start.25 = (bf16[272,4352]{1,0:T(8,128)(2,1)S(1)}, bf16[272,4352]{1,0:T(8,128)(2,1)}, u32[]{:S(2)}, u32[]{:S(2)}) collective-permute-start(bf16[272,4352]{1,0:T(8,128)(2,1)S(1)} %add_convert_fusion.refs_5_.total.total_tail), channel_id=1, source_target_pairs={{0,1},{1,0},{2,3},{3,2},{4,5},{5,4},{6,7},{7,6},{8,9},{9,8},{10,11... | collective-permute-start | bytes 7102472 | tf_op jit(solution)/shard_map/ppermute | solution.py:1319
  521.2 34.9 %copy-start.41 = (f32[1088]{0:T(1024)S(1)}, f32[1088]{0:T(1024)}, u32[]{:S(2)}) copy-start(f32[1088]{0:T(1024)} %param.27) | copy-start | bytes 13060
  521.2 35.5 %copy-start.33 = (f32[1,4352]{1,0:T(1,128)S(1)}, f32[1,4352]{1,0:T(1,128)}, u32[]{:S(2)}) copy-start(f32[1,4352]{1,0:T(1,128)} %get-tuple-element.102) | copy-start | bytes 52228
  555.6 10.8 %collective-permute-start.23 = (bf16[512,1152]{1,0:T(8,128)(2,1)}, bf16[512,1152]{1,0:T(8,128)(2,1)}, u32[]{:S(2)}, u32[]{:S(2)}) collective-permute-start(bf16[512,1152]{1,0:T(8,128)(2,1)} %get-tuple-element.94), channel_id=1, source_target_pairs={{0,1},{1,0},{2,3},{3,2},{4,5},{5,4},{6,7},{7,6},{8,9},{9,8},{10,11... | collective-permute-start | bytes 3538952 | tf_op jit(solution)/shard_map/ppermute | solution.py:1564
  555.7 10.7 %collective-permute-start.24 = (bf16[512,1152]{1,0:T(8,128)(2,1)}, bf16[512,1152]{1,0:T(8,128)(2,1)}, u32[]{:S(2)}, u32[]{:S(2)}) collective-permute-start(bf16[512,1152]{1,0:T(8,128)(2,1)} %get-tuple-element.95), channel_id=1, source_target_pairs={{0,1},{1,0},{2,3},{3,2},{4,5},{5,4},{6,7},{7,6},{8,9},{9,8},{10,11... | collective-permute-start | bytes 3538952 | tf_op jit(solution)/shard_map/ppermute | solution.py:1564
  561.3 62.1 %all-to-all-start.2 = ((bf16[4,272,1088]{2,1,0:T(8,128)(2,1)}), bf16[4,272,1088]{2,1,0:T(8,128)(2,1)}, u32[]{:S(2)}, u32[]{:S(2)}) async-start(bf16[4,272,1088]{2,1,0:T(8,128)(2,1)} %pair_blocks.1.refs_0_), calls=%async_computation.2 | async-start | bytes 5013504 | tf_op jit(solution)/shard_map/all_to_all | solution.py:1219
  577.6 21.1 %copy-start.21 = (bf16[1280,1088]{1,0:T(8,128)(2,1)S(1)}, bf16[1280,1088]{1,0:T(8,128)(2,1)}, u32[]{:S(2)}) copy-start(bf16[1280,1088]{1,0:T(8,128)(2,1)} %get-tuple-element.62.rows) | copy-start | bytes 8355844
  577.6 21.1 %copy-start.30 = (f32[1280]{0:T(1024)S(1)}, f32[1280]{0:T(1024)}, u32[]{:S(2)}) copy-start(f32[1280]{0:T(1024)} %copy-done.29) | copy-start | bytes 15364
  577.7 21.1 %copy-start.43 = (f32[1280]{0:T(1024)S(1)}, f32[1280]{0:T(1024)}, u32[]{:S(2)}) copy-start(f32[1280]{0:T(1024)} %copy-done.42) | copy-start | bytes 15364
  577.7 21.1 %copy-start.50 = (f32[1088]{0:T(1024)S(1)}, f32[1088]{0:T(1024)}, u32[]{:S(2)}) copy-start(f32[1088]{0:T(1024)} %param.28) | copy-start | bytes 13060
  598.8 15.4 %copy-start.8 = (bf16[1088,1152]{1,0:T(8,128)(2,1)S(1)}, bf16[1088,1152]{1,0:T(8,128)(2,1)}, u32[]{:S(2)}) copy-start(bf16[1088,1152]{1,0:T(8,128)(2,1)} %get-tuple-element.97.out) | copy-start | bytes 7520260
  629.0 108.3 %copy-start.12 = (f32[272,544]{1,0:T(8,128)}, f32[272,544]{1,0:T(8,128)S(1)}, u32[]{:S(2)}) copy-start(f32[272,544]{1,0:T(8,128)S(1)} %copy.108.refs_0_) | copy-start | bytes 1775620
  (35 other events, 129.6 us)

commit v5 on v4

--- a/solution.py
+++ b/solution.py
@@ -651,7 +651,6 @@
         copy.start()
         sends.append(copy)
     small_col[col] = small[...]
-    own.wait()
     f32 = jnp.float32
     each = tokens.shape[1] // grain
 
@@ -676,6 +675,7 @@
                     pltpu.make_async_copy(source, target, x_recv).start()
 
     each_chunk(lambda copy: copy.start(), True)
+    own.wait()
 
     def add(target, source):
         target[...] = (target[...].astype(f32) + source[...].astype(f32)).astype(target.dtype)

time: 759 us -> 759 us (level)
  no operation moved by 1% of the time
where the time goes in v5:
time: 759 us; the launch traced here: 749 us
  Pallas kernels  566 us (75%)
  local copies, waits for them, and re-layouts  51 us (7%)
  waiting for transfers between devices  39.7 us (5%)
  matrix products  31.6 us (4%)
  starting transfers between devices  30.8 us (4%)
  other arithmetic  27.4 us (4%)
    pallas_call x1, Pallas kernels, feed_forward(): pl.pallas_call(partial(ffn_kernel, load, len(specs), outs, chunk), grid_s...  125 us
    pallas_call x1, Pallas kernels, end_exchange(): pl.pallas_call(partial(end_kernel, grain), in_specs=[HOLD, pl.BlockSpec(m...  106 us
    pallas_call x1, Pallas kernels, start_exchange(): pl.pallas_call(partial(start_kernel, grain), in_specs=[HOLD] * 3, out_spe...  99.2 us
    pallas_call x2, Pallas kernels, attention_backward(): pl.pallas_call(partial(bwd_kernel, parts, heads, start, len(deps)), grid=...  81.3 us
    pallas_call x3, Pallas kernels, attention_forward(): pl.pallas_call(partial(fwd_kernel, parts, heads, start, len(deps)), grid=...  56.4 us
    pallas_call x3, Pallas kernels, by_rows(): pl.pallas_call(kernel, grid=(5,), in_specs=[block(v.shape[1]) for v in ch...  52.4 us
    unnamed x118, local copies, waits for them, and re-layouts  27 us
    ppermute x8, waiting for transfers between devices, across(): lax.ppermute(value, 'row', [(r, r ^ shift) for r in range(lax.axis_size('...  21.9 us
  transfers between devices with their start and end apart: 29, of which 7 were waited for; matrix products, arithmetic and copies ran while one was open for 10% of the time, Pallas kernels for 31%

profile of v5, /device:TPU:8, one launch (start us, length us, event | category | flops | bytes accessed | tf_op | source)
XLA Modules:
  0.0 749.1 jit_solution(18146049394772803926)
XLA Ops:
  0.7 3.7 copy.132.refs_0_
  6.5 99.2 %start_exchange.1 = (bf16[2,4,4,272,544]{4,3,2,1,0:T(8,128)(2,1)}, bf16[1280,1088]{1,0:T(8,128)(2,1)}, bf16[272,1088]{1,0:T(8,128)(2,1)}) custom-call(bf16[272,544]{1,0:T(8,128)(2,1)} %pad_maximum_fusion.6.pack, bf16[272,1088]{1,0:T(8,128)(2,1)} %concatenate.44.later_pack, bf16[4,320,1088]{2,1,0:T(8,128)(2,1)} %value.1), custom_call_target="tpu_custom_call" | custom-call | flops 99999997952 | tf_op jit(solution)/shard_map/start_exchange/pallas_call | solution.py:608
  105.8 2.7 collective-permute-start.1
  109.2 2.3 convert_reduce_fusion
  112.6 9.0 %assemble_weights.1 = (bf16[1088,3456]{1,0:T(8,128)(2,1)}, bf16[1152,1152]{1,0:T(8,128)(2,1)S(1)}) custom-call(bf16[2,4,4,272,544]{4,3,2,1,0:T(8,128)(2,1)} %get-tuple-element.63.full), custom_call_target="tpu_custom_call" | custom-call | flops 12000000000 | tf_op jit(solution)/shard_map/assemble_weights/pallas_call | solution.py:821
  121.7 16.2 %fusion.1.q_ref.k_ref.v_ref = bf16[1280,3456]{1,0:T(8,128)(2,1)S(1)} fusion(bf16[1088,3456]{1,0:T(8,128)(2,1)} %get-tuple-element.64.weight, f32[3456]{0:T(1024)S(1)} %select_maximum_fusion, f32[3456]{0:T(1024)S(1)} %copy-done.52, bf16[1280,1088]{1,0:T(8,128)(2,1)S(1)} %copy-done.20, f32[1088]{0:T(1024)S(1)} %copy-done.49, f32[1088]{0:T(1024)S(1)} %copy-done.40, ...), kind=kOutput, calls=%fused_computation.5 | convolution fusion | flops 9647554560 | bytes 19199488 | tf_op jit(solution)/shard_map/dot_general | solution.py:21
  137.9 1.7 slice.225
  139.6 2.4 copy-done.16
  142.5 1.7 fusion.23
  144.2 1.6 copy.100.mg_ref
  148.4 2.5 copy.99.mt_ref
  151.0 12.6 %collective-permute-done.2.refs_3_ = bf16[272,1088]{1,0:T(8,128)(2,1)} collective-permute-done((bf16[272,1088]{1,0:T(8,128)(2,1)}, bf16[272,1088]{1,0:T(8,128)(2,1)}, u32[]{:S(2)}, u32[]{:S(2)}) %collective-permute-start.2) | collective-permute-done | bytes 591904 | tf_op jit(solution)/shard_map/ppermute | solution.py:1379
  164.7 3.6 in_order.1.refs_0_.refs_1_.refs_10_
  170.8 4.9 all-to-all-start
  177.0 37.5 %attention_forward.3 = (bf16[1280,1152]{1,0:T(8,128)(2,1)}, f32[1280,1152]{1,0:T(8,128)}) custom-call(bf16[1280,3456]{1,0:T(8,128)(2,1)} %copy-done.16, bf16[1280,3456]{1,0:T(8,128)(2,1)} %copy-done.16, bf16[1280,3456]{1,0:T(8,128)(2,1)} %copy-done.16, bf16[512,2304]{1,0:T(8,128)(2,1)S(1)} %collective-permute-done.12.ko_ref.vo_ref, ...), custom_call_target="tpu_custom_call" | custom-call | flops 39936000000 | bytes 23040000 | tf_op jit(solution)/shard_map/attention_forward/pallas_call | solution.py:112
  214.5 9.3 %collective-permute-done.3.refs_1_.refs_11_ = bf16[4,272,1088]{2,1,0:T(8,128)(2,1)} collective-permute-done((bf16[4,272,1088]{2,1,0:T(8,128)(2,1)}, bf16[4,272,1088]{2,1,0:T(8,128)(2,1)}, u32[]{:S(2)}, u32[]{:S(2)}) %collective-permute-start.3) | collective-permute-done | bytes 2367520 | tf_op jit(solution)/shard_map/ppermute | solution.py:1303
  229.0 13.8 %attention_forward.4 = (bf16[1280,1152]{1,0:T(8,128)(2,1)}, f32[1280,1152]{1,0:T(8,128)}) custom-call(bf16[1280,3456]{1,0:T(8,128)(2,1)} %copy-done.16, bf16[1280,3456]{1,0:T(8,128)(2,1)} %copy-done.16, bf16[1280,3456]{1,0:T(8,128)(2,1)} %copy-done.16, bf16[512,2304]{1,0:T(8,128)(2,1)} %copy-done, ...), custom_call_target="tpu_custom_call", output_to_operand_aliasing={{0}: (7, {}), {1}: (8, {})} | custom-call | flops 13312000000 | bytes 23040000 | tf_op jit(solution)/shard_map/attention_forward/pallas_call | solution.py:112
  242.8 9.9 %collective-permute-done.5.refs_2_.refs_3_.refs_13_ = bf16[2,272,1088]{2,1,0:T(8,128)(2,1)S(1)} collective-permute-done((bf16[2,272,1088]{2,1,0:T(8,128)(2,1)S(1)}, bf16[2,272,1088]{2,1,0:T(8,128)(2,1)S(1)}, u32[]{:S(2)}, u32[]{:S(2)}) %collective-permute-start.5) | collective-permute-done | bytes 1183776 | tf_op jit(solution)/shard_map/ppermute | solution.py:1303
  252.7 2.7 collective-permute-done.6.refs_3_.refs_4_.refs_14_
  255.4 5.1 attention_forward.5
  265.5 1.8 collective-permute-done.13
  268.9 10.1 %project_out.1 = (f32[1280,1088]{1,0:T(8,128)}, bf16[1280,1088]{1,0:T(8,128)(2,1)}) custom-call(bf16[1280,1152]{1,0:T(8,128)(2,1)} %get-tuple-element.69.mixed.refs_1_.o_ref, bf16[1280,1088]{1,0:T(8,128)(2,1)} %get-tuple-element.62.rows, bf16[1152,1152]{1,0:T(8,128)(2,1)} %copy-done.15, f32[1,1088]{1,0:T(1,128)} %reshape.579.bias, f32[1,1088]{1,0:T(1,128)} %reshape.580.gain, ...), custom_call_target="tpu_custom_call" | custom-call | flops 12000000000 | tf_op jit(solution)/shard_map/project_out/pallas_call | solution.py:945
  279.0 3.8 spread_rows.1.refs_21_.seed
  282.8 1.6 copy-done.4
  284.5 125.5 %feed_forward.1 = (f32[1280,1088]{1,0:T(8,128)}, f32[1280,1088]{1,0:T(8,128)}, f32[1,4352]{1,0:T(1,128)}, bf16[272,4352]{1,0:T(8,128)(2,1)}, bf16[272,4352]{1,0:...) custom-call(s32[6]{0:T(128)} %stack.46.scalars, ...), custom_call_target="tpu_custom_call" | custom-call | flops 145458462720 | bytes 65732608 | tf_op jit(solution)/shard_map/feed_forward/pallas_call | solution.py:465
  411.7 3.1 collective-permute-done.14
  414.8 2.3 add_convert_fusion.1
  422.1 22.1 %middle_back.1 = (bf16[1280,1088]{1,0:T(8,128)(2,1)}, f32[1280,1088]{1,0:T(8,128)}, bf16[1280,1152]{1,0:T(8,128)(2,1)}, f32[4,1088]{1,0:T(4,128)}, bf16[1088,1152]{1,0:T(8,128)(2,1)}) custom-call(f32[1280,1088]{1,0:T(8,128)} %get-tuple-element.72.second_grad, f32[1280,1088]{1,0:T(8,128)} %get-tuple-element.73.lowered, ...), custom_call_target="tpu_custom_call" | custom-call | flops 24999999488 | tf_op jit(solution)/shard_map/middle_back/pallas_call | solution.py:945
  444.2 2.1 convert_add_fusion.1
  446.6 1.6 copy-done.5
  451.5 1.6 pad_maximum_fusion.refs_1_
  458.4 4.4 collect_rows.1
  462.8 5.0 all-to-all-start.1
  467.9 46.9 %attention_backward.2 = (bf16[1280,1152]{1,0:T(8,128)(2,1)}, bf16[1280,1152]{1,0:T(8,128)(2,1)}, bf16[1280,1152]{1,0:T(8,128)(2,1)}, bf16[512,1152]{1,0:T(8,128)(2,1)}, bf16[512,1152]{1,0:T(8,128)(2,1)}) custom-call(bf16[1280,3456]{1,0:T(8,128)(2,1)} %copy-done.16, bf16[1280,3456]{1,0:T(8,128)(2,1)} %copy-done.16, bf16[1280,3456]{1,0:T(8,128)(2,1)} %copy-done.16, ...), custom_call_target="tpu_custom_call" | custom-call | flops 6400000000 | bytes 46080000 | tf_op jit(solution)/shard_map/attention_backward/pallas_call | solution.py:251
  514.8 4.9 add_convert_fusion.refs_5_.total.total_tail
  521.2 34.3 %attention_backward.3 = (bf16[1280,1152]{1,0:T(8,128)(2,1)}, bf16[1280,1152]{1,0:T(8,128)(2,1)}, bf16[1280,1152]{1,0:T(8,128)(2,1)}, bf16[512,1152]{1,0:T(8,128)(2,1)}, bf16[512,1152]{1,0:T(8,128)(2,1)}) custom-call(bf16[1280,3456]{1,0:T(8,128)(2,1)} %copy-done.16, ...), custom_call_target="tpu_custom_call", output_to_operand_aliasing={{0}: (10, {}), {1}: (11, {}), {2}: (12, {}), {3}: (13, {}),... | custom-call | flops 5120000000 | bytes 46080000 | tf_op jit(solution)/shard_map/attention_backward/pallas_call | solution.py:251
  556.9 4.4 pair_blocks.1.refs_0_
  561.3 4.9 all-to-all-start.2
  566.4 11.2 %finish_gradients.1 = (bf16[1280,3456]{1,0:T(8,128)(2,1)}, f32[1,3456]{1,0:T(1,128)S(1)}) custom-call(bf16[1280,1152]{1,0:T(8,128)(2,1)} %get-tuple-element.91.dq, bf16[1280,1152]{1,0:T(8,128)(2,1)} %get-tuple-element.92.dk, bf16[1280,1152]{1,0:T(8,128)(2,1)} %get-tuple-element.93.dv, bf16[512,1152]{1,0:T(8,128)(2,1)} %collective-permute-done.23.other_k, ...), custom_call_target="tpu_custom_call" | custom-call | flops 1000000000 | tf_op jit(solution)/shard_map/finish_gradients/pallas_call | solution.py:898
  577.7 20.2 %first_back.1 = (bf16[1280,1088]{1,0:T(8,128)(2,1)}, f32[2,1088]{1,0:T(2,128)}) custom-call(bf16[1280,3456]{1,0:T(8,128)(2,1)} %get-tuple-element.96.triple_grad, bf16[1280,1088]{1,0:T(8,128)(2,1)} %get-tuple-element.62.rows, f32[1280,1088]{1,0:T(8,128)} %get-tuple-element.98.middle_grad, bf16[1088,3456]{1,0:T(8,128)(2,1)} %get-tuple-element.64.weight, ...), custom_call_target="tpu_custom_call" | custom-call | flops 4000000000 | tf_op jit(solution)/shard_map/first_back/pallas_call | solution.py:945
  598.8 15.4 %convolution_convert_fusion.triple = bf16[1088,3456]{1,0:T(8,128)(2,1)} fusion(bf16[1280,3456]{1,0:T(8,128)(2,1)} %get-tuple-element.96.triple_grad, bf16[1280,1088]{1,0:T(8,128)(2,1)S(1)} %copy-done.21, f32[1088]{0:T(1024)S(1)} %copy-done.50, f32[1088]{0:T(1024)S(1)} %copy-done.41, f32[1280]{0:T(1024)S(1)} %copy-done.43, f32[1280]{0:T(1024)S(1)} %copy-done.30), kind=kOutput, calls=%fused_computation.6 | convolution fusion | flops 9638043648 | bytes 19171840 | tf_op jit(solution)/shard_map/dot_general | solution.py:29
  614.2 9.2 %divide_gradients.1.grads = bf16[2,4,4,272,544]{4,3,2,1,0:T(8,128)(2,1)} custom-call(bf16[1088,3456]{1,0:T(8,128)(2,1)} %convolution_convert_fusion.triple, bf16[1088,1152]{1,0:T(8,128)(2,1)S(1)} %copy-done.8), custom_call_target="tpu_custom_call" | custom-call | flops 1000000000 | tf_op jit(solution)/shard_map/divide_gradients/pallas_call | solution.py:852
  623.4 2.2 convert_reduce_fusion.1
  629.0 2.1 copy-done.14
  631.1 106.2 %end_exchange.1 = (f32[272,544]{1,0:T(8,128)S(1)}, f32[104,128]{1,0:T(8,128)S(1)}, bf16[4,320,1088]{2,1,0:T(8,128)(2,1)S(1)}) custom-call(bf16[2,4,4,272,544]{4,3,2,1,0:T(8,128)(2,1)} %divide_gradients.1.grads, f32[104,128]{1,0:T(8,128)S(1)} %pad_bitcast_fusion.small, bf16[1280,1088]{1,0:T(8,128)(2,1)S(1)} %copy-done.14, f32[272,544]{1,0:T(8,128)S(1)} %copy.108.refs_0_, ...), custom_call_target="tpu_custom_call" | custom-call | flops 99999997952 | tf_op jit(solution)/shard_map/end_exchange/pallas_call | solution.py:758
  737.3 1.6 copy-done.6
  743.3 3.8 copy.133
  747.1 1.6 copy.134
  (241 shorter events, 50.7 us)
Async XLA Ops:
  105.7 45.3 %collective-permute-start = (bf16[272,1088]{1,0:T(8,128)(2,1)}, bf16[272,1088]{1,0:T(8,128)(2,1)}, u32[]{:S(2)}, u32[]{:S(2)}) collective-permute-start(bf16[272,1088]{1,0:T(8,128)(2,1)} %get-tuple-element.61.refs_0_), channel_id=1, source_target_pairs={{0,2},{1,3},{2,0},{3,1},{4,6},{5,7},{6,4},{7,5},{8,10},{9,11},{10,... | collective-permute-start | bytes 1775624 | tf_op jit(solution)/shard_map/ppermute | solution.py:1379
  105.8 45.2 %collective-permute-start.1 = (bf16[272,1088]{1,0:T(8,128)(2,1)}, bf16[272,1088]{1,0:T(8,128)(2,1)}, u32[]{:S(2)}, u32[]{:S(2)}) collective-permute-start(bf16[272,1088]{1,0:T(8,128)(2,1)} %get-tuple-element.61.refs_0_), channel_id=1, source_target_pairs={{0,4},{1,5},{2,6},{3,7},{4,0},{5,1},{6,2},{7,3},{8,12},{9,13},{10,... | collective-permute-start | bytes 1775624 | tf_op jit(solution)/shard_map/ppermute | solution.py:1379
  108.4 55.2 %collective-permute-start.2 = (bf16[272,1088]{1,0:T(8,128)(2,1)}, bf16[272,1088]{1,0:T(8,128)(2,1)}, u32[]{:S(2)}, u32[]{:S(2)}) collective-permute-start(bf16[272,1088]{1,0:T(8,128)(2,1)} %get-tuple-element.61.refs_0_), channel_id=1, source_target_pairs={{0,6},{1,7},{2,4},{3,5},{4,2},{5,3},{6,0},{7,1},{8,14},{9,15},{10,... | collective-permute-start | bytes 1775624 | tf_op jit(solution)/shard_map/ppermute | solution.py:1379
  111.6 10.1 %copy-start.29 = (f32[1280]{0:T(1024)}, f32[1280]{0:T(1024)S(1)}, u32[]{:S(2)}) copy-start(f32[1280]{0:T(1024)S(1)} %broadcast_multiply_fusion.1) | copy-start | bytes 15364
  112.5 9.1 %copy-start.42 = (f32[1280]{0:T(1024)}, f32[1280]{0:T(1024)S(1)}, u32[]{:S(2)}) copy-start(f32[1280]{0:T(1024)S(1)} %add_rsqrt_fusion) | copy-start | bytes 15364
  112.6 9.1 %copy-start.40 = (f32[1088]{0:T(1024)S(1)}, f32[1088]{0:T(1024)}, u32[]{:S(2)}) copy-start(f32[1088]{0:T(1024)} %param.27) | copy-start | bytes 13060
  112.6 9.1 %copy-start.49 = (f32[1088]{0:T(1024)S(1)}, f32[1088]{0:T(1024)}, u32[]{:S(2)}) copy-start(f32[1088]{0:T(1024)} %param.28) | copy-start | bytes 13060
  112.6 9.1 %copy-start.52 = (f32[3456]{0:T(1024)S(1)}, f32[3456]{0:T(1024)}, u32[]{:S(2)}) copy-start(f32[3456]{0:T(1024)} %constant.175.clone.1) | copy-start | bytes 41476
  121.6 16.3 %copy-start.15 = (bf16[1152,1152]{1,0:T(8,128)(2,1)}, bf16[1152,1152]{1,0:T(8,128)(2,1)S(1)}, u32[]{:S(2)}) copy-start(bf16[1152,1152]{1,0:T(8,128)(2,1)S(1)} %get-tuple-element.70.weight) | copy-start | bytes 7962628
  141.9 33.8 %collective-permute-start.12 = (bf16[512,2304]{1,0:T(8,128)(2,1)}, bf16[512,2304]{1,0:T(8,128)(2,1)S(1)}, u32[]{:S(2)}, u32[]{:S(2)}) collective-permute-start(bf16[512,2304]{1,0:T(8,128)(2,1)} %slice.225), channel_id=1, source_target_pairs={{0,1},{1,0},{2,3},{3,2},{4,5},{5,4},{6,7},{7,6},{8,9},{9,8},{10,11... | collective-permute-start | bytes 7077896 | tf_op jit(solution)/shard_map/ppermute | solution.py:1504
  168.3 55.5 %collective-permute-start.3 = (bf16[4,272,1088]{2,1,0:T(8,128)(2,1)}, bf16[4,272,1088]{2,1,0:T(8,128)(2,1)}, u32[]{:S(2)}, u32[]{:S(2)}) collective-permute-start(bf16[4,272,1088]{2,1,0:T(8,128)(2,1)} %in_order.1.refs_0_.refs_1_.refs_10_), channel_id=1, source_target_pairs={{0,8},{8,0},{16,24},{24,16},{1,9},{9,1},{17,25},{25,17},{2,10},{10... | collective-permute-start | bytes 7102472 | tf_op jit(solution)/shard_map/ppermute | solution.py:1303
  169.8 57.0 %collective-permute-start.4 = (bf16[4,272,1088]{2,1,0:T(8,128)(2,1)}, bf16[4,272,1088]{2,1,0:T(8,128)(2,1)}, u32[]{:S(2)}, u32[]{:S(2)}) collective-permute-start(bf16[4,272,1088]{2,1,0:T(8,128)(2,1)} %in_order.1.refs_0_.refs_1_.refs_10_), channel_id=1, source_target_pairs={{0,16},{8,24},{16,0},{24,8},{1,17},{9,25},{17,1},{25,9},{2,18},{10... | collective-permute-start | bytes 7102472 | tf_op jit(solution)/shard_map/ppermute | solution.py:1303
  170.8 90.7 %all-to-all-start = ((bf16[4,320,1088]{2,1,0:T(8,128)(2,1)}), bf16[4,320,1088]{2,1,0:T(8,128)(2,1)}, u32[]{:S(2)}, u32[]{:S(2)}) async-start(bf16[4,320,1088]{2,1,0:T(8,128)(2,1)} %after.3), calls=%async_computation | async-start | bytes 5898240 | tf_op jit(solution)/shard_map/all_to_all | solution.py:1219
  177.0 37.5 %copy-start = (bf16[512,2304]{1,0:T(8,128)(2,1)}, bf16[512,2304]{1,0:T(8,128)(2,1)S(1)}, u32[]{:S(2)}) copy-start(bf16[512,2304]{1,0:T(8,128)(2,1)S(1)} %collective-permute-done.12.ko_ref.vo_ref) | copy-start | bytes 7077892
  214.5 14.5 %copy-start.3 = (f32[2,256,512]{2,1,0:T(8,128)S(1)}, f32[2,256,512]{2,1,0:T(8,128)}, u32[]{:S(2)}) copy-start(f32[2,256,512]{2,1,0:T(8,128)} %copy.99.mt_ref) | copy-start | bytes 3145732
  225.2 27.5 %collective-permute-start.5 = (bf16[2,272,1088]{2,1,0:T(8,128)(2,1)S(1)}, bf16[2,272,1088]{2,1,0:T(8,128)(2,1)S(1)}, u32[]{:S(2)}, u32[]{:S(2)}) collective-permute-start(bf16[2,272,1088]{2,1,0:T(8,128)(2,1)S(1)} %slice.223.refs_2_), channel_id=1, source_target_pairs={{0,16},{8,24},{16,0},{24,8},{1,17},{9,25},{17,1},{25,9},{2,18},{10... | collective-permute-start | bytes 3551240 | tf_op jit(solution)/shard_map/ppermute | solution.py:1303
  228.2 27.2 %collective-permute-start.6 = (bf16[2,272,1088]{2,1,0:T(8,128)(2,1)S(1)}, bf16[2,272,1088]{2,1,0:T(8,128)(2,1)S(1)}, u32[]{:S(2)}, u32[]{:S(2)}) collective-permute-start(bf16[2,272,1088]{2,1,0:T(8,128)(2,1)S(1)} %slice.224.refs_3_), channel_id=1, source_target_pairs={{0,8},{8,0},{16,24},{24,16},{1,9},{9,1},{17,25},{25,17},{2,10},{10... | collective-permute-start | bytes 3551240 | tf_op jit(solution)/shard_map/ppermute | solution.py:1303
  252.7 12.7 %copy-start.9 = (bf16[2,272,1088]{2,1,0:T(8,128)(2,1)}, bf16[2,272,1088]{2,1,0:T(8,128)(2,1)S(1)}, u32[]{:S(2)}) copy-start(bf16[2,272,1088]{2,1,0:T(8,128)(2,1)S(1)} %collective-permute-done.5.refs_2_.refs_3_.refs_13_) | copy-start | bytes 3551236
  261.6 5.8 collective-permute-start.13
  261.7 22.8 %collective-permute-start.7 = (bf16[4,272,1088]{2,1,0:T(8,128)(2,1)}, bf16[4,272,1088]{2,1,0:T(8,128)(2,1)}, u32[]{:S(2)}, u32[]{:S(2)}) collective-permute-start(bf16[4,272,1088]{2,1,0:T(8,128)(2,1)} %in_order.1.refs_0_.refs_1_.refs_10_), channel_id=1, source_target_pairs={{0,1},{1,0},{2,3},{3,2},{4,5},{5,4},{6,7},{7,6},{8,9},{9,8},{10,11... | collective-permute-start | bytes 7102472 | tf_op jit(solution)/shard_map/ppermute | solution.py:1319
  262.2 22.3 %collective-permute-start.8 = (bf16[4,272,1088]{2,1,0:T(8,128)(2,1)}, bf16[4,272,1088]{2,1,0:T(8,128)(2,1)}, u32[]{:S(2)}, u32[]{:S(2)}) collective-permute-start(bf16[4,272,1088]{2,1,0:T(8,128)(2,1)} %collective-permute-done.3.refs_1_.refs_11_), channel_id=1, source_target_pairs={{0,1},{1,0},{2,3},{3,2},{4,5},{5,4},{6,7},{7,6},{8,9},{9,8},{10,11... | collective-permute-start | bytes 7102472 | tf_op jit(solution)/shard_map/ppermute | solution.py:1319
  262.2 22.2 %collective-permute-start.9 = (bf16[4,272,1088]{2,1,0:T(8,128)(2,1)}, bf16[4,272,1088]{2,1,0:T(8,128)(2,1)}, u32[]{:S(2)}, u32[]{:S(2)}) collective-permute-start(bf16[4,272,1088]{2,1,0:T(8,128)(2,1)} %collective-permute-done.4.refs_2_.refs_12_), channel_id=1, source_target_pairs={{0,1},{1,0},{2,3},{3,2},{4,5},{5,4},{6,7},{7,6},{8,9},{9,8},{10,11... | collective-permute-start | bytes 7102472 | tf_op jit(solution)/shard_map/ppermute | solution.py:1319
  265.4 19.1 %collective-permute-start.10 = (bf16[2,272,1088]{2,1,0:T(8,128)(2,1)S(1)}, bf16[2,272,1088]{2,1,0:T(8,128)(2,1)}, u32[]{:S(2)}, u32[]{:S(2)}) collective-permute-start(bf16[2,272,1088]{2,1,0:T(8,128)(2,1)S(1)} %collective-permute-done.5.refs_2_.refs_3_.refs_13_), channel_id=1, source_target_pairs={{0,1},{1,0},{2,3},{3,2},{4,5},{5,4},{6,7},{7,6},{8,9},{9,8},{10,11... | collective-permute-start | bytes 3551240 | tf_op jit(solution)/shard_map/ppermute | solution.py:1319
  267.4 17.1 %collective-permute-start.11 = (bf16[2,272,1088]{2,1,0:T(8,128)(2,1)S(1)}, bf16[2,272,1088]{2,1,0:T(8,128)(2,1)}, u32[]{:S(2)}, u32[]{:S(2)}) collective-permute-start(bf16[2,272,1088]{2,1,0:T(8,128)(2,1)S(1)} %copy-done.11), channel_id=1, source_target_pairs={{0,1},{1,0},{2,3},{3,2},{4,5},{5,4},{6,7},{7,6},{8,9},{9,8},{10,11... | collective-permute-start | bytes 3551240 | tf_op jit(solution)/shard_map/ppermute | solution.py:1319
  284.5 126.1 %copy-start.39 = (f32[1088]{0:T(1024)S(1)}, f32[1088]{0:T(1024)}, u32[]{:S(2)}) copy-start(f32[1088]{0:T(1024)} %param.39) | copy-start | bytes 13060
  410.0 4.8 collective-permute-start.14
  410.4 11.2 %collective-permute-start.18 = (bf16[272,4352]{1,0:T(8,128)(2,1)}, bf16[272,4352]{1,0:T(8,128)(2,1)S(1)}, u32[]{:S(2)}, u32[]{:S(2)}) collective-permute-start(bf16[272,4352]{1,0:T(8,128)(2,1)} %get-tuple-element.83), channel_id=1, source_target_pairs={{0,1},{1,0},{2,3},{3,2},{4,5},{5,4},{6,7},{7,6},{8,9},{9,8},{10,11... | collective-permute-start | bytes 7102472 | tf_op jit(solution)/shard_map/ppermute | solution.py:1319
  411.1 33.1 %collective-permute-start.16 = (bf16[272,4352]{1,0:T(8,128)(2,1)}, bf16[272,4352]{1,0:T(8,128)(2,1)}, u32[]{:S(2)}, u32[]{:S(2)}) collective-permute-start(bf16[272,4352]{1,0:T(8,128)(2,1)} %get-tuple-element.81), channel_id=1, source_target_pairs={{0,1},{1,0},{2,3},{3,2},{4,5},{5,4},{6,7},{7,6},{8,9},{9,8},{10,11... | collective-permute-start | bytes 7102472 | tf_op jit(solution)/shard_map/ppermute | solution.py:1319
  411.5 103.3 %collective-permute-start.20 = (bf16[272,4352]{1,0:T(8,128)(2,1)}, bf16[272,4352]{1,0:T(8,128)(2,1)}, u32[]{:S(2)}, u32[]{:S(2)}) collective-permute-start(bf16[272,4352]{1,0:T(8,128)(2,1)} %get-tuple-element.90), channel_id=1, source_target_pairs={{0,1},{1,0},{2,3},{3,2},{4,5},{5,4},{6,7},{7,6},{8,9},{9,8},{10,11... | collective-permute-start | bytes 7102472 | tf_op jit(solution)/shard_map/ppermute | solution.py:1319
  419.3 29.2 %collective-permute-start.19 = (bf16[128,4352]{1,0:T(8,128)(2,1)}, bf16[128,4352]{1,0:T(8,128)(2,1)}, u32[]{:S(2)}, u32[]{:S(2)}) collective-permute-start(bf16[128,4352]{1,0:T(8,128)(2,1)} %slice.229.refs_1_), channel_id=1, source_target_pairs={{0,8},{8,0},{16,24},{24,16},{1,9},{9,1},{17,25},{25,17},{2,10},{10... | collective-permute-start | bytes 3342344 | tf_op jit(solution)/shard_map/ppermute | solution.py:1303
  419.9 30.1 %collective-permute-start.17 = (bf16[144,4352]{1,0:T(8,128)(2,1)}, bf16[144,4352]{1,0:T(8,128)(2,1)}, u32[]{:S(2)}, u32[]{:S(2)}) collective-permute-start(bf16[144,4352]{1,0:T(8,128)(2,1)} %slice.228.refs_0_), channel_id=1, source_target_pairs={{0,16},{8,24},{16,0},{24,8},{1,17},{9,25},{17,1},{25,9},{2,18},{10... | collective-permute-start | bytes 3760136 | tf_op jit(solution)/shard_map/ppermute | solution.py:1303
  422.1 22.2 %copy-start.22 = (bf16[272,4352]{1,0:T(8,128)(2,1)S(1)}, bf16[272,4352]{1,0:T(8,128)(2,1)}, u32[]{:S(2)}) copy-start(bf16[272,4352]{1,0:T(8,128)(2,1)} %get-tuple-element.80) | copy-start | bytes 7102468
  448.2 10.2 %collective-permute-start.15 = (bf16[20,64,1088]{2,1,0:T(8,128)(2,1)S(1)}, bf16[20,64,1088]{2,1,0:T(8,128)(2,1)}, u32[]{:S(2)}, u32[]{:S(2)}) collective-permute-start(bf16[20,64,1088]{2,1,0:T(8,128)(2,1)S(1)} %bitcast.38), channel_id=1, source_target_pairs={{0,1},{1,0},{2,3},{3,2},{4,5},{5,4},{6,7},{7,6},{8,9},{9,8},{10,11... | collective-permute-start | bytes 8355848 | tf_op jit(solution)/shard_map/ppermute | solution.py:1239
  453.1 61.7 %collective-permute-start.21 = (bf16[272,4352]{1,0:T(8,128)(2,1)}, bf16[272,4352]{1,0:T(8,128)(2,1)}, u32[]{:S(2)}, u32[]{:S(2)}) collective-permute-start(bf16[272,4352]{1,0:T(8,128)(2,1)} %pad_maximum_fusion.refs_1_), channel_id=1, source_target_pairs={{0,8},{8,0},{16,24},{24,16},{1,9},{9,1},{17,25},{25,17},{2,10},{10... | collective-permute-start | bytes 7102472 | tf_op jit(solution)/shard_map/ppermute | solution.py:1303
  455.9 58.9 %collective-permute-start.22 = (bf16[272,4352]{1,0:T(8,128)(2,1)}, bf16[272,4352]{1,0:T(8,128)(2,1)}, u32[]{:S(2)}, u32[]{:S(2)}) collective-permute-start(bf16[272,4352]{1,0:T(8,128)(2,1)} %pad_maximum_fusion.1.refs_2_), channel_id=1, source_target_pairs={{0,16},{8,24},{16,0},{24,8},{1,17},{9,25},{17,1},{25,9},{2,18},{10... | collective-permute-start | bytes 7102472 | tf_op jit(solution)/shard_map/ppermute | solution.py:1303
  462.8 98.5 %all-to-all-start.1 = ((bf16[4,320,1088]{2,1,0:T(8,128)(2,1)}), bf16[4,320,1088]{2,1,0:T(8,128)(2,1)}, u32[]{:S(2)}, u32[]{:S(2)}) async-start(bf16[4,320,1088]{2,1,0:T(8,128)(2,1)} %bitcast.19.refs_0_), calls=%async_computation.1 | async-start | bytes 5898240 | tf_op jit(solution)/shard_map/all_to_all | solution.py:1219
  519.8 37.2 %collective-permute-start.25 = (bf16[272,4352]{1,0:T(8,128)(2,1)S(1)}, bf16[272,4352]{1,0:T(8,128)(2,1)}, u32[]{:S(2)}, u32[]{:S(2)}) collective-permute-start(bf16[272,4352]{1,0:T(8,128)(2,1)S(1)} %add_convert_fusion.refs_5_.total.total_tail), channel_id=1, source_target_pairs={{0,1},{1,0},{2,3},{3,2},{4,5},{5,4},{6,7},{7,6},{8,9},{9,8},{10,11... | collective-permute-start | bytes 7102472 | tf_op jit(solution)/shard_map/ppermute | solution.py:1319
  521.2 34.9 %copy-start.41 = (f32[1088]{0:T(1024)S(1)}, f32[1088]{0:T(1024)}, u32[]{:S(2)}) copy-start(f32[1088]{0:T(1024)} %param.27) | copy-start | bytes 13060
  521.2 35.5 %copy-start.33 = (f32[1,4352]{1,0:T(1,128)S(1)}, f32[1,4352]{1,0:T(1,128)}, u32[]{:S(2)}) copy-start(f32[1,4352]{1,0:T(1,128)} %get-tuple-element.102) | copy-start | bytes 52228
  555.6 10.8 %collective-permute-start.23 = (bf16[512,1152]{1,0:T(8,128)(2,1)}, bf16[512,1152]{1,0:T(8,128)(2,1)}, u32[]{:S(2)}, u32[]{:S(2)}) collective-permute-start(bf16[512,1152]{1,0:T(8,128)(2,1)} %get-tuple-element.94), channel_id=1, source_target_pairs={{0,1},{1,0},{2,3},{3,2},{4,5},{5,4},{6,7},{7,6},{8,9},{9,8},{10,11... | collective-permute-start | bytes 3538952 | tf_op jit(solution)/shard_map/ppermute | solution.py:1564
  555.7 10.7 %collective-permute-start.24 = (bf16[512,1152]{1,0:T(8,128)(2,1)}, bf16[512,1152]{1,0:T(8,128)(2,1)}, u32[]{:S(2)}, u32[]{:S(2)}) collective-permute-start(bf16[512,1152]{1,0:T(8,128)(2,1)} %get-tuple-element.95), channel_id=1, source_target_pairs={{0,1},{1,0},{2,3},{3,2},{4,5},{5,4},{6,7},{7,6},{8,9},{9,8},{10,11... | collective-permute-start | bytes 3538952 | tf_op jit(solution)/shard_map/ppermute | solution.py:1564
  561.3 62.1 %all-to-all-start.2 = ((bf16[4,272,1088]{2,1,0:T(8,128)(2,1)}), bf16[4,272,1088]{2,1,0:T(8,128)(2,1)}, u32[]{:S(2)}, u32[]{:S(2)}) async-start(bf16[4,272,1088]{2,1,0:T(8,128)(2,1)} %pair_blocks.1.refs_0_), calls=%async_computation.2 | async-start | bytes 5013504 | tf_op jit(solution)/shard_map/all_to_all | solution.py:1219
  577.6 21.1 %copy-start.21 = (bf16[1280,1088]{1,0:T(8,128)(2,1)S(1)}, bf16[1280,1088]{1,0:T(8,128)(2,1)}, u32[]{:S(2)}) copy-start(bf16[1280,1088]{1,0:T(8,128)(2,1)} %get-tuple-element.62.rows) | copy-start | bytes 8355844
  577.6 21.1 %copy-start.30 = (f32[1280]{0:T(1024)S(1)}, f32[1280]{0:T(1024)}, u32[]{:S(2)}) copy-start(f32[1280]{0:T(1024)} %copy-done.29) | copy-start | bytes 15364
  577.7 21.1 %copy-start.43 = (f32[1280]{0:T(1024)S(1)}, f32[1280]{0:T(1024)}, u32[]{:S(2)}) copy-start(f32[1280]{0:T(1024)} %copy-done.42) | copy-start | bytes 15364
  577.7 21.1 %copy-start.50 = (f32[1088]{0:T(1024)S(1)}, f32[1088]{0:T(1024)}, u32[]{:S(2)}) copy-start(f32[1088]{0:T(1024)} %param.28) | copy-start | bytes 13060
  598.8 15.4 %copy-start.8 = (bf16[1088,1152]{1,0:T(8,128)(2,1)S(1)}, bf16[1088,1152]{1,0:T(8,128)(2,1)}, u32[]{:S(2)}) copy-start(bf16[1088,1152]{1,0:T(8,128)(2,1)} %get-tuple-element.97.out) | copy-start | bytes 7520260
  629.0 108.3 %copy-start.12 = (f32[272,544]{1,0:T(8,128)}, f32[272,544]{1,0:T(8,128)S(1)}, u32[]{:S(2)}) copy-start(f32[272,544]{1,0:T(8,128)S(1)} %copy.108.refs_0_) | copy-start | bytes 1775620
  (35 other events, 129.6 us)
